TPU v7x, 1024 devices: a whole 8x8x8 slice. The times are simulated.
1024 devices in a mesh: row: 16 (over y, z_hi), col: 8 (over z_lo, core), feat: 8 (over x).
Axes of the slice: x: 8, y: 8, z: 8 (z_hi: 2, z_lo: 4; z = z_hi * 4 + z_lo), core: 2. Of those that a mesh axis runs over, the one named last changes fastest.
Arguments:
- features: bfloat16 [131072, 256], P(('col', 'row'), 'feat'), may hold values from -6 to 6
- weight: bfloat16 [256, 256], P('feat'), may hold values from -0.375 to 0.375
- grad_out: bfloat16 [131072, 256], P(('row', 'col', 'feat')), may hold values from -6 to 6
- adjacency: bfloat16 [24576, 128, 128], P(('row', 'col')), may hold values from 0 to 0.029907227
- tile_rows: int32 [24576], P(('row', 'col')), may hold values from 0 to 63, as said below
- tile_cols: int32 [24576], P(('row', 'col')), may hold values from 0 to 127
- tile_count: int32 [128], P(('row', 'col')), may hold values from 48 to 192, as said below
Outputs:
- activated: bfloat16 [131072, 256], P(('row', 'col', 'feat'))
- weight_grad: float32 [256, 256], P('feat')
- feature_grad: float32 [131072, 256], P(('col', 'row'), 'feat')
Inputs may be any that keep to these rules, and one draw needn't show every extreme that they name: Within one device pair the positions (tile_rows, tile_cols) of its 192 slots are all different. `tile_count`: some device pair has all 192 slots live.
All inputs are finite; a program needn't handle non-finite values.
Results may differ from a plain program's by a relative error of at most 0.0049.
Values may be sent and summed in bfloat16 or wider, within the bound.
No kernel may reach another device: no remote copies, remote signals or barrier semaphores. Data moves between devices by JAX's collectives and lax.ppermute only.
A program may use at most 32 MiB of HBM per device.

v0:
```python
import math

import jax
import jax.numpy as jnp
from jax import lax
from jax.sharding import PartitionSpec as P

BR_DEV = 64


def local(features, weight, grad_out, adjacency, tile_rows, tile_cols, tile_count):
    highest_precision = lax.Precision.HIGHEST
    feat_width = weight.shape[0]
    tile_extent = adjacency.shape[1]
    slot_count = adjacency.shape[0]
    live_mask = (jnp.arange(slot_count, dtype=jnp.int32) < tile_count[0]).astype(jnp.float32)
    gathered = lax.all_gather(features, "row", axis=0, tiled=True)
    col_blocks = gathered.shape[0] // tile_extent
    node_total = gathered.shape[0] * lax.axis_size("col")
    chosen = gathered.reshape(col_blocks, tile_extent, feat_width)[tile_cols]
    products = jnp.einsum("tab,tbf->taf", adjacency, chosen, preferred_element_type=jnp.float32)
    row_hot = (tile_rows[None, :] == jnp.arange(BR_DEV, dtype=jnp.int32)[:, None]).astype(
        jnp.float32
    )
    row_hot = row_hot * live_mask[None, :]
    partial_value = jnp.einsum("rt,taf->raf", row_hot, products, precision=highest_precision)
    partial_value = partial_value.reshape(BR_DEV * tile_extent, feat_width)
    row_total = lax.psum_scatter(partial_value, "col", scatter_dimension=0, tiled=True)
    weighted = jnp.dot(row_total, weight.astype(jnp.float32), precision=highest_precision)
    pre_act = lax.psum_scatter(weighted, "feat", scatter_dimension=0, tiled=True)
    gate_value = jax.nn.sigmoid(pre_act)
    activated = (pre_act * gate_value).astype(jnp.bfloat16)
    derivative = gate_value * (1.0 + pre_act * (1.0 - gate_value))
    grad_pre = (grad_out.astype(jnp.float32) * derivative).astype(jnp.bfloat16)
    block_grad = lax.all_gather(grad_pre, ("col", "feat"), axis=0, tiled=True)
    row_count = row_total.shape[0]
    grad_part = lax.dynamic_slice_in_dim(
        block_grad, lax.axis_index("col") * row_count, row_count, 0
    )
    weight_term = jnp.einsum(
        "nf,ng->fg", row_total, grad_part.astype(jnp.float32), precision=highest_precision
    )
    weight_grad = lax.psum(weight_term, ("row", "col")) * (1.0 / math.sqrt(node_total))
    projected = jnp.einsum(
        "ng,fg->nf", block_grad, weight, preferred_element_type=jnp.float32
    ).astype(jnp.bfloat16)
    proj_blocks = projected.reshape(BR_DEV, tile_extent, feat_width)[tile_rows]
    backward_pieces = jnp.einsum(
        "tab,taf->tbf", adjacency, proj_blocks, preferred_element_type=jnp.float32
    )
    column_onehot = (tile_cols[None, :] == jnp.arange(col_blocks, dtype=jnp.int32)[:, None]).astype(
        jnp.float32
    )
    column_onehot = column_onehot * live_mask[None, :]
    spread_factor = jnp.einsum(
        "oi,ihn->ohn", column_onehot, backward_pieces, precision=highest_precision
    )
    spread_factor = spread_factor.reshape(col_blocks * tile_extent, feat_width)
    feature_grad = lax.psum_scatter(spread_factor, "row", scatter_dimension=0, tiled=True)
    return (activated, weight_grad, feature_grad)


def solution(mesh):
    placed = (
        P(("col", "row"), "feat"),
        P("feat", None),
        P(("row", "col", "feat"), None),
        P(("row", "col"), None, None),
        P(("row", "col")),
        P(("row", "col")),
        P(("row", "col")),
    )
    return jax.shard_map(
        local,
        mesh=mesh,
        in_specs=placed,
        out_specs=(P(("row", "col", "feat"), None), P("feat", None), P(("col", "row"), "feat")),
        check_vma=False,
    )
```

profile of v0, /device:TPU:1, one launch (start us, length us, event | category | flops | bytes accessed | tf_op | source)
XLA Modules:
  0.0 932.9 jit_solution(237117965864762636)
XLA Ops:
  7.2 0.0 copy-start
  7.2 0.0 all-gather.3.cloned.1.call-start
  7.2 0.7 all-gather.3.cloned.1.call-update
  7.9 0.0 reduce-scatter.4.cloned.1.call-start
  8.6 0.7 compare_select_fusion.1
  9.3 111.0 %all-gather.3.cloned.1.call-done = bf16[16384,32]{0,1:T(8,128)(2,1)} async-done(((bf16[1024,32]{0,1:T(8,128)(2,1)}), bf16[16384,32]{0,1:T(8,128)(2,1)}) %all-gather.3.cloned.1.call-update) | async-done | bytes 1048592 | tf_op jit(solution)/shard_map/all_gather | solution.py:17
  120.3 1.4 copy_bitcast_fusion.2
  121.7 0.9 gather_fusion
  122.6 0.0 copy-start.4
  122.6 5.4 convolution_bitcast_fusion.1
  128.0 0.0 copy-done.4
  128.0 3.8 fusion.2
  131.8 0.0 copy-start.2
  131.8 1.6 copy.28
  133.4 0.0 reduce-scatter.4.cloned.1.call-update
  133.4 0.0 reduce-scatter.6.cloned.1.call-start
  133.5 39.4 %reduce-scatter.4.cloned.1.call-done = f32[1024,32]{0,1:T(8,128)} async-done(((f32[8192,32]{0,1:T(8,128)}), f32[1024,32]{0,1:T(8,128)}) %reduce-scatter.4.cloned.1.call-update) | async-done | bytes 131088 | tf_op jit(solution)/shard_map/reduce_scatter | solution.py:28
  172.9 0.0 copy-done
  172.9 2.5 fusion.20
  175.4 0.0 reduce-scatter.6.cloned.1.call-update
  175.4 0.0 all-gather.5.cloned.1.call-start
  175.5 41.2 %reduce-scatter.6.cloned.1.call-done = f32[128,256]{1,0:T(8,128)} async-done(((f32[1024,256]{1,0:T(8,128)}), f32[128,256]{1,0:T(8,128)}) %reduce-scatter.6.cloned.1.call-update) | async-done | bytes 131088 | tf_op jit(solution)/shard_map/reduce_scatter | solution.py:30
  216.7 0.0 copy-done.2
  216.7 1.6 multiply_convert_fusion
  218.3 0.0 all-gather.5.cloned.1.call-update
  218.3 0.2 reduce-scatter.8.cloned.1.call-start
  218.6 199.5 %all-gather.5.cloned.1.call-done = bf16[8192,256]{1,0:T(8,128)(2,1)} async-done(((bf16[128,256]{1,0:T(8,128)(2,1)}), bf16[8192,256]{1,0:T(8,128)(2,1)}) %all-gather.5.cloned.1.call-update) | async-done | bytes 4194320 | tf_op jit(solution)/shard_map/all_gather | solution.py:35
  418.0 3.5 fusion.4
  421.5 0.1 copy.29
  421.7 0.9 gather_fusion.1
  422.6 0.0 copy-start.3
  422.6 3.8 convolution_bitcast_fusion
  426.4 0.0 copy-done.3
  426.4 3.9 fusion
  430.3 0.0 copy-start.1
  430.3 2.5 copy.27
  432.8 0.0 reduce-scatter.8.cloned.1.call-update
  432.8 0.0 copy-done.1
  432.9 1.4 fusion.5
  434.3 491.5 %psum.7 = f32[32,256]{1,0:T(8,128)S(1)} all-reduce(f32[32,256]{1,0:T(8,128)S(1)} %fusion.5), channel_id=1, replica_groups=mesh['row'=16,'col'=8,'feat'=8] {'row','col'}, use_global_device_ids=true, to_apply=%region_2.0 | all-reduce | flops 8192 | bytes 65536 | tf_op jit(solution)/shard_map/psum | solution.py:43
  925.8 0.6 broadcast_multiply_fusion
  926.4 0.0 reduce-scatter.8.cloned.1.call-done
  (4 shorter events, 0.0 us)
Async XLA Ops:
  7.2 165.7 %copy-start = (bf16[32,256]{1,0:T(8,128)(2,1)S(1)}, bf16[32,256]{1,0:T(8,128)(2,1)}, u32[]{:S(2)}) copy-start(bf16[32,256]{1,0:T(8,128)(2,1)} %param.8) | copy-start | bytes 49156
  7.2 113.1 %all-gather.3.cloned.1.call-start = ((), (), s32[]{:S(2)}) async-start(), calls=%async_computation.3 | async-start | bytes 1114112 | tf_op jit(solution)/shard_map/all_gather | solution.py:17
  7.9 165.0 %reduce-scatter.4.cloned.1.call-start = ((), (), s32[]{:S(2)}) async-start(), calls=%async_computation.4 | async-start | bytes 1179648 | tf_op jit(solution)/shard_map/reduce_scatter | solution.py:28
  122.6 5.4 copy-start.4
  131.8 84.8 %copy-start.2 = (bf16[128,256]{1,0:T(8,128)(2,1)S(1)}, bf16[128,256]{1,0:T(8,128)(2,1)}, u32[]{:S(2)}) copy-start(bf16[128,256]{1,0:T(8,128)(2,1)} %param.9) | copy-start | bytes 196612
  133.4 83.2 %reduce-scatter.6.cloned.1.call-start = ((), (), s32[]{:S(2)}) async-start(), calls=%async_computation.5 | async-start | bytes 1179648 | tf_op jit(solution)/shard_map/reduce_scatter | solution.py:30
  175.4 242.6 %all-gather.5.cloned.1.call-start = ((), (), s32[]{:S(2)}) async-start(), calls=%async_computation.6 | async-start | bytes 4259840 | tf_op jit(solution)/shard_map/all_gather | solution.py:35
  218.3 708.1 %reduce-scatter.8.cloned.1.call-start = ((), (), s32[]{:S(2)}) async-start(), calls=%async_computation.7 | async-start | bytes 2228224 | tf_op jit(solution)/shard_map/reduce_scatter | solution.py:59
  422.6 3.8 copy-start.3
  430.3 2.6 copy-start.1
Sparse Core Ops, SparseCore 0:
  12.4 107.8 all-gather.2
  133.6 39.3 reduce-scatter.3
  176.3 40.3 reduce-scatter.5
  219.8 198.2 all-gather.4
  433.0 235.4 reduce-scatter.7
where the time goes:
time: 943 us; the launch traced here: 933 us
  blocking collectives  492 us (52%)
  waiting for transfers between devices  392 us (42%)
  matrix products  24.2 us (3%)
  between operations  14.6 us (2%)
    psum x1, blocking collectives, local(): lax.psum(weight_term, ('row', 'col')) * (1.0 / math.sqrt(node_total))  492 us
    all_gather x1, waiting for transfers between devices, local(): block_grad = lax.all_gather(grad_pre, ('col', 'feat'), axis=0, tiled=True)  199 us
    all_gather x1, waiting for transfers between devices, local(): gathered = lax.all_gather(features, 'row', axis=0, tiled=True)  111 us
    reduce_scatter x1, waiting for transfers between devices, local(): lax.psum_scatter(weighted, 'feat', scatter_dimension=0, tiled=True)  41.2 us
    reduce_scatter x1, waiting for transfers between devices, local(): lax.psum_scatter(partial_value, 'col', scatter_dimension=0, tiled=True)  39.4 us
  transfers between devices with their start and end apart: 5, of which 4 were waited for; matrix products, arithmetic and copies ran while one was open for 0% of the time, Pallas kernels for 0%

commit v1 on v0

v1 whole, which is shorter than its diff:
```python
import functools
import math

import jax
import jax.numpy as jnp
from jax import lax
from jax.experimental import pallas as pl
from jax.experimental.pallas import tpu as pltpu
from jax.sharding import PartitionSpec as P

BR_DEV = 64
CHUNK = 32
UNROLL = 8
VMEM_LIMIT = 40 * 1024 * 1024
NT = (((1,), (1,)), ((), ()))
NN = (((1,), (0,)), ((), ()))
TN = (((0,), (0,)), ((), ()))


def dot(a, b, dims):
    return lax.dot_general(a, b, dims, preferred_element_type=jnp.float32)


def accumulate_tiles(count, source, adj_ref, acc_ref, target_of, dims):
    first = pl.program_id(0) * CHUNK

    @pl.when(first < count)
    def _():
        @pl.loop(0, CHUNK // UNROLL)
        def _(group):
            base = group * UNROLL
            terms = []
            for u in range(UNROLL):
                slot = first + base + u
                term = dot(source(slot), adj_ref[base + u], dims)
                terms.append(jnp.where(slot < count, term, 0.0))
            for u in range(UNROLL):
                target = target_of(first + base + u)
                acc_ref[target] += terms[u]


def forward_kernel(rows, cols, count, adj_ref, feat_ref, out_ref, acc_ref):
    @pl.when(pl.program_id(0) == 0)
    def _():
        acc_ref[...] = jnp.zeros_like(acc_ref)

    accumulate_tiles(
        count[0], lambda s: feat_ref[cols[s]], adj_ref, acc_ref, lambda s: rows[s], NT
    )

    @pl.when(pl.program_id(0) == pl.num_programs(0) - 1)
    def _():
        out_ref[...] = acc_ref[...].astype(out_ref.dtype)


def dense_kernel(feat_index, summed_ref, wide_ref, weight_ref, out_ref, act_ref):
    feats, blocks, width, extent = summed_ref.shape
    own = feat_index[0]
    weight_all = wide_ref[:, :width].reshape(feats * width, feats * width)
    weight_own = weight_ref[...]
    weight_term = jnp.zeros((width, feats * width), jnp.float32)
    for block in range(blocks):
        summed = summed_ref[:, block].reshape(feats * width, extent)
        pre_act = dot(summed, weight_all, TN)
        gate = jax.nn.sigmoid(pre_act)
        grad_out = wide_ref[block, width:].astype(jnp.float32)
        derivative = gate * (1.0 + pre_act * (1.0 - gate))
        grad_pre = (grad_out * derivative).astype(jnp.bfloat16)
        out_ref[block] = dot(weight_own, grad_pre, NT).astype(out_ref.dtype)
        weight_term += dot(summed_ref[own, block], grad_pre, NN)

        @pl.when(own == block)
        def _():
            act_ref[...] = (pre_act * gate).astype(act_ref.dtype)

    for part in range(feats * width // extent):
        out_ref[blocks + part] = weight_term[:, part * extent : (part + 1) * extent].astype(
            out_ref.dtype
        )


def backward_kernel(rows, cols, count, adj_ref, proj_ref, out_ref, acc_ref):
    per_col = BR_DEV // proj_ref.shape[0]
    row_devices, blocks = out_ref.shape[0], acc_ref.shape[0] // out_ref.shape[0]

    @pl.when(pl.program_id(0) == 0)
    def _():
        acc_ref[...] = jnp.zeros_like(acc_ref)

    accumulate_tiles(
        count[0],
        lambda s: proj_ref[rows[s] // per_col, rows[s] % per_col],
        adj_ref,
        acc_ref,
        lambda s: cols[s],
        NN,
    )

    @pl.when(pl.program_id(0) == pl.num_programs(0) - 1)
    def _():
        terms = jnp.sum(proj_ref[:, per_col:].astype(jnp.float32), axis=0).astype(out_ref.dtype)
        for row in range(row_devices):
            out_ref[row, :blocks] = acc_ref[row * blocks : (row + 1) * blocks].astype(
                out_ref.dtype
            )
            out_ref[row, blocks:] = terms


def tile_call(kernel, scalars, adjacency, source, out_shape, acc_shape):
    slots, extent, _ = adjacency.shape
    whole = lambda shape: pl.BlockSpec(shape, lambda i, *_: (0,) * len(shape))
    return pl.pallas_call(
        kernel,
        out_shape=jax.ShapeDtypeStruct(out_shape, jnp.bfloat16),
        grid_spec=pltpu.PrefetchScalarGridSpec(
            num_scalar_prefetch=3,
            grid=(slots // CHUNK,),
            in_specs=[
                pl.BlockSpec((CHUNK, extent, extent), lambda i, *_: (i, 0, 0)),
                whole(source.shape),
            ],
            out_specs=whole(out_shape),
            scratch_shapes=[pltpu.VMEM(acc_shape, jnp.float32)],
        ),
        compiler_params=pltpu.CompilerParams(vmem_limit_bytes=VMEM_LIMIT),
    )(*scalars, adjacency, source)


def local(features, weight, grad_out, adjacency, tile_rows, tile_cols, tile_count):
    nodes, width = features.shape
    extent = adjacency.shape[1]
    rows, cols, feats = (lax.axis_size(name) for name in ("row", "col", "feat"))
    full = feats * width
    blocks = nodes // extent
    scalars = (tile_rows, tile_cols, tile_count)

    wide = lax.all_gather(
        jnp.concatenate([weight, grad_out], axis=0), "feat", axis=0, tiled=True
    ).reshape(feats, width + extent, full)

    own = features.T.reshape(width, blocks, extent).transpose(1, 0, 2)
    gathered = lax.all_to_all(
        jnp.broadcast_to(own[None], (rows,) + own.shape), "row", 0, 0, tiled=False
    )
    gathered = gathered.reshape(rows * blocks, width, extent)

    partial_value = tile_call(
        forward_kernel,
        scalars,
        adjacency,
        gathered,
        (BR_DEV, width, extent),
        (BR_DEV, width, extent),
    )
    per_col = BR_DEV // cols
    terms = lax.all_to_all(
        partial_value.reshape(cols, per_col, width, extent), "col", 0, 0, tiled=False
    )
    summed = jnp.sum(terms.astype(jnp.float32), axis=0).astype(jnp.bfloat16)
    summed = lax.all_gather(summed, "feat", axis=0, tiled=False)

    parts = full // extent
    feat_index = lax.axis_index("feat").astype(jnp.int32).reshape(1)
    vmem = pl.BlockSpec(memory_space=pltpu.VMEM)
    outgoing, activated = pl.pallas_call(
        dense_kernel,
        out_shape=(
            jax.ShapeDtypeStruct((per_col + parts, width, extent), jnp.bfloat16),
            jax.ShapeDtypeStruct((extent, full), jnp.bfloat16),
        ),
        in_specs=[pl.BlockSpec(memory_space=pltpu.SMEM), vmem, vmem, vmem],
        out_specs=(vmem, vmem),
        compiler_params=pltpu.CompilerParams(vmem_limit_bytes=VMEM_LIMIT),
    )(feat_index, summed, wide, weight)

    projected = lax.all_gather(outgoing, "col", axis=0, tiled=False)
    pieces = tile_call(
        backward_kernel,
        scalars,
        adjacency,
        projected,
        (rows, blocks + parts, width, extent),
        (rows * blocks, width, extent),
    )
    pieces = lax.all_to_all(pieces, "row", 0, 0, tiled=False)
    total = jnp.sum(pieces.astype(jnp.float32), axis=0)
    total = total.transpose(1, 0, 2).reshape(width, (blocks + parts) * extent)
    feature_grad = total[:, :nodes].T
    weight_grad = total[:, nodes:] * (1.0 / math.sqrt(nodes * rows * cols))
    return (activated, weight_grad, feature_grad)


def solution(mesh):
    placed = (
        P(("col", "row"), "feat"),
        P("feat", None),
        P(("row", "col", "feat"), None),
        P(("row", "col"), None, None),
        P(("row", "col")),
        P(("row", "col")),
        P(("row", "col")),
    )
    return jax.shard_map(
        local,
        mesh=mesh,
        in_specs=placed,
        out_specs=(P(("row", "col", "feat"), None), P("feat", None), P(("col", "row"), "feat")),
        check_vma=False,
    )
```

time: 943 us -> 198 us (0.21)
  blocking collectives: 492 us -> 110 us
  waiting for transfers between devices: 392 us -> 33.3 us
  starting transfers between devices: 0.38 us -> 26.5 us
  matrix products: 24.2 us -> 0 us
  Pallas kernels: 0 us -> 16.5 us
  between operations: 14.6 us -> 1.34 us
    psum x1 -> x0, blocking collectives: 492 us -> none  [local(): lax.psum(weight_term, ('row', 'col')) * (1.0 / math.sqrt(node_total))]
    all_gather x2 -> x0, waiting for transfers between devices: 310 us -> none  [the longest x1 199 us: local(): block_grad = lax.all_gather(grad_pre, ('col', 'feat'), axis=0, tiled=True)]
    reduce_scatter x3 -> x0, waiting for transfers between devices: 80.6 us -> none  [the longest x1 41.2 us: local(): lax.psum_scatter(weighted, 'feat', scatter_dimension=0, tiled=True)]
    all_gather x0 -> x3, blocking collectives: none -> 68.2 us  [the longest x1 27 us: local(): projected = lax.all_gather(outgoing, 'col', axis=0, tiled=False)]
    all_to_all x0 -> x1, blocking collectives: none -> 41.9 us  [local(): pieces = lax.all_to_all(pieces, 'row', 0, 0, tiled=False)]
    all_to_all x0 -> x2, waiting for transfers between devices: none -> 33.3 us  [the longest x1 33.3 us: local(): lax.all_to_all(jnp.broadcast_to(own[None], (rows,) + own.shape), 'row', 0...]
    all_to_all x0 -> x2, starting transfers between devices: none -> 26.5 us  [the longest x1 20.4 us: local(): lax.all_to_all(jnp.broadcast_to(own[None], (rows,) + own.shape), 'row', 0...]
    dot_general x7 -> x0, matrix products: 24.2 us -> none  [the longest x1 5.38 us: local(): jnp.einsum('tab,tbf->taf', adjacency, chosen, preferred_element_type=jnp....]
  transfers between devices with their start and end apart: 5 -> 2, of which waited for: 4 -> 1; matrix products, arithmetic and copies ran while one was open for 0% -> 0% of each run, Pallas kernels for 0% -> 0%
where the time goes in v1:
time: 198 us; the launch traced here: 197 us
  blocking collectives  110 us (56%)
  waiting for transfers between devices  33.3 us (17%)
  starting transfers between devices  26.5 us (13%)
  Pallas kernels  16.5 us (8%)
  local copies, waits for them, and re-layouts  8.3 us (4%)
    all_to_all x1, blocking collectives, local(): pieces = lax.all_to_all(pieces, 'row', 0, 0, tiled=False)  41.9 us
    all_to_all x1, waiting for transfers between devices, local(): lax.all_to_all(jnp.broadcast_to(own[None], (rows,) + own.shape), 'row', 0...  33.3 us
    all_gather x1, blocking collectives, local(): projected = lax.all_gather(outgoing, 'col', axis=0, tiled=False)  27 us
    all_gather x1, blocking collectives, local(): lax.all_gather(jnp.concatenate([weight, grad_out], axis=0), 'feat', axis=...  21.4 us
    all_to_all x1, starting transfers between devices, local(): lax.all_to_all(jnp.broadcast_to(own[None], (rows,) + own.shape), 'row', 0...  20.4 us
    all_gather x1, blocking collectives, local(): summed = lax.all_gather(summed, 'feat', axis=0, tiled=False)  19.8 us
    pallas_call x2, Pallas kernels, tile_call(): pl.pallas_call(kernel, out_shape=jax.ShapeDtypeStruct(out_shape, jnp.bflo...  13.1 us
    unnamed x13, local copies, waits for them, and re-layouts  6.44 us
  transfers between devices with their start and end apart: 2, of which 1 were waited for; matrix products, arithmetic and copies ran while one was open for 0% of the time, Pallas kernels for 0%

profile of v1, /device:TPU:1, one launch (start us, length us, event | category | flops | bytes accessed | tf_op | source)
XLA Modules:
  0.0 196.9 jit_solution(7016325586084134856)
XLA Ops:
  0.6 0.9 copy.15
  1.5 1.2 broadcast_in_dim.2
  2.7 0.0 copy-start.3
  2.7 0.0 copy-start.4
  2.7 20.4 %all-to-all-start = ((bf16[16,8,32,128]{3,2,1,0:T(8,128)(2,1)}), bf16[16,8,32,128]{3,2,1,0:T(8,128)(2,1)S(1)}, u32[]{:S(2)}, u32[]{:S(2)}) async-start(bf16[16,8,32,128]{3,2,1,0:T(8,128)(2,1)} %broadcast_in_dim.2), calls=%async_computation | async-start | bytes 2097152 | tf_op jit(solution)/shard_map/all_to_all | solution.py:142
  23.8 33.3 %all-to-all-done = bf16[16,8,32,128]{3,2,1,0:T(8,128)(2,1)S(1)} async-done(((bf16[16,8,32,128]{3,2,1,0:T(8,128)(2,1)}), bf16[16,8,32,128]{3,2,1,0:T(8,128)(2,1)S(1)}, u32[]{:S(2)}, u32[]{:S(2)}) %all-to-all-start) | async-done | bytes 1048608 | tf_op jit(solution)/shard_map/all_to_all | solution.py:142
  57.0 0.0 copy-done.3
  57.0 0.0 copy-done.4
  57.0 0.0 copy-start
  57.0 2.8 %copy-done = bf16[192,128,128]{2,1,0:T(8,128)(2,1)S(1)} copy-done((bf16[192,128,128]{2,1,0:T(8,128)(2,1)S(1)}, bf16[192,128,128]{2,1,0:T(8,128)(2,1)}, u32[]{:S(2)}) %copy-start) | copy-done | bytes 6291480
  59.8 0.0 copy-start.2
  59.8 0.0 copy-start.5
  59.8 7.6 %shard_map.94 = bf16[64,32,128]{2,1,0:T(8,128)(2,1)} custom-call(s32[192]{0:T(256)S(1)} %copy-done.3, s32[192]{0:T(256)S(1)} %copy-done.4, s32[1]{0:T(128)S(6)} %copy.17.count, bf16[192,128,128]{2,1,0:T(8,128)(2,1)S(1)} %copy-done, bf16[128,32,128]{2,1,0:T(8,128)(2,1)S(1)} %bitcast.19), custom_call_target="tpu_custom_call" | custom-call | tf_op jit(solution)/shard_map/pallas_call | solution.py:112
  67.5 6.1 %all-to-all-start.1 = ((bf16[8,8,32,128]{3,2,1,0:T(8,128)(2,1)}), bf16[8,8,32,128]{3,2,1,0:T(8,128)(2,1)S(1)}, u32[]{:S(2)}, u32[]{:S(2)}) async-start(bf16[8,8,32,128]{3,2,1,0:T(8,128)(2,1)} %bitcast.4), calls=%async_computation.1 | async-start | bytes 1048576 | tf_op jit(solution)/shard_map/all_to_all | solution.py:156
  73.5 0.0 copy-done.2
  73.5 0.0 copy-done.5
  73.6 21.4 %all_gather.17 = bf16[1280,256]{1,0:T(8,128)(2,1)S(1)} all-gather(bf16[160,256]{1,0:T(8,128)(2,1)S(1)} %pad_maximum_fusion), channel_id=1, replica_groups=mesh['row'=16,'col'=8,'feat'=8] {'feat'}, dimensions={0}, use_global_device_ids=true | all-gather | bytes 737280 | tf_op jit(solution)/shard_map/all_gather | solution.py:137
  95.0 0.0 all-to-all-done.1
  95.0 0.1 reduce_sum.21
  95.0 19.8 %all-gather = bf16[64,32,128]{2,1,0:T(8,128)(2,1)S(1)} all-gather(bf16[8,32,128]{2,1,0:T(8,128)(2,1)S(1)} %reduce_sum.21), channel_id=2, replica_groups=mesh['row'=16,'col'=8,'feat'=8] {'feat'}, dimensions={0}, use_global_device_ids=true | all-gather | bytes 589824 | tf_op jit(solution)/shard_map/all_gather | solution.py:160
  114.9 3.4 %shard_map.95 = (bf16[10,32,128]{2,1,0:T(8,128)(2,1)S(1)}, bf16[128,256]{1,0:T(8,128)(2,1)}) custom-call(s32[1]{0:T(128)} %bitcast.feat_index, bf16[8,8,32,128]{3,2,1,0:T(8,128)(2,1)S(1)} %bitcast.22, bf16[8,160,256]{2,1,0:T(8,128)(2,1)S(1)} %bitcast.21, bf16[32,256]{1,0:T(8,128)(2,1)S(1)} %copy-done.2), custom_call_target="tpu_custom_call" | custom-call | tf_op jit(solution)/shard_map/pallas_call | solution.py:165
  118.3 27.0 %all-gather.1 = bf16[80,32,128]{2,1,0:T(8,128)(2,1)S(1)} all-gather(bf16[10,32,128]{2,1,0:T(8,128)(2,1)S(1)} %get-tuple-element.6), channel_id=3, replica_groups=mesh['row'=16,'col'=8,'feat'=8] {'col'}, dimensions={0}, use_global_device_ids=true | all-gather | bytes 737280 | tf_op jit(solution)/shard_map/all_gather | solution.py:176
  145.3 0.0 copy-start.1
  145.3 2.8 %copy-done.1 = bf16[192,128,128]{2,1,0:T(8,128)(2,1)S(1)} copy-done((bf16[192,128,128]{2,1,0:T(8,128)(2,1)S(1)}, bf16[192,128,128]{2,1,0:T(8,128)(2,1)}, u32[]{:S(2)}) %copy-start.1) | copy-done | bytes 6291480
  148.1 5.4 %shard_map.96 = bf16[16,10,32,128]{3,2,1,0:T(8,128)(2,1)S(1)} custom-call(s32[192]{0:T(256)S(1)} %copy-done.3, s32[192]{0:T(256)S(1)} %copy-done.4, s32[1]{0:T(128)S(6)} %copy.17.count, bf16[192,128,128]{2,1,0:T(8,128)(2,1)S(1)} %copy-done.1, bf16[8,10,32,128]{3,2,1,0:T(8,128)(2,1)S(1)} %bitcast.20), custom_call_target="tpu_custom_call" | custom-call | tf_op jit(solution)/shard_map/pallas_call | solution.py:112
  153.5 41.9 %all_to_all.15 = bf16[16,10,32,128]{3,2,1,0:T(8,128)(2,1)S(1)} all-to-all(bf16[16,10,32,128]{3,2,1,0:T(8,128)(2,1)S(1)} %shard_map.96), channel_id=1, replica_groups=mesh['row'=16,'col'=8,'feat'=8] {'row'}, dimensions={0} | all-to-all | bytes 2621440 | tf_op jit(solution)/shard_map/all_to_all | solution.py:185
  195.4 0.2 convert_reduce_fusion
  195.6 0.6 slice_multiply_fusion
  196.3 0.7 slice_bitcast_fusion
  (3 shorter events, 0.0 us)
Async XLA Ops:
  2.7 54.4 %copy-start.3 = (s32[192]{0:T(256)S(1)}, s32[192]{0:T(256)}, u32[]{:S(2)}) copy-start(s32[192]{0:T(256)} %rows.3) | copy-start | bytes 2308
  2.7 54.4 %copy-start.4 = (s32[192]{0:T(256)S(1)}, s32[192]{0:T(256)}, u32[]{:S(2)}) copy-start(s32[192]{0:T(256)} %cols.3) | copy-start | bytes 2308
  2.7 54.4 %all-to-all-start = ((bf16[16,8,32,128]{3,2,1,0:T(8,128)(2,1)}), bf16[16,8,32,128]{3,2,1,0:T(8,128)(2,1)S(1)}, u32[]{:S(2)}, u32[]{:S(2)}) async-start(bf16[16,8,32,128]{3,2,1,0:T(8,128)(2,1)} %broadcast_in_dim.2), calls=%async_computation | async-start | bytes 2097152 | tf_op jit(solution)/shard_map/all_to_all | solution.py:142
  57.0 2.8 %copy-start = (bf16[192,128,128]{2,1,0:T(8,128)(2,1)S(1)}, bf16[192,128,128]{2,1,0:T(8,128)(2,1)}, u32[]{:S(2)}) copy-start(bf16[192,128,128]{2,1,0:T(8,128)(2,1)} %adj_ref.3) | copy-start | bytes 18874372
  59.8 13.7 %copy-start.2 = (bf16[32,256]{1,0:T(8,128)(2,1)S(1)}, bf16[32,256]{1,0:T(8,128)(2,1)}, u32[]{:S(2)}) copy-start(bf16[32,256]{1,0:T(8,128)(2,1)} %weight_ref.1) | copy-start | bytes 49156
  59.8 13.7 %copy-start.5 = (bf16[128,256]{1,0:T(8,128)(2,1)S(1)}, bf16[128,256]{1,0:T(8,128)(2,1)}, u32[]{:S(2)}) copy-start(bf16[128,256]{1,0:T(8,128)(2,1)} %param.9) | copy-start | bytes 196612
  67.5 27.5 %all-to-all-start.1 = ((bf16[8,8,32,128]{3,2,1,0:T(8,128)(2,1)}), bf16[8,8,32,128]{3,2,1,0:T(8,128)(2,1)S(1)}, u32[]{:S(2)}, u32[]{:S(2)}) async-start(bf16[8,8,32,128]{3,2,1,0:T(8,128)(2,1)} %bitcast.4), calls=%async_computation.1 | async-start | bytes 1048576 | tf_op jit(solution)/shard_map/all_to_all | solution.py:156
  145.3 2.8 %copy-start.1 = (bf16[192,128,128]{2,1,0:T(8,128)(2,1)S(1)}, bf16[192,128,128]{2,1,0:T(8,128)(2,1)}, u32[]{:S(2)}) copy-start(bf16[192,128,128]{2,1,0:T(8,128)(2,1)} %adj_ref.3) | copy-start | bytes 18874372

commit v2 on v1

v2 whole, which is shorter than its diff:
```python
import math

import jax
import jax.numpy as jnp
from jax import lax
from jax.experimental import pallas as pl
from jax.experimental.pallas import tpu as pltpu
from jax.sharding import PartitionSpec as P

CHUNK = 24
UNROLL = 8
PIECE = 8
VMEM_LIMIT = 58 * 1024 * 1024
NT = (((1,), (1,)), ((), ()))
NN = (((1,), (0,)), ((), ()))
TN = (((0,), (0,)), ((), ()))


def dot(a, b, dims):
    return lax.dot_general(a, b, dims, preferred_element_type=jnp.float32)


def accumulate_tiles(count, source, adj_ref, acc_ref, target_of, dims):
    first = pl.program_id(0) * CHUNK

    @pl.when(first < count)
    def _():
        @pl.loop(0, CHUNK // UNROLL)
        def _(group):
            base = group * UNROLL
            terms = []
            for u in range(UNROLL):
                slot = first + base + u
                term = dot(source(slot), adj_ref[base + u], dims)
                terms.append(jnp.where(slot < count, term, 0.0))
            for u in range(UNROLL):
                target = target_of(first + base + u)
                acc_ref[target] += terms[u]


def forward_kernel(rows, cols, count, adj_ref, feat_ref, out_ref, acc_ref):
    extent = adj_ref.shape[1]
    blocks = feat_ref.shape[2] // extent

    @pl.when(pl.program_id(0) == 0)
    def _():
        acc_ref[...] = jnp.zeros_like(acc_ref)

    def source(slot):
        col = cols[slot]
        start = pl.multiple_of((col % blocks) * extent, extent)
        return feat_ref[col // blocks, :, pl.ds(start, extent)]

    accumulate_tiles(count[0], source, adj_ref, acc_ref, lambda s: rows[s], NT)

    @pl.when(pl.program_id(0) == pl.num_programs(0) - 1)
    def _():
        out_ref[...] = acc_ref[...].astype(out_ref.dtype)


def dense_kernel(terms_ref, weight_ref, grad_ref, out_ref, act_ref):
    cols, feats, width, extent = terms_ref.shape
    full = feats * width
    weight = weight_ref[...]
    summed = jnp.sum(terms_ref[...].astype(jnp.float32), axis=0).reshape(full, extent)
    high = summed.astype(jnp.bfloat16)
    low = (summed - high.astype(jnp.float32)).astype(jnp.bfloat16)
    pre_act = dot(high, weight, TN) + dot(low, weight, TN)
    gate = jax.nn.sigmoid(pre_act)
    act_ref[...] = (pre_act * gate).astype(act_ref.dtype)
    derivative = gate * (1.0 + pre_act * (1.0 - gate))
    grad_pre = (grad_ref[...].astype(jnp.float32) * derivative).astype(jnp.bfloat16)
    projected = dot(weight, grad_pre, NT).astype(out_ref.dtype)
    weight_term = dot(high, grad_pre, NN) + dot(low, grad_pre, NN)
    halves = full // extent
    for col in range(cols):
        for feat in range(feats):
            top = feat * width + (col // halves) * PIECE
            left = (col % halves) * extent
            out_ref[col * feats + feat, :width] = projected[feat * width : (feat + 1) * width]
            out_ref[col * feats + feat, width:] = weight_term[
                top : top + PIECE, left : left + extent
            ].astype(out_ref.dtype)


def backward_kernel(rows, cols, count, adj_ref, proj_ref, out_ref, acc_ref):
    row_devices = out_ref.shape[0]
    blocks, width = acc_ref.shape[0] // row_devices, acc_ref.shape[1]

    @pl.when(pl.program_id(0) == 0)
    def _():
        acc_ref[...] = jnp.zeros_like(acc_ref)

    accumulate_tiles(
        count[0], lambda s: proj_ref[rows[s], :width], adj_ref, acc_ref, lambda s: cols[s], NN
    )

    @pl.when(pl.program_id(0) == pl.num_programs(0) - 1)
    def _():
        weight_term = jnp.sum(proj_ref[:, width:].astype(jnp.float32), axis=0)
        for row in range(row_devices):
            for block in range(blocks):
                out_ref[row, block * width : (block + 1) * width] = acc_ref[
                    row * blocks + block
                ].astype(out_ref.dtype)
            out_ref[row, blocks * width :] = weight_term.astype(out_ref.dtype)


def final_kernel(scale, pieces_ref, grad_ref, weight_ref):
    width, nodes = grad_ref.shape
    extent = pieces_ref.shape[2]
    for block in range(nodes // extent):
        grad_ref[:, block * extent : (block + 1) * extent] = jnp.sum(
            pieces_ref[:, block * width : (block + 1) * width].astype(jnp.float32), axis=0
        )
    rest = pieces_ref[:, nodes // extent * width :].astype(jnp.float32)
    weight_ref[...] = jnp.sum(rest, axis=0) * scale


def tile_call(kernel, scalars, adjacency, source, out_shape, acc_shape):
    slots, extent, _ = adjacency.shape
    whole = lambda shape: pl.BlockSpec(shape, lambda i, *_: (0,) * len(shape))
    return pl.pallas_call(
        kernel,
        out_shape=jax.ShapeDtypeStruct(out_shape, jnp.bfloat16),
        grid_spec=pltpu.PrefetchScalarGridSpec(
            num_scalar_prefetch=3,
            grid=(slots // CHUNK,),
            in_specs=[
                pl.BlockSpec((CHUNK, extent, extent), lambda i, *_: (i, 0, 0)),
                whole(source.shape),
            ],
            out_specs=whole(out_shape),
            scratch_shapes=[pltpu.VMEM(acc_shape, jnp.float32)],
        ),
        compiler_params=pltpu.CompilerParams(vmem_limit_bytes=VMEM_LIMIT),
    )(*scalars, adjacency, source)


def local(features, weight, grad_out, adjacency, tile_rows, tile_cols, tile_count):
    nodes, width = features.shape
    extent = adjacency.shape[1]
    rows, cols, feats = (lax.axis_size(name) for name in ("row", "col", "feat"))
    full = feats * width
    blocks = nodes // extent
    owners = cols * feats
    scalars = (tile_rows, tile_cols, tile_count)
    vmem = pl.BlockSpec(memory_space=pltpu.VMEM)

    weight_all = lax.all_gather(weight, "feat", axis=0, tiled=True)
    own = features.T
    gathered = lax.all_to_all(
        jnp.broadcast_to(own[None], (rows,) + own.shape), "row", 0, 0, tiled=False
    )
    gathered, weight_all = lax.optimization_barrier((gathered, weight_all))

    terms = tile_call(
        forward_kernel,
        scalars,
        adjacency,
        gathered,
        (owners, width, extent),
        (owners, width, extent),
    )
    terms = lax.all_to_all(terms, ("col", "feat"), 0, 0, tiled=False)
    outgoing, activated = pl.pallas_call(
        dense_kernel,
        out_shape=(
            jax.ShapeDtypeStruct((owners, width + PIECE, extent), jnp.bfloat16),
            jax.ShapeDtypeStruct((extent, full), jnp.bfloat16),
        ),
        in_specs=[vmem, vmem, vmem],
        out_specs=(vmem, vmem),
    )(terms.reshape(cols, feats, width, extent), weight_all, grad_out)

    projected = lax.all_to_all(outgoing, ("col", "feat"), 0, 0, tiled=False)
    pieces = tile_call(
        backward_kernel,
        scalars,
        adjacency,
        projected,
        (rows, blocks * width + PIECE, extent),
        (rows * blocks, width, extent),
    )
    pieces = lax.all_to_all(pieces, "row", 0, 0, tiled=False)
    scale = 1.0 / math.sqrt(nodes * rows * cols)
    feature_grad, weight_piece = pl.pallas_call(
        lambda *refs: final_kernel(scale, *refs),
        out_shape=(
            jax.ShapeDtypeStruct((width, nodes), jnp.float32),
            jax.ShapeDtypeStruct((PIECE, extent), jnp.float32),
        ),
        in_specs=[vmem],
        out_specs=(vmem, vmem),
    )(pieces)
    weight_grad = lax.all_gather(weight_piece, "col", axis=0, tiled=True)
    weight_grad = weight_grad.reshape(width // PIECE, full // extent, PIECE, extent)
    weight_grad = weight_grad.transpose(0, 2, 1, 3).reshape(width, full)
    return (activated, weight_grad, feature_grad.T)


def solution(mesh):
    placed = (
        P(("col", "row"), "feat"),
        P("feat", None),
        P(("row", "col", "feat"), None),
        P(("row", "col"), None, None),
        P(("row", "col")),
        P(("row", "col")),
        P(("row", "col")),
    )
    return jax.shard_map(
        local,
        mesh=mesh,
        in_specs=placed,
        out_specs=(P(("row", "col", "feat"), None), P("feat", None), P(("col", "row"), "feat")),
        check_vma=False,
    )
```

time: 198 us -> 197 us (level)
  blocking collectives: 110 us -> 138 us
  waiting for transfers between devices: 33.3 us -> 11 us
  starting transfers between devices: 26.5 us -> 20.4 us
  local copies, waits for them, and re-layouts: 8.3 us -> 3.53 us
  Pallas kernels: 16.5 us -> 21.1 us
    all_to_all x0 -> x2, blocking collectives: none -> 58.6 us  [the longest x1 32.4 us: local(): terms = lax.all_to_all(terms, ('col', 'feat'), 0, 0, tiled=False)]
    all_gather x3 -> x2, blocking collectives: 68.2 us -> 38.3 us  [the longest x1 22.2 us: local(): weight_all = lax.all_gather(weight, 'feat', axis=0, tiled=True)]
    all_to_all x1, waiting for transfers between devices: 33.3 us -> 11 us  [local(): lax.all_to_all(jnp.broadcast_to(own[None], (rows,) + own.shape), 'row', 0...]
    all_to_all x1 -> x0, starting transfers between devices: 6.06 us -> none  [local(): lax.all_to_all(partial_value.reshape(cols, per_col, width, extent), 'col'...]
    unnamed x13 -> x5, local copies, waits for them, and re-layouts: 6.44 us -> 1.59 us
    pallas_call x2, Pallas kernels: 13.1 us -> 16.5 us  [tile_call(): pl.pallas_call(kernel, out_shape=jax.ShapeDtypeStruct(out_shape, jnp.bflo...]
    pallas_call x1 -> x2, Pallas kernels: 3.42 us -> 4.59 us  [the longest x1 2.56 us: local(): pl.pallas_call(dense_kernel, out_shape=(jax.ShapeDtypeStruct((owners, wid...]
  transfers between devices with their start and end apart: 2 -> 1, of which waited for: 1 -> 1; matrix products, arithmetic and copies ran while one was open for 0% -> 0% of each run, Pallas kernels for 0% -> 0%
where the time goes in v2:
time: 197 us; the launch traced here: 196 us
  blocking collectives  138 us (70%)
  Pallas kernels  21.1 us (11%)
  starting transfers between devices  20.4 us (10%)
  waiting for transfers between devices  11 us (6%)
  local copies, waits for them, and re-layouts  3.53 us (2%)
    all_to_all x1, blocking collectives, local(): pieces = lax.all_to_all(pieces, 'row', 0, 0, tiled=False)  41.4 us
    all_to_all x1, blocking collectives, local(): terms = lax.all_to_all(terms, ('col', 'feat'), 0, 0, tiled=False)  32.4 us
    all_to_all x1, blocking collectives, local(): projected = lax.all_to_all(outgoing, ('col', 'feat'), 0, 0, tiled=False)  26.3 us
    all_gather x1, blocking collectives, local(): weight_all = lax.all_gather(weight, 'feat', axis=0, tiled=True)  22.2 us
    all_to_all x1, starting transfers between devices, local(): lax.all_to_all(jnp.broadcast_to(own[None], (rows,) + own.shape), 'row', 0...  20.4 us
    pallas_call x2, Pallas kernels, tile_call(): pl.pallas_call(kernel, out_shape=jax.ShapeDtypeStruct(out_shape, jnp.bflo...  16.5 us
    all_gather x1, blocking collectives, local(): weight_grad = lax.all_gather(weight_piece, 'col', axis=0, tiled=True)  16.1 us
    all_to_all x1, waiting for transfers between devices, local(): lax.all_to_all(jnp.broadcast_to(own[None], (rows,) + own.shape), 'row', 0...  11 us
  transfers between devices with their start and end apart: 1, of which 1 were waited for; matrix products, arithmetic and copies ran while one was open for 0% of the time, Pallas kernels for 0%

profile of v2, /device:TPU:1, one launch (start us, length us, event | category | flops | bytes accessed | tf_op | source)
XLA Modules:
  0.0 195.8 jit_solution(1871969348285759056)
XLA Ops:
  0.6 1.9 broadcast_in_dim.2
  2.6 0.0 copy-start.1
  2.6 20.4 %all-to-all-start = ((bf16[16,32,1024]{2,1,0:T(8,128)(2,1)}), bf16[16,32,1024]{2,1,0:T(8,128)(2,1)S(1)}, u32[]{:S(2)}, u32[]{:S(2)}) async-start(bf16[16,32,1024]{2,1,0:T(8,128)(2,1)} %broadcast_in_dim.2), calls=%async_computation | async-start | bytes 2097152 | tf_op jit(solution)/shard_map/all_to_all | solution.py:152
  23.7 0.0 copy-done.1
  23.7 22.2 %all_gather.6.weight_ref = bf16[256,256]{1,0:T(8,128)(2,1)} all-gather(bf16[32,256]{1,0:T(8,128)(2,1)S(1)} %copy-done.1), channel_id=1, replica_groups=mesh['row'=16,'col'=8,'feat'=8] {'feat'}, dimensions={0}, use_global_device_ids=true | all-gather | bytes 147456 | tf_op jit(solution)/shard_map/all_gather | solution.py:150
  45.9 11.0 %all-to-all-done.feat_ref = bf16[16,32,1024]{2,1,0:T(8,128)(2,1)S(1)} async-done(((bf16[16,32,1024]{2,1,0:T(8,128)(2,1)}), bf16[16,32,1024]{2,1,0:T(8,128)(2,1)S(1)}, u32[]{:S(2)}, u32[]{:S(2)}) %all-to-all-start) | async-done | bytes 1048608 | tf_op jit(solution)/shard_map/all_to_all | solution.py:152
  56.9 0.0 copy-start
  56.9 1.0 copy-done
  57.9 8.4 %shard_map.94 = bf16[64,32,128]{2,1,0:T(8,128)(2,1)} custom-call(s32[192]{0:T(256)} %rows.3, s32[192]{0:T(256)} %cols.3, s32[1]{0:T(128)S(6)} %copy.11.count, bf16[192,128,128]{2,1,0:T(8,128)(2,1)} %adj_ref.3, bf16[16,32,1024]{2,1,0:T(8,128)(2,1)} %copy-done), custom_call_target="tpu_custom_call" | custom-call | tf_op jit(solution)/shard_map/pallas_call | solution.py:123
  66.3 32.4 %all_to_all.20 = bf16[64,32,128]{2,1,0:T(8,128)(2,1)} all-to-all(bf16[64,32,128]{2,1,0:T(8,128)(2,1)} %shard_map.94), channel_id=1, replica_groups=mesh['row'=16,'col'=8,'feat'=8] {'col','feat'}, dimensions={0} | all-to-all | bytes 1048576 | tf_op jit(solution)/shard_map/all_to_all | solution.py:165
  98.6 2.6 %shard_map.95 = (bf16[64,40,128]{2,1,0:T(8,128)(2,1)}, bf16[128,256]{1,0:T(8,128)(2,1)}) custom-call(bf16[8,8,32,128]{3,2,1,0:T(8,128)(2,1)} %bitcast.8, bf16[256,256]{1,0:T(8,128)(2,1)} %all_gather.6.weight_ref, bf16[128,256]{1,0:T(8,128)(2,1)} %grad_ref.1), custom_call_target="tpu_custom_call" | custom-call | tf_op jit(solution)/shard_map/pallas_call | solution.py:166
  101.2 26.3 %all_to_all.21.proj_ref = bf16[64,40,128]{2,1,0:T(8,128)(2,1)} all-to-all(bf16[64,40,128]{2,1,0:T(8,128)(2,1)} %get-tuple-element.12), channel_id=1, replica_groups=mesh['row'=16,'col'=8,'feat'=8] {'col','feat'}, dimensions={0} | all-to-all | bytes 1310720 | tf_op jit(solution)/shard_map/all_to_all | solution.py:176
  127.5 8.1 %shard_map.96 = bf16[16,264,128]{2,1,0:T(8,128)(2,1)} custom-call(s32[192]{0:T(256)} %rows.3, s32[192]{0:T(256)} %cols.3, s32[1]{0:T(128)S(6)} %copy.11.count, bf16[192,128,128]{2,1,0:T(8,128)(2,1)} %adj_ref.3, bf16[64,40,128]{2,1,0:T(8,128)(2,1)} %all_to_all.21.proj_ref), custom_call_target="tpu_custom_call" | custom-call | tf_op jit(solution)/shard_map/pallas_call | solution.py:123
  135.6 41.4 %all_to_all.22.refs_0_ = bf16[16,264,128]{2,1,0:T(8,128)(2,1)} all-to-all(bf16[16,264,128]{2,1,0:T(8,128)(2,1)} %shard_map.96), channel_id=1, replica_groups=mesh['row'=16,'col'=8,'feat'=8] {'row'}, dimensions={0} | all-to-all | bytes 2162688 | tf_op jit(solution)/shard_map/all_to_all | solution.py:185
  177.0 2.0 %shard_map.97 = (f32[32,1024]{1,0:T(8,128)}, f32[8,128]{1,0:T(8,128)}) custom-call(bf16[16,264,128]{2,1,0:T(8,128)(2,1)} %all_to_all.22.refs_0_), custom_call_target="tpu_custom_call" | custom-call | tf_op jit(solution)/shard_map/pallas_call | solution.py:187
  179.0 16.1 %all_gather.7 = f32[64,128]{1,0:T(8,128)S(1)} all-gather(f32[8,128]{1,0:T(8,128)} %get-tuple-element.13), channel_id=1, replica_groups=mesh['row'=16,'col'=8,'feat'=8] {'col'}, dimensions={0}, use_global_device_ids=true | all-gather | bytes 36864 | tf_op jit(solution)/shard_map/all_gather | solution.py:196
  195.1 0.6 copy.12
Async XLA Ops:
  2.6 21.1 %copy-start.1 = (bf16[32,256]{1,0:T(8,128)(2,1)S(1)}, bf16[32,256]{1,0:T(8,128)(2,1)}, u32[]{:S(2)}) copy-start(bf16[32,256]{1,0:T(8,128)(2,1)} %param.8) | copy-start | bytes 49156
  2.6 54.4 %all-to-all-start = ((bf16[16,32,1024]{2,1,0:T(8,128)(2,1)}), bf16[16,32,1024]{2,1,0:T(8,128)(2,1)S(1)}, u32[]{:S(2)}, u32[]{:S(2)}) async-start(bf16[16,32,1024]{2,1,0:T(8,128)(2,1)} %broadcast_in_dim.2), calls=%async_computation | async-start | bytes 2097152 | tf_op jit(solution)/shard_map/all_to_all | solution.py:152
  56.9 1.0 copy-start

commit v3 on v2

v3 whole, which is shorter than its diff:
```python
import math

import jax
import jax.numpy as jnp
from jax import lax
from jax.experimental import pallas as pl
from jax.experimental.pallas import tpu as pltpu
from jax.sharding import PartitionSpec as P

UNROLL = 8
PIECE = 16
CORES = 2
VMEM_LIMIT = 24 * 1024 * 1024
NT = (((1,), (1,)), ((), ()))
NN = (((1,), (0,)), ((), ()))
TN = (((0,), (0,)), ((), ()))


def dot(a, b, dims):
    return lax.dot_general(a, b, dims, preferred_element_type=jnp.float32)


def stage_kernel(source_ref, out_ref, done):
    copy = pltpu.make_async_copy(source_ref, out_ref, done)
    copy.start()
    copy.wait()


def accumulate_tiles(count, source, adj_ref, acc_ref, target_of, dims):
    acc_ref[...] = jnp.zeros_like(acc_ref)

    @pl.loop(0, adj_ref.shape[0] // UNROLL)
    def _(group):
        first = group * UNROLL

        @pl.when(first < count)
        def _():
            terms = []
            for u in range(UNROLL):
                term = dot(source(first + u), adj_ref[first + u], dims)
                terms.append(jnp.where(first + u < count, term, 0.0))
            for u in range(UNROLL):
                target = target_of(first + u)
                acc_ref[target] += terms[u]


def forward_kernel(core, rows, cols, count, adj_ref, feat_ref, keep_ref, send_ref, acc_ref):
    extent = adj_ref.shape[1]
    blocks = feat_ref.shape[2] // extent

    def source(slot):
        col = cols[slot]
        start = pl.multiple_of((col % blocks) * extent, extent)
        return feat_ref[col // blocks, :, pl.ds(start, extent)]

    accumulate_tiles(count[0], source, adj_ref, acc_ref, lambda s: rows[s], NT)
    near, feats = keep_ref.shape[:2]
    for pair in range(near):
        keep_ref[pair] = acc_ref[pl.ds((pair * CORES + core[0]) * feats, feats)]
        send_ref[pair] = acc_ref[pl.ds((pair * CORES + 1 - core[0]) * feats, feats)]


def dense_kernel(terms_ref, weight_ref, grad_ref, out_ref, act_ref):
    near, feats, width, extent = terms_ref.shape
    full = feats * width
    weight = weight_ref[...]
    summed = jnp.sum(terms_ref[...].astype(jnp.float32), axis=0).reshape(full, extent)
    high = summed.astype(jnp.bfloat16)
    low = (summed - high.astype(jnp.float32)).astype(jnp.bfloat16)
    pre_act = dot(high, weight, TN) + dot(low, weight, TN)
    gate = jax.nn.sigmoid(pre_act)
    act_ref[...] = (pre_act * gate).astype(act_ref.dtype)
    derivative = gate * (1.0 + pre_act * (1.0 - gate))
    grad_pre = (grad_ref[...].astype(jnp.float32) * derivative).astype(jnp.bfloat16)
    projected = dot(weight, grad_pre, NT).astype(out_ref.dtype)
    weight_term = (dot(high, grad_pre, NN) + dot(low, grad_pre, NN)).astype(out_ref.dtype)
    halves = full // extent
    for pair in range(near):
        for feat in range(feats):
            top = feat * width + (pair // halves) * PIECE
            left = (pair % halves) * extent
            out_ref[pair * feats + feat, :width] = projected[feat * width : (feat + 1) * width]
            out_ref[pair * feats + feat, width:] = weight_term[
                top : top + PIECE, left : left + extent
            ]


def backward_kernel(
    core, rows, cols, count, adj_ref, mine_ref, other_ref, out_ref, proj_ref, acc_ref
):
    row_devices = out_ref.shape[0]
    blocks, width = acc_ref.shape[0] // row_devices, acc_ref.shape[1]
    feats = proj_ref.shape[2]
    for pair in range(proj_ref.shape[0]):
        part = slice(pair * feats, (pair + 1) * feats)
        proj_ref[pair, core[0]] = mine_ref[part, :width]
        proj_ref[pair, 1 - core[0]] = other_ref[part, :width]

    def source(slot):
        row = rows[slot]
        return proj_ref[row // (CORES * feats), (row // feats) % CORES, row % feats]

    accumulate_tiles(count[0], source, adj_ref, acc_ref, lambda s: cols[s], NN)
    weight_term = jnp.sum(mine_ref[:, width:].astype(jnp.float32), axis=0) + jnp.sum(
        other_ref[:, width:].astype(jnp.float32), axis=0
    )
    for row in range(row_devices):
        for block in range(blocks):
            out_ref[row, block * width : (block + 1) * width] = acc_ref[
                row * blocks + block
            ].astype(out_ref.dtype)
        out_ref[row, blocks * width :] = weight_term.astype(out_ref.dtype)


def final_kernel(scale, pieces_ref, grad_ref, weight_ref):
    width, nodes = grad_ref.shape
    extent = pieces_ref.shape[2]
    for block in range(nodes // extent):
        grad_ref[:, block * extent : (block + 1) * extent] = jnp.sum(
            pieces_ref[:, block * width : (block + 1) * width].astype(jnp.float32), axis=0
        )
    rest = pieces_ref[:, nodes // extent * width :].astype(jnp.float32)
    weight_ref[...] = jnp.sum(rest, axis=0) * scale


SMEM_SPEC = pl.BlockSpec(memory_space=pltpu.SMEM)
VMEM_SPEC = pl.BlockSpec(memory_space=pltpu.VMEM)


def stage(array):
    return pl.pallas_call(
        stage_kernel,
        out_shape=pltpu.VMEM(array.shape, array.dtype),
        in_specs=[pl.BlockSpec(memory_space=pltpu.HBM)],
        out_specs=VMEM_SPEC,
        scratch_shapes=[pltpu.SemaphoreType.DMA],
        compiler_params=pltpu.CompilerParams(vmem_limit_bytes=VMEM_LIMIT),
        cost_estimate=pl.CostEstimate(
            flops=0, bytes_accessed=2 * array.size * 2, transcendentals=0
        ),
    )(pltpu.with_memory_space_constraint(array, pltpu.HBM))


def tile_call(kernel, scalars, adjacency, sources, out_shapes, scratch):
    return pl.pallas_call(
        kernel,
        out_shape=out_shapes,
        in_specs=[SMEM_SPEC] * len(scalars) + [VMEM_SPEC] * (1 + len(sources)),
        out_specs=jax.tree.map(lambda _: VMEM_SPEC, out_shapes),
        scratch_shapes=scratch,
        compiler_params=pltpu.CompilerParams(vmem_limit_bytes=VMEM_LIMIT),
    )(*scalars, pltpu.with_memory_space_constraint(adjacency, pltpu.VMEM), *sources)


def local(features, weight, grad_out, adjacency, tile_rows, tile_cols, tile_count):
    nodes, width = features.shape
    extent = adjacency.shape[1]
    rows, near, feats = (lax.axis_size(name) for name in ("row", "near", "feat"))
    full = feats * width
    blocks = nodes // extent
    owners = near * feats
    swap = [(i, CORES - 1 - i) for i in range(CORES)]
    core = lax.axis_index("core").astype(jnp.int32).reshape(1)
    scalars = (core, tile_rows, tile_cols, tile_count)

    weight_all = lax.all_gather(weight, "feat", axis=0, tiled=True)
    adjacency = stage(adjacency)
    own = features.T
    gathered = lax.all_to_all(
        jnp.broadcast_to(own[None], (rows,) + own.shape), "row", 0, 0, tiled=False
    )
    gathered, weight_all, adjacency = lax.optimization_barrier((gathered, weight_all, adjacency))

    half = jax.ShapeDtypeStruct((near, feats, width, extent), jnp.float32)
    keep, send = tile_call(
        forward_kernel,
        scalars,
        adjacency,
        (gathered,),
        (half, half),
        [pltpu.VMEM((CORES * owners, width, extent), jnp.float32)],
    )
    terms = (keep + lax.ppermute(send, "core", swap)).astype(jnp.bfloat16)
    terms = lax.all_to_all(
        terms.reshape(owners, width, extent), ("near", "feat"), 0, 0, tiled=False
    )
    outgoing, activated = pl.pallas_call(
        dense_kernel,
        out_shape=(
            jax.ShapeDtypeStruct((owners, width + PIECE, extent), jnp.bfloat16),
            jax.ShapeDtypeStruct((extent, full), jnp.bfloat16),
        ),
        in_specs=[VMEM_SPEC] * 3,
        out_specs=(VMEM_SPEC, VMEM_SPEC),
    )(terms.reshape(near, feats, width, extent), weight_all, grad_out)

    mine = lax.all_to_all(outgoing, ("near", "feat"), 0, 0, tiled=False)
    other = lax.ppermute(mine, "core", swap)
    pieces = tile_call(
        backward_kernel,
        scalars,
        adjacency,
        (mine, other),
        jax.ShapeDtypeStruct((rows, blocks * width + PIECE, extent), jnp.bfloat16),
        [
            pltpu.VMEM((near, CORES, feats, width, extent), jnp.bfloat16),
            pltpu.VMEM((rows * blocks, width, extent), jnp.float32),
        ],
    )
    pieces = lax.all_to_all(pieces, "row", 0, 0, tiled=False)
    scale = 1.0 / math.sqrt(nodes * rows * near * CORES)
    feature_grad, weight_piece = pl.pallas_call(
        lambda *refs: final_kernel(scale, *refs),
        out_shape=(
            jax.ShapeDtypeStruct((width, nodes), jnp.float32),
            jax.ShapeDtypeStruct((PIECE, extent), jnp.float32),
        ),
        in_specs=[VMEM_SPEC],
        out_specs=(VMEM_SPEC, VMEM_SPEC),
    )(pieces)
    weight_grad = lax.all_gather(weight_piece, "near", axis=0, tiled=True)
    weight_grad = weight_grad.reshape(width // PIECE, full // extent, PIECE, extent)
    weight_grad = weight_grad.transpose(0, 2, 1, 3).reshape(width, full)
    return (activated, weight_grad, feature_grad.T)


def solution(mesh):
    rows, cols, feats = (mesh.shape[name] for name in ("row", "col", "feat"))
    fine = jax.sharding.Mesh(
        mesh.devices.reshape(rows, cols // CORES, CORES, feats), ("row", "near", "core", "feat")
    )
    pair = P(("row", "near", "core"))
    owner = P(("row", "near", "core", "feat"), None)
    by_column = P(("near", "core", "row"), "feat")
    return jax.shard_map(
        local,
        mesh=fine,
        in_specs=(by_column, P("feat", None), owner, pair, pair, pair, pair),
        out_specs=(owner, P("feat", None), by_column),
        check_vma=False,
    )
```

time: 197 us -> 185 us (0.939)
  the two profiles are of different devices: /device:TPU:1 before, /device:TPU:2 now
where the time goes in v3:
time: 185 us; the launch traced here: 184 us
  blocking collectives  127 us (69%)
  starting transfers between devices  23.6 us (13%)
  Pallas kernels  13.3 us (7%)
  local copies, waits for them, and re-layouts  10.8 us (6%)
  waiting for transfers between devices  8.38 us (5%)
    all_to_all x1, blocking collectives, local(): pieces = lax.all_to_all(pieces, 'row', 0, 0, tiled=False)  44.6 us
    all_gather x1, blocking collectives, local(): weight_all = lax.all_gather(weight, 'feat', axis=0, tiled=True)  26.7 us
    all_to_all x1, blocking collectives, local(): lax.all_to_all(terms.reshape(owners, width, extent), ('near', 'feat'), 0,...  23.2 us
    all_to_all x1, starting transfers between devices, local(): lax.all_to_all(jnp.broadcast_to(own[None], (rows,) + own.shape), 'row', 0...  19.7 us
    all_to_all x1, blocking collectives, local(): mine = lax.all_to_all(outgoing, ('near', 'feat'), 0, 0, tiled=False)  19 us
    all_gather x1, blocking collectives, local(): weight_grad = lax.all_gather(weight_piece, 'near', axis=0, tiled=True)  13.3 us
    unnamed x13, local copies, waits for them, and re-layouts  8.85 us
    pallas_call x2, Pallas kernels, tile_call(): pl.pallas_call(kernel, out_shape=out_shapes, in_specs=[SMEM_SPEC] * len(s...  6.1 us
  transfers between devices with their start and end apart: 3, of which 3 were waited for; matrix products, arithmetic and copies ran while one was open for 0% of the time, Pallas kernels for 2%

profile of v3, /device:TPU:2, one launch (start us, length us, event | category | flops | bytes accessed | tf_op | source)
XLA Modules:
  0.0 184.4 jit_solution(9757420966768050207)
XLA Ops:
  0.6 1.9 %broadcast_in_dim.2 = bf16[16,32,1024]{2,1,0:T(8,128)(2,1)} broadcast(bf16[32,1024]{1,0:T(8,128)(2,1)} %bitcast.17), dimensions={1,2} | broadcast | bytes 1114112 | tf_op jit(solution)/shard_map/broadcast_in_dim | solution.py:170
  2.6 19.7 %all-to-all-start = ((bf16[16,32,1024]{2,1,0:T(8,128)(2,1)}), bf16[16,32,1024]{2,1,0:T(8,128)(2,1)S(1)}, u32[]{:S(2)}, u32[]{:S(2)}) async-start(bf16[16,32,1024]{2,1,0:T(8,128)(2,1)} %broadcast_in_dim.2), calls=%async_computation | async-start | bytes 2097152 | tf_op jit(solution)/shard_map/all_to_all | solution.py:169
  23.0 0.0 copy-start.5
  23.0 0.0 copy-start.3
  23.0 0.0 copy-start.4
  23.0 2.8 %shard_map.94.adj_ref = bf16[192,128,128]{2,1,0:T(8,128)(2,1)S(1)} custom-call(bf16[192,128,128]{2,1,0:T(8,128)(2,1)} %source_ref.1), custom_call_target="tpu_custom_call" | custom-call | bytes 12582912 | tf_op jit(solution)/shard_map/pallas_call | solution.py:131
  25.8 0.0 copy-start
  25.8 2.6 %copy-done = bf16[192,128,128]{2,1,0:T(8,128)(2,1)} copy-done((bf16[192,128,128]{2,1,0:T(8,128)(2,1)}, bf16[192,128,128]{2,1,0:T(8,128)(2,1)S(1)}, u32[]{:S(2)}) %copy-start) | copy-done | bytes 6291480
  28.5 0.0 copy-done.5
  28.5 26.7 %all_gather.6.weight_ref = bf16[256,256]{1,0:T(8,128)(2,1)} all-gather(bf16[32,256]{1,0:T(8,128)(2,1)S(1)} %copy-done.5), channel_id=1, replica_groups=mesh['row'=16,'near'=4,'core'=2,'feat'=8] {'feat'}, dimensions={0}, use_global_device_ids=true | all-gather | bytes 147456 | tf_op jit(solution)/shard_map/all_gather | solution.py:166
  55.2 4.8 %all-to-all-done.feat_ref = bf16[16,32,1024]{2,1,0:T(8,128)(2,1)S(1)} async-done(((bf16[16,32,1024]{2,1,0:T(8,128)(2,1)}), bf16[16,32,1024]{2,1,0:T(8,128)(2,1)S(1)}, u32[]{:S(2)}, u32[]{:S(2)}) %all-to-all-start) | async-done | bytes 1048608 | tf_op jit(solution)/shard_map/all_to_all | solution.py:169
  60.0 0.0 copy-done.3
  60.0 0.0 copy-done.4
  60.0 0.0 copy-start.1
  60.0 2.8 %copy-done.1 = bf16[192,128,128]{2,1,0:T(8,128)(2,1)S(1)} copy-done((bf16[192,128,128]{2,1,0:T(8,128)(2,1)S(1)}, bf16[192,128,128]{2,1,0:T(8,128)(2,1)}, u32[]{:S(2)}) %copy-start.1) | copy-done | bytes 6291480
  62.8 3.1 %shard_map.95 = (f32[4,8,32,128]{3,2,1,0:T(8,128)S(1)}, f32[4,8,32,128]{3,2,1,0:T(8,128)S(1)}) custom-call(s32[1]{0:T(128)} %bitcast.core, s32[192]{0:T(256)S(1)} %copy-done.3, s32[192]{0:T(256)S(1)} %copy-done.4, s32[1]{0:T(128)S(6)} %copy.14.count, bf16[192,128,128]{2,1,0:T(8,128)(2,1)S(1)} %copy-done.1, bf16[16,32,1024]{2,1,0:T(8,128)(2,1)S(1)} %all-to-all-done.feat_ref), custom_call_target="tpu_custom_call" | custom-call | tf_op jit(solution)/shard_map/pallas_call | solution.py:145
  66.0 1.9 %collective-permute-start = (f32[4,8,32,128]{3,2,1,0:T(8,128)S(1)}, f32[4,8,32,128]{3,2,1,0:T(8,128)S(1)}, u32[]{:S(2)}, u32[]{:S(2)}) collective-permute-start(f32[4,8,32,128]{3,2,1,0:T(8,128)S(1)} %get-tuple-element.15), channel_id=1, source_target_pairs={{0,8},{8,0},{1,9},{9,1},{2,10},{10,2},{3,11},{11,3},{4,12},{12,4},... | collective-permute-start | bytes 1572872 | tf_op jit(solution)/shard_map/ppermute | solution.py:183
  67.9 1.9 %collective-permute-done = f32[4,8,32,128]{3,2,1,0:T(8,128)S(1)} collective-permute-done((f32[4,8,32,128]{3,2,1,0:T(8,128)S(1)}, f32[4,8,32,128]{3,2,1,0:T(8,128)S(1)}, u32[]{:S(2)}, u32[]{:S(2)}) %collective-permute-start) | collective-permute-done | bytes 524320 | tf_op jit(solution)/shard_map/ppermute | solution.py:183
  69.8 0.1 add_convert_fusion
  69.9 23.2 %all_to_all.20 = bf16[32,32,128]{2,1,0:T(8,128)(2,1)} all-to-all(bf16[32,32,128]{2,1,0:T(8,128)(2,1)S(1)} %bitcast.13), channel_id=1, replica_groups=mesh['row'=16,'near'=4,'core'=2,'feat'=8] {'near','feat'}, dimensions={0} | all-to-all | bytes 524288 | tf_op jit(solution)/shard_map/all_to_all | solution.py:184
  93.1 2.3 %shard_map.96 = (bf16[32,48,128]{2,1,0:T(8,128)(2,1)}, bf16[128,256]{1,0:T(8,128)(2,1)}) custom-call(bf16[4,8,32,128]{3,2,1,0:T(8,128)(2,1)} %bitcast.14, bf16[256,256]{1,0:T(8,128)(2,1)} %all_gather.6.weight_ref, bf16[128,256]{1,0:T(8,128)(2,1)} %grad_ref.1), custom_call_target="tpu_custom_call" | custom-call | tf_op jit(solution)/shard_map/pallas_call | solution.py:187
  95.4 19.0 %all_to_all.21.mine_ref = bf16[32,48,128]{2,1,0:T(8,128)(2,1)S(1)} all-to-all(bf16[32,48,128]{2,1,0:T(8,128)(2,1)} %get-tuple-element.18), channel_id=1, replica_groups=mesh['row'=16,'near'=4,'core'=2,'feat'=8] {'near','feat'}, dimensions={0} | all-to-all | bytes 786432 | tf_op jit(solution)/shard_map/all_to_all | solution.py:197
  114.4 1.9 %collective-permute-start.1 = (bf16[32,48,128]{2,1,0:T(8,128)(2,1)S(1)}, bf16[32,48,128]{2,1,0:T(8,128)(2,1)S(1)}, u32[]{:S(2)}, u32[]{:S(2)}) collective-permute-start(bf16[32,48,128]{2,1,0:T(8,128)(2,1)S(1)} %all_to_all.21.mine_ref), channel_id=1, source_target_pairs={{0,8},{8,0},{1,9},{9,1},{2,10},{10,2},{3,11},{11,3},{4,12},{12,4},... | collective-permute-start | bytes 1179656 | tf_op jit(solution)/shard_map/ppermute | solution.py:198
  116.4 1.7 collective-permute-done.1.other_ref
  118.1 0.0 copy-start.2
  118.1 2.8 %copy-done.2 = bf16[192,128,128]{2,1,0:T(8,128)(2,1)S(1)} copy-done((bf16[192,128,128]{2,1,0:T(8,128)(2,1)S(1)}, bf16[192,128,128]{2,1,0:T(8,128)(2,1)}, u32[]{:S(2)}) %copy-start.2) | copy-done | bytes 6291480
  120.8 3.0 %shard_map.97 = bf16[16,272,128]{2,1,0:T(8,128)(2,1)S(1)} custom-call(s32[1]{0:T(128)} %bitcast.core, s32[192]{0:T(256)S(1)} %copy-done.3, s32[192]{0:T(256)S(1)} %copy-done.4, s32[1]{0:T(128)S(6)} %copy.14.count, bf16[192,128,128]{2,1,0:T(8,128)(2,1)S(1)} %copy-done.2, bf16[32,48,128]{2,1,0:T(8,128)(2,1)S(1)} %all_to_all.21.mine_ref, ...), custom_call_target="tpu_custom_call" | custom-call | tf_op jit(solution)/shard_map/pallas_call | solution.py:145
  123.8 44.6 %all_to_all.22.refs_0_ = bf16[16,272,128]{2,1,0:T(8,128)(2,1)} all-to-all(bf16[16,272,128]{2,1,0:T(8,128)(2,1)S(1)} %shard_map.97), channel_id=1, replica_groups=mesh['row'=16,'near'=4,'core'=2,'feat'=8] {'row'}, dimensions={0} | all-to-all | bytes 2228224 | tf_op jit(solution)/shard_map/all_to_all | solution.py:210
  168.4 2.0 %shard_map.98 = (f32[32,1024]{1,0:T(8,128)}, f32[16,128]{1,0:T(8,128)}) custom-call(bf16[16,272,128]{2,1,0:T(8,128)(2,1)} %all_to_all.22.refs_0_), custom_call_target="tpu_custom_call" | custom-call | tf_op jit(solution)/shard_map/pallas_call | solution.py:212
  170.4 13.3 %all_gather.7 = f32[64,128]{1,0:T(8,128)S(1)} all-gather(f32[16,128]{1,0:T(8,128)} %get-tuple-element.19), channel_id=1, replica_groups=mesh['row'=16,'near'=4,'core'=2,'feat'=8] {'near'}, dimensions={0}, use_global_device_ids=true | all-gather | bytes 40960 | tf_op jit(solution)/shard_map/all_gather | solution.py:221
  183.8 0.6 copy.13
  (1 shorter events, 0.0 us)
Async XLA Ops:
  2.6 57.5 %all-to-all-start = ((bf16[16,32,1024]{2,1,0:T(8,128)(2,1)}), bf16[16,32,1024]{2,1,0:T(8,128)(2,1)S(1)}, u32[]{:S(2)}, u32[]{:S(2)}) async-start(bf16[16,32,1024]{2,1,0:T(8,128)(2,1)} %broadcast_in_dim.2), calls=%async_computation | async-start | bytes 2097152 | tf_op jit(solution)/shard_map/all_to_all | solution.py:169
  23.0 5.5 %copy-start.5 = (bf16[32,256]{1,0:T(8,128)(2,1)S(1)}, bf16[32,256]{1,0:T(8,128)(2,1)}, u32[]{:S(2)}) copy-start(bf16[32,256]{1,0:T(8,128)(2,1)} %param.8) | copy-start | bytes 49156
  23.0 37.0 %copy-start.3 = (s32[192]{0:T(256)S(1)}, s32[192]{0:T(256)}, u32[]{:S(2)}) copy-start(s32[192]{0:T(256)} %rows.3) | copy-start | bytes 2308
  23.0 37.0 %copy-start.4 = (s32[192]{0:T(256)S(1)}, s32[192]{0:T(256)}, u32[]{:S(2)}) copy-start(s32[192]{0:T(256)} %cols.3) | copy-start | bytes 2308
  25.8 2.7 %copy-start = (bf16[192,128,128]{2,1,0:T(8,128)(2,1)}, bf16[192,128,128]{2,1,0:T(8,128)(2,1)S(1)}, u32[]{:S(2)}) copy-start(bf16[192,128,128]{2,1,0:T(8,128)(2,1)S(1)} %shard_map.94.adj_ref) | copy-start | bytes 18874372
  60.0 2.8 %copy-start.1 = (bf16[192,128,128]{2,1,0:T(8,128)(2,1)S(1)}, bf16[192,128,128]{2,1,0:T(8,128)(2,1)}, u32[]{:S(2)}) copy-start(bf16[192,128,128]{2,1,0:T(8,128)(2,1)} %copy-done) | copy-start | bytes 18874372
  66.0 3.8 %collective-permute-start = (f32[4,8,32,128]{3,2,1,0:T(8,128)S(1)}, f32[4,8,32,128]{3,2,1,0:T(8,128)S(1)}, u32[]{:S(2)}, u32[]{:S(2)}) collective-permute-start(f32[4,8,32,128]{3,2,1,0:T(8,128)S(1)} %get-tuple-element.15), channel_id=1, source_target_pairs={{0,8},{8,0},{1,9},{9,1},{2,10},{10,2},{3,11},{11,3},{4,12},{12,4},... | collective-permute-start | bytes 1572872 | tf_op jit(solution)/shard_map/ppermute | solution.py:183
  114.4 3.6 %collective-permute-start.1 = (bf16[32,48,128]{2,1,0:T(8,128)(2,1)S(1)}, bf16[32,48,128]{2,1,0:T(8,128)(2,1)S(1)}, u32[]{:S(2)}, u32[]{:S(2)}) collective-permute-start(bf16[32,48,128]{2,1,0:T(8,128)(2,1)S(1)} %all_to_all.21.mine_ref), channel_id=1, source_target_pairs={{0,8},{8,0},{1,9},{9,1},{2,10},{10,2},{3,11},{11,3},{4,12},{12,4},... | collective-permute-start | bytes 1179656 | tf_op jit(solution)/shard_map/ppermute | solution.py:198
  118.1 2.8 %copy-start.2 = (bf16[192,128,128]{2,1,0:T(8,128)(2,1)S(1)}, bf16[192,128,128]{2,1,0:T(8,128)(2,1)}, u32[]{:S(2)}) copy-start(bf16[192,128,128]{2,1,0:T(8,128)(2,1)} %copy-done) | copy-start | bytes 18874372

commit v4 on v3

--- a/solution.py
+++ b/solution.py
@@ -60,21 +60,43 @@
         send_ref[pair] = acc_ref[pl.ds((pair * CORES + 1 - core[0]) * feats, feats)]
 
 
-def dense_kernel(terms_ref, weight_ref, grad_ref, out_ref, act_ref):
-    near, feats, width, extent = terms_ref.shape
+def spread_kernel(value_ref, out_ref):
+    for copy in range(out_ref.shape[0]):
+        out_ref[copy] = value_ref[...]
+
+
+def combine_kernel(near, keep_ref, received_ref, weight_ref, out_ref):
+    owners, width, extent = keep_ref.shape
+    halves = weight_ref.shape[1] // extent
+    out_ref[:, :width] = (keep_ref[...] + received_ref[...]).astype(out_ref.dtype)
+    top = pl.multiple_of((near[0] // halves) * PIECE, PIECE)
+    left = pl.multiple_of((near[0] % halves) * extent, extent)
+    piece = weight_ref[pl.ds(top, PIECE), pl.ds(left, extent)]
+    for owner in range(owners):
+        out_ref[owner, width:] = piece
+
+
+def dense_kernel(terms_ref, grad_ref, out_ref, act_ref, weight_ref):
+    near, feats, height, extent = terms_ref.shape
+    width = height - PIECE
     full = feats * width
+    halves = full // extent
+    for pair in range(near):
+        for feat in range(feats):
+            top = feat * width + (pair // halves) * PIECE
+            left = (pair % halves) * extent
+            weight_ref[top : top + PIECE, left : left + extent] = terms_ref[pair, feat, width:]
     weight = weight_ref[...]
-    summed = jnp.sum(terms_ref[...].astype(jnp.float32), axis=0).reshape(full, extent)
+    summed = jnp.sum(terms_ref[:, :, :width].astype(jnp.float32), axis=0).reshape(full, extent)
     high = summed.astype(jnp.bfloat16)
     low = (summed - high.astype(jnp.float32)).astype(jnp.bfloat16)
     pre_act = dot(high, weight, TN) + dot(low, weight, TN)
     gate = jax.nn.sigmoid(pre_act)
     act_ref[...] = (pre_act * gate).astype(act_ref.dtype)
     derivative = gate * (1.0 + pre_act * (1.0 - gate))
-    grad_pre = (grad_ref[...].astype(jnp.float32) * derivative).astype(jnp.bfloat16)
+    grad_pre = (grad_ref[...] * derivative).astype(jnp.bfloat16)
     projected = dot(weight, grad_pre, NT).astype(out_ref.dtype)
     weight_term = (dot(high, grad_pre, NN) + dot(low, grad_pre, NN)).astype(out_ref.dtype)
-    halves = full // extent
     for pair in range(near):
         for feat in range(feats):
             top = feat * width + (pair // halves) * PIECE
@@ -120,7 +142,9 @@
             pieces_ref[:, block * width : (block + 1) * width].astype(jnp.float32), axis=0
         )
     rest = pieces_ref[:, nodes // extent * width :].astype(jnp.float32)
-    weight_ref[...] = jnp.sum(rest, axis=0) * scale
+    weight_term = jnp.sum(rest, axis=0) * scale
+    for pair in range(weight_ref.shape[0]):
+        weight_ref[pair] = weight_term
 
 
 SMEM_SPEC = pl.BlockSpec(memory_space=pltpu.SMEM)
@@ -141,15 +165,19 @@
     )(pltpu.with_memory_space_constraint(array, pltpu.HBM))
 
 
-def tile_call(kernel, scalars, adjacency, sources, out_shapes, scratch):
+def in_vmem(array):
+    return pltpu.with_memory_space_constraint(array, pltpu.VMEM)
+
+
+def call(kernel, scalars, arrays, out_shapes, scratch=()):
     return pl.pallas_call(
         kernel,
         out_shape=out_shapes,
-        in_specs=[SMEM_SPEC] * len(scalars) + [VMEM_SPEC] * (1 + len(sources)),
+        in_specs=[SMEM_SPEC] * len(scalars) + [VMEM_SPEC] * len(arrays),
         out_specs=jax.tree.map(lambda _: VMEM_SPEC, out_shapes),
         scratch_shapes=scratch,
         compiler_params=pltpu.CompilerParams(vmem_limit_bytes=VMEM_LIMIT),
-    )(*scalars, pltpu.with_memory_space_constraint(adjacency, pltpu.VMEM), *sources)
+    )(*scalars, *(in_vmem(array) for array in arrays))
 
 
 def local(features, weight, grad_out, adjacency, tile_rows, tile_cols, tile_count):
@@ -160,65 +188,73 @@
     blocks = nodes // extent
     owners = near * feats
     swap = [(i, CORES - 1 - i) for i in range(CORES)]
-    core = lax.axis_index("core").astype(jnp.int32).reshape(1)
+    core, near_index = (
+        lax.axis_index(name).astype(jnp.int32).reshape(1) for name in ("core", "near")
+    )
     scalars = (core, tile_rows, tile_cols, tile_count)
-
-    weight_all = lax.all_gather(weight, "feat", axis=0, tiled=True)
-    adjacency = stage(adjacency)
-    own = features.T
-    gathered = lax.all_to_all(
-        jnp.broadcast_to(own[None], (rows,) + own.shape), "row", 0, 0, tiled=False
-    )
-    gathered, weight_all, adjacency = lax.optimization_barrier((gathered, weight_all, adjacency))
-
-    half = jax.ShapeDtypeStruct((near, feats, width, extent), jnp.float32)
-    keep, send = tile_call(
+    bf16, f32 = jnp.bfloat16, jnp.float32
+
+    own = call(spread_kernel, (), (features.T,), pltpu.VMEM((rows, width, nodes), bf16))
+    gathered = lax.all_to_all(own, "row", 0, 0, tiled=False)
+    tiles = stage(adjacency)
+
+    half = jax.ShapeDtypeStruct((near, feats, width, extent), f32)
+    keep, send = call(
         forward_kernel,
         scalars,
-        adjacency,
-        (gathered,),
+        (tiles, gathered),
         (half, half),
-        [pltpu.VMEM((CORES * owners, width, extent), jnp.float32)],
-    )
-    terms = (keep + lax.ppermute(send, "core", swap)).astype(jnp.bfloat16)
-    terms = lax.all_to_all(
-        terms.reshape(owners, width, extent), ("near", "feat"), 0, 0, tiled=False
-    )
-    outgoing, activated = pl.pallas_call(
+        [pltpu.VMEM((CORES * owners, width, extent), f32)],
+    )
+    received = lax.ppermute(send, "core", swap)
+    flat = (owners, width, extent)
+    terms = call(
+        combine_kernel,
+        (near_index,),
+        (keep.reshape(flat), received.reshape(flat), weight),
+        pltpu.VMEM((owners, width + PIECE, extent), bf16),
+    )
+    terms, grad_out = lax.optimization_barrier((terms, grad_out))
+    terms = lax.all_to_all(terms, ("near", "feat"), 0, 0, tiled=False)
+    outgoing, activated = call(
         dense_kernel,
-        out_shape=(
-            jax.ShapeDtypeStruct((owners, width + PIECE, extent), jnp.bfloat16),
-            jax.ShapeDtypeStruct((extent, full), jnp.bfloat16),
+        (),
+        (terms.reshape(near, feats, width + PIECE, extent), grad_out.astype(f32)),
+        (
+            pltpu.VMEM((owners, width + PIECE, extent), bf16),
+            jax.ShapeDtypeStruct((extent, full), f32),
         ),
-        in_specs=[VMEM_SPEC] * 3,
-        out_specs=(VMEM_SPEC, VMEM_SPEC),
-    )(terms.reshape(near, feats, width, extent), weight_all, grad_out)
-
+        [pltpu.VMEM((full, full), bf16)],
+    )
+
+    outgoing, adjacency = lax.optimization_barrier((outgoing, adjacency))
     mine = lax.all_to_all(outgoing, ("near", "feat"), 0, 0, tiled=False)
+    tiles = stage(adjacency)
     other = lax.ppermute(mine, "core", swap)
-    pieces = tile_call(
+    pieces = call(
         backward_kernel,
         scalars,
-        adjacency,
-        (mine, other),
-        jax.ShapeDtypeStruct((rows, blocks * width + PIECE, extent), jnp.bfloat16),
+        (tiles, mine, other),
+        pltpu.VMEM((rows, blocks * width + PIECE, extent), bf16),
         [
-            pltpu.VMEM((near, CORES, feats, width, extent), jnp.bfloat16),
-            pltpu.VMEM((rows * blocks, width, extent), jnp.float32),
+            pltpu.VMEM((near, CORES, feats, width, extent), bf16),
+            pltpu.VMEM((rows * blocks, width, extent), f32),
         ],
     )
+    pieces, activated = lax.optimization_barrier((pieces, activated))
     pieces = lax.all_to_all(pieces, "row", 0, 0, tiled=False)
+    activated = activated.astype(bf16)
     scale = 1.0 / math.sqrt(nodes * rows * near * CORES)
-    feature_grad, weight_piece = pl.pallas_call(
+    feature_grad, weight_piece = call(
         lambda *refs: final_kernel(scale, *refs),
-        out_shape=(
-            jax.ShapeDtypeStruct((width, nodes), jnp.float32),
-            jax.ShapeDtypeStruct((PIECE, extent), jnp.float32),
+        (),
+        (pieces,),
+        (
+            jax.ShapeDtypeStruct((width, nodes), f32),
+            pltpu.VMEM((near, PIECE, extent), f32),
         ),
-        in_specs=[VMEM_SPEC],
-        out_specs=(VMEM_SPEC, VMEM_SPEC),
-    )(pieces)
-    weight_grad = lax.all_gather(weight_piece, "near", axis=0, tiled=True)
+    )
+    weight_grad = lax.all_to_all(weight_piece, "near", 0, 0, tiled=False)
     weight_grad = weight_grad.reshape(width // PIECE, full // extent, PIECE, extent)
     weight_grad = weight_grad.transpose(0, 2, 1, 3).reshape(width, full)
     return (activated, weight_grad, feature_grad.T)

time: 185 us -> 180 us (0.973)
  the two profiles are of different devices: /device:TPU:2 before, /device:TPU:1 now
where the time goes in v4:
time: 180 us; the launch traced here: 178 us
  blocking collectives  61 us (34%)
  waiting for transfers between devices  45.4 us (25%)
  starting transfers between devices  43.2 us (24%)
  Pallas kernels  19 us (11%)
  local copies, waits for them, and re-layouts  6.93 us (4%)
    all_to_all x1, blocking collectives, local(): pieces = lax.all_to_all(pieces, 'row', 0, 0, tiled=False)  42 us
    all_to_all x1, waiting for transfers between devices, local(): gathered = lax.all_to_all(own, 'row', 0, 0, tiled=False)  27.7 us
    all_to_all x1, starting transfers between devices, local(): gathered = lax.all_to_all(own, 'row', 0, 0, tiled=False)  20.3 us
    all_to_all x1, blocking collectives, local(): mine = lax.all_to_all(outgoing, ('near', 'feat'), 0, 0, tiled=False)  19 us
    pallas_call x6, Pallas kernels, call(): pl.pallas_call(kernel, out_shape=out_shapes, in_specs=[SMEM_SPEC] * len(s...  13.4 us
    all_to_all x1, waiting for transfers between devices, local(): terms = lax.all_to_all(terms, ('near', 'feat'), 0, 0, tiled=False)  12.3 us
    all_to_all x1, starting transfers between devices, local(): terms = lax.all_to_all(terms, ('near', 'feat'), 0, 0, tiled=False)  10.7 us
    unnamed x15, local copies, waits for them, and re-layouts  6.92 us
  transfers between devices with their start and end apart: 5, of which 4 were waited for; matrix products, arithmetic and copies ran while one was open for 0% of the time, Pallas kernels for 3%

profile of v4, /device:TPU:1, one launch (start us, length us, event | category | flops | bytes accessed | tf_op | source)
XLA Modules:
  0.0 177.6 jit_solution(15953031185111525652)
XLA Ops:
  0.6 0.0 copy-start.2
  0.6 0.8 copy-done.2
  1.5 1.1 shard_map.95
  2.5 20.3 %all-to-all-start = ((bf16[16,32,1024]{2,1,0:T(8,128)(2,1)}), bf16[16,32,1024]{2,1,0:T(8,128)(2,1)S(1)}, u32[]{:S(2)}, u32[]{:S(2)}) async-start(bf16[16,32,1024]{2,1,0:T(8,128)(2,1)} %shard_map.95), calls=%async_computation | async-start | bytes 2097152 | tf_op jit(solution)/shard_map/all_to_all | solution.py:198
  23.5 0.0 copy-start.4
  23.5 0.0 copy-start.5
  23.5 0.0 copy-start.3
  23.5 0.0 copy-start.6
  23.5 2.8 %shard_map.94.adj_ref = bf16[192,128,128]{2,1,0:T(8,128)(2,1)S(1)} custom-call(bf16[192,128,128]{2,1,0:T(8,128)(2,1)} %source_ref.2), custom_call_target="tpu_custom_call" | custom-call | bytes 12582912 | tf_op jit(solution)/shard_map/pallas_call | solution.py:155
  26.4 0.0 copy-start
  26.4 2.7 %copy-done = bf16[192,128,128]{2,1,0:T(8,128)(2,1)} copy-done((bf16[192,128,128]{2,1,0:T(8,128)(2,1)}, bf16[192,128,128]{2,1,0:T(8,128)(2,1)S(1)}, u32[]{:S(2)}) %copy-start) | copy-done | bytes 6291480
  29.0 27.7 %all-to-all-done.feat_ref = bf16[16,32,1024]{2,1,0:T(8,128)(2,1)S(1)} async-done(((bf16[16,32,1024]{2,1,0:T(8,128)(2,1)}), bf16[16,32,1024]{2,1,0:T(8,128)(2,1)S(1)}, u32[]{:S(2)}, u32[]{:S(2)}) %all-to-all-start) | async-done | bytes 1048608 | tf_op jit(solution)/shard_map/all_to_all | solution.py:198
  56.8 0.0 copy-done.4
  56.8 0.0 copy-done.5
  56.8 0.0 copy-start.1
  56.8 2.8 %copy-done.1 = bf16[192,128,128]{2,1,0:T(8,128)(2,1)S(1)} copy-done((bf16[192,128,128]{2,1,0:T(8,128)(2,1)S(1)}, bf16[192,128,128]{2,1,0:T(8,128)(2,1)}, u32[]{:S(2)}) %copy-start.1) | copy-done | bytes 6291480
  59.6 5.3 %shard_map.96 = (f32[4,8,32,128]{3,2,1,0:T(8,128)S(1)}, f32[4,8,32,128]{3,2,1,0:T(8,128)S(1)}) custom-call(s32[1]{0:T(128)} %bitcast.core, s32[192]{0:T(256)S(1)} %copy-done.4, s32[192]{0:T(256)S(1)} %copy-done.5, s32[1]{0:T(128)S(6)} %copy.14.count, bf16[192,128,128]{2,1,0:T(8,128)(2,1)S(1)} %copy-done.1, bf16[16,32,1024]{2,1,0:T(8,128)(2,1)S(1)} %all-to-all-done.feat_ref), custom_call_target="tpu_custom_call" | custom-call | tf_op jit(solution)/shard_map/pallas_call | solution.py:173
  64.9 4.0 %collective-permute-start = (f32[4,8,32,128]{3,2,1,0:T(8,128)S(1)}, f32[4,8,32,128]{3,2,1,0:T(8,128)S(1)}, u32[]{:S(2)}, u32[]{:S(2)}) collective-permute-start(f32[4,8,32,128]{3,2,1,0:T(8,128)S(1)} %get-tuple-element.16), channel_id=1, source_target_pairs={{0,8},{8,0},{1,9},{9,1},{2,10},{10,2},{3,11},{11,3},{4,12},{12,4},... | collective-permute-start | bytes 1572872 | tf_op jit(solution)/shard_map/ppermute | solution.py:209
  68.9 1.5 collective-permute-done
  70.4 0.0 copy-done.3
  70.4 0.8 shard_map.97
  71.2 10.7 %all-to-all-start.1 = ((bf16[32,48,128]{2,1,0:T(8,128)(2,1)}), bf16[32,48,128]{2,1,0:T(8,128)(2,1)S(1)}, u32[]{:S(2)}, u32[]{:S(2)}) async-start(bf16[32,48,128]{2,1,0:T(8,128)(2,1)} %shard_map.97), calls=%async_computation.1 | async-start | bytes 786432 | tf_op jit(solution)/shard_map/all_to_all | solution.py:218
  81.9 0.0 copy-done.6
  81.9 12.3 %all-to-all-done.1 = bf16[32,48,128]{2,1,0:T(8,128)(2,1)S(1)} async-done(((bf16[32,48,128]{2,1,0:T(8,128)(2,1)}), bf16[32,48,128]{2,1,0:T(8,128)(2,1)S(1)}, u32[]{:S(2)}, u32[]{:S(2)}) %all-to-all-start.1) | async-done | bytes 393248 | tf_op jit(solution)/shard_map/all_to_all | solution.py:218
  94.2 0.6 shard_map.98
  94.8 19.0 %all_to_all.25.mine_ref = bf16[32,48,128]{2,1,0:T(8,128)(2,1)S(1)} all-to-all(bf16[32,48,128]{2,1,0:T(8,128)(2,1)S(1)} %get-tuple-element.21), channel_id=1, replica_groups=mesh['row'=16,'near'=4,'core'=2,'feat'=8] {'near','feat'}, dimensions={0} | all-to-all | bytes 786432 | tf_op jit(solution)/shard_map/all_to_all | solution.py:231
  113.8 5.0 %collective-permute-start.1 = (bf16[32,48,128]{2,1,0:T(8,128)(2,1)S(1)}, bf16[32,48,128]{2,1,0:T(8,128)(2,1)S(1)}, u32[]{:S(2)}, u32[]{:S(2)}) collective-permute-start(bf16[32,48,128]{2,1,0:T(8,128)(2,1)S(1)} %all_to_all.25.mine_ref), channel_id=1, source_target_pairs={{0,8},{8,0},{1,9},{9,1},{2,10},{10,2},{3,11},{11,3},{4,12},{12,4},... | collective-permute-start | bytes 1179656 | tf_op jit(solution)/shard_map/ppermute | solution.py:233
  118.8 2.8 %shard_map.99.adj_ref = bf16[192,128,128]{2,1,0:T(8,128)(2,1)S(1)} custom-call(bf16[192,128,128]{2,1,0:T(8,128)(2,1)} %source_ref.2), custom_call_target="tpu_custom_call" | custom-call | bytes 12582912 | tf_op jit(solution)/shard_map/pallas_call | solution.py:155
  121.6 0.0 collective-permute-done.1.other_ref
  121.6 4.8 %shard_map.100 = bf16[16,272,128]{2,1,0:T(8,128)(2,1)S(1)} custom-call(s32[1]{0:T(128)} %bitcast.core, s32[192]{0:T(256)S(1)} %copy-done.4, s32[192]{0:T(256)S(1)} %copy-done.5, s32[1]{0:T(128)S(6)} %copy.14.count, bf16[192,128,128]{2,1,0:T(8,128)(2,1)S(1)} %shard_map.99.adj_ref, bf16[32,48,128]{2,1,0:T(8,128)(2,1)S(1)} %all_to_all.25.mine_ref, ...), custom_call_target="tpu_custom_call" | custom-call | tf_op jit(solution)/shard_map/pallas_call | solution.py:173
  126.4 42.0 %all_to_all.26.refs_0_ = bf16[16,272,128]{2,1,0:T(8,128)(2,1)S(1)} all-to-all(bf16[16,272,128]{2,1,0:T(8,128)(2,1)S(1)} %shard_map.100), channel_id=1, replica_groups=mesh['row'=16,'near'=4,'core'=2,'feat'=8] {'row'}, dimensions={0} | all-to-all | bytes 2228224 | tf_op jit(solution)/shard_map/all_to_all | solution.py:245
  168.4 0.8 shard_map.101
  169.2 3.3 %all-to-all-start.4 = ((f32[4,16,128]{2,1,0:T(8,128)}), f32[4,16,128]{2,1,0:T(8,128)S(1)}, u32[]{:S(2)}, u32[]{:S(2)}) async-start(f32[4,16,128]{2,1,0:T(8,128)} %get-tuple-element.25), calls=%async_computation.4 | async-start | bytes 65536 | tf_op jit(solution)/shard_map/all_to_all | solution.py:257
  172.5 0.6 convert_element_type.7
  173.1 3.8 %all-to-all-done.4 = f32[4,16,128]{2,1,0:T(8,128)S(1)} async-done(((f32[4,16,128]{2,1,0:T(8,128)}), f32[4,16,128]{2,1,0:T(8,128)S(1)}, u32[]{:S(2)}, u32[]{:S(2)}) %all-to-all-start.4) | async-done | bytes 32800 | tf_op jit(solution)/shard_map/all_to_all | solution.py:257
  177.0 0.6 copy.13
  (2 shorter events, 0.0 us)
Async XLA Ops:
  0.6 0.8 copy-start.2
  2.5 54.2 %all-to-all-start = ((bf16[16,32,1024]{2,1,0:T(8,128)(2,1)}), bf16[16,32,1024]{2,1,0:T(8,128)(2,1)S(1)}, u32[]{:S(2)}, u32[]{:S(2)}) async-start(bf16[16,32,1024]{2,1,0:T(8,128)(2,1)} %shard_map.95), calls=%async_computation | async-start | bytes 2097152 | tf_op jit(solution)/shard_map/all_to_all | solution.py:198
  23.5 33.3 %copy-start.4 = (s32[192]{0:T(256)S(1)}, s32[192]{0:T(256)}, u32[]{:S(2)}) copy-start(s32[192]{0:T(256)} %rows.3) | copy-start | bytes 2308
  23.5 33.3 %copy-start.5 = (s32[192]{0:T(256)S(1)}, s32[192]{0:T(256)}, u32[]{:S(2)}) copy-start(s32[192]{0:T(256)} %cols.3) | copy-start | bytes 2308
  23.5 46.9 %copy-start.3 = (bf16[32,256]{1,0:T(8,128)(2,1)S(1)}, bf16[32,256]{1,0:T(8,128)(2,1)}, u32[]{:S(2)}) copy-start(bf16[32,256]{1,0:T(8,128)(2,1)} %weight_ref.1) | copy-start | bytes 49156
  23.5 58.4 %copy-start.6 = (bf16[128,256]{1,0:T(8,128)(2,1)S(1)}, bf16[128,256]{1,0:T(8,128)(2,1)}, u32[]{:S(2)}) copy-start(bf16[128,256]{1,0:T(8,128)(2,1)} %param.9) | copy-start | bytes 196612
  26.4 2.7 %copy-start = (bf16[192,128,128]{2,1,0:T(8,128)(2,1)}, bf16[192,128,128]{2,1,0:T(8,128)(2,1)S(1)}, u32[]{:S(2)}) copy-start(bf16[192,128,128]{2,1,0:T(8,128)(2,1)S(1)} %shard_map.94.adj_ref) | copy-start | bytes 18874372
  56.8 2.8 %copy-start.1 = (bf16[192,128,128]{2,1,0:T(8,128)(2,1)S(1)}, bf16[192,128,128]{2,1,0:T(8,128)(2,1)}, u32[]{:S(2)}) copy-start(bf16[192,128,128]{2,1,0:T(8,128)(2,1)} %copy-done) | copy-start | bytes 18874372
  64.9 5.5 %collective-permute-start = (f32[4,8,32,128]{3,2,1,0:T(8,128)S(1)}, f32[4,8,32,128]{3,2,1,0:T(8,128)S(1)}, u32[]{:S(2)}, u32[]{:S(2)}) collective-permute-start(f32[4,8,32,128]{3,2,1,0:T(8,128)S(1)} %get-tuple-element.16), channel_id=1, source_target_pairs={{0,8},{8,0},{1,9},{9,1},{2,10},{10,2},{3,11},{11,3},{4,12},{12,4},... | collective-permute-start | bytes 1572872 | tf_op jit(solution)/shard_map/ppermute | solution.py:209
  71.2 23.0 %all-to-all-start.1 = ((bf16[32,48,128]{2,1,0:T(8,128)(2,1)}), bf16[32,48,128]{2,1,0:T(8,128)(2,1)S(1)}, u32[]{:S(2)}, u32[]{:S(2)}) async-start(bf16[32,48,128]{2,1,0:T(8,128)(2,1)} %shard_map.97), calls=%async_computation.1 | async-start | bytes 786432 | tf_op jit(solution)/shard_map/all_to_all | solution.py:218
  113.8 7.8 %collective-permute-start.1 = (bf16[32,48,128]{2,1,0:T(8,128)(2,1)S(1)}, bf16[32,48,128]{2,1,0:T(8,128)(2,1)S(1)}, u32[]{:S(2)}, u32[]{:S(2)}) collective-permute-start(bf16[32,48,128]{2,1,0:T(8,128)(2,1)S(1)} %all_to_all.25.mine_ref), channel_id=1, source_target_pairs={{0,8},{8,0},{1,9},{9,1},{2,10},{10,2},{3,11},{11,3},{4,12},{12,4},... | collective-permute-start | bytes 1179656 | tf_op jit(solution)/shard_map/ppermute | solution.py:233
  169.2 7.8 %all-to-all-start.4 = ((f32[4,16,128]{2,1,0:T(8,128)}), f32[4,16,128]{2,1,0:T(8,128)S(1)}, u32[]{:S(2)}, u32[]{:S(2)}) async-start(f32[4,16,128]{2,1,0:T(8,128)} %get-tuple-element.25), calls=%async_computation.4 | async-start | bytes 65536 | tf_op jit(solution)/shard_map/all_to_all | solution.py:257

commit v5 on v4

v5 whole, which is shorter than its diff:
```python
import math

import jax
import jax.numpy as jnp
from jax import lax
from jax.experimental import pallas as pl
from jax.experimental.pallas import tpu as pltpu
from jax.sharding import PartitionSpec as P

UNROLL = 8
CHUNK = 16
PIECE = 16
CORES = 2
SIDES = 2
VMEM_LIMIT = 24 * 1024 * 1024
NT = (((1,), (1,)), ((), ()))
NN = (((1,), (0,)), ((), ()))
TN = (((0,), (0,)), ((), ()))


def dot(a, b, dims):
    return lax.dot_general(a, b, dims, preferred_element_type=jnp.float32)


def accumulate_tiles(count, source, adj_ref, tiles_ref, done, acc_ref, target_of, dims):
    chunks = adj_ref.shape[0] // CHUNK

    def load(chunk):
        part = pl.ds(chunk * CHUNK, CHUNK)
        return pltpu.make_async_copy(adj_ref.at[part], tiles_ref.at[part], done.at[chunk])

    for chunk in range(chunks):
        load(chunk).start()
    acc_ref[...] = jnp.zeros_like(acc_ref)

    @pl.loop(0, chunks)
    def _(chunk):
        load(chunk).wait()

        @pl.loop(0, CHUNK // UNROLL)
        def _(group):
            first = chunk * CHUNK + group * UNROLL

            @pl.when(first < count)
            def _():
                terms = []
                for u in range(UNROLL):
                    term = dot(source(first + u), tiles_ref[first + u], dims)
                    terms.append(jnp.where(first + u < count, term, 0.0))
                for u in range(UNROLL):
                    target = target_of(first + u)
                    acc_ref[target] += terms[u]


def forward_kernel(
    place, rows, cols, count, adj_ref, same_ref, far_ref, keep_ref, send_ref, acc_ref, *tiles
):
    core, side = place[0], place[1]
    extent = adj_ref.shape[1]
    blocks = same_ref.shape[2] // extent

    def source(slot):
        col = cols[slot]
        row_device = col // blocks
        nodes = pl.ds(pl.multiple_of((col % blocks) * extent, extent), extent)
        ring = row_device // SIDES
        return jnp.where(
            row_device % SIDES == side, same_ref[ring, :, nodes], far_ref[ring, :, nodes]
        )

    accumulate_tiles(count[0], source, adj_ref, *tiles, acc_ref, lambda s: rows[s], NT)
    near, feats = keep_ref.shape[:2]
    for pair in range(near):
        keep_ref[pair] = acc_ref[pl.ds((pair * CORES + core) * feats, feats)]
        send_ref[pair] = acc_ref[pl.ds((pair * CORES + 1 - core) * feats, feats)]


def spread_kernel(value_ref, out_ref):
    for copy in range(out_ref.shape[0]):
        out_ref[copy] = value_ref[...]


def combine_kernel(near, keep_ref, received_ref, weight_ref, out_ref):
    owners, width, extent = keep_ref.shape
    halves = weight_ref.shape[1] // extent
    out_ref[:, :width] = (keep_ref[...] + received_ref[...]).astype(out_ref.dtype)
    top = pl.multiple_of((near[0] // halves) * PIECE, PIECE)
    left = pl.multiple_of((near[0] % halves) * extent, extent)
    piece = weight_ref[pl.ds(top, PIECE), pl.ds(left, extent)]
    for owner in range(owners):
        out_ref[owner, width:] = piece


def dense_kernel(terms_ref, grad_ref, out_ref, act_ref, weight_ref):
    near, feats, height, extent = terms_ref.shape
    width = height - PIECE
    full = feats * width
    halves = full // extent
    for pair in range(near):
        for feat in range(feats):
            top = feat * width + (pair // halves) * PIECE
            left = (pair % halves) * extent
            weight_ref[top : top + PIECE, left : left + extent] = terms_ref[pair, feat, width:]
    weight = weight_ref[...]
    summed = jnp.sum(terms_ref[:, :, :width].astype(jnp.float32), axis=0).reshape(full, extent)
    high = summed.astype(jnp.bfloat16)
    low = (summed - high.astype(jnp.float32)).astype(jnp.bfloat16)
    pre_act = dot(high, weight, TN) + dot(low, weight, TN)
    gate = jax.nn.sigmoid(pre_act)
    act_ref[...] = (pre_act * gate).astype(act_ref.dtype)
    derivative = gate * (1.0 + pre_act * (1.0 - gate))
    grad_pre = (grad_ref[...].astype(jnp.float32) * derivative).astype(jnp.bfloat16)
    projected = dot(weight, grad_pre, NT).astype(out_ref.dtype)
    weight_term = (dot(high, grad_pre, NN) + dot(low, grad_pre, NN)).astype(out_ref.dtype)
    for pair in range(near):
        for feat in range(feats):
            top = feat * width + (pair // halves) * PIECE
            left = (pair % halves) * extent
            out_ref[pair * feats + feat, :width] = projected[feat * width : (feat + 1) * width]
            out_ref[pair * feats + feat, width:] = weight_term[
                top : top + PIECE, left : left + extent
            ]


def backward_kernel(
    place, rows, cols, count, adj_ref, mine_ref, other_ref, far_ref, same_ref, proj_ref, acc_ref, *tiles
):
    core, side = place[0], place[1]
    rings = far_ref.shape[0]
    width = acc_ref.shape[1]
    blocks = acc_ref.shape[0] // (rings * SIDES)
    feats = proj_ref.shape[2]
    for pair in range(proj_ref.shape[0]):
        part = slice(pair * feats, (pair + 1) * feats)
        proj_ref[pair, core] = mine_ref[part, :width]
        proj_ref[pair, 1 - core] = other_ref[part, :width]

    def source(slot):
        row = rows[slot]
        return proj_ref[row // (CORES * feats), (row // feats) % CORES, row % feats]

    accumulate_tiles(count[0], source, adj_ref, *tiles, acc_ref, lambda s: cols[s], NN)
    weight_term = jnp.sum(mine_ref[:, width:].astype(jnp.float32), axis=0) + jnp.sum(
        other_ref[:, width:].astype(jnp.float32), axis=0
    )
    for ring in range(rings):
        for out_ref, out_side in ((far_ref, 1 - side), (same_ref, side)):
            start = (ring * SIDES + out_side) * blocks
            for block in range(blocks):
                out_ref[ring, block * width : (block + 1) * width] = acc_ref[start + block].astype(
                    out_ref.dtype
                )
        far_ref[ring, blocks * width :] = weight_term.astype(far_ref.dtype)


def reduce_kernel(pieces_ref, out_ref):
    out_ref[...] = jnp.sum(pieces_ref[...].astype(jnp.float32), axis=0)


def final_kernel(scale, same_ref, swapped_ref, summed_ref, grad_ref, weight_ref):
    width, nodes = grad_ref.shape
    extent = same_ref.shape[2]
    for block in range(nodes // extent):
        part = slice(block * width, (block + 1) * width)
        grad_ref[:, block * extent : (block + 1) * extent] = swapped_ref[part] + jnp.sum(
            same_ref[:, part].astype(jnp.float32), axis=0
        )
    rest = slice(nodes // extent * width, None)
    weight_term = (summed_ref[rest] + swapped_ref[rest]) * scale
    for pair in range(weight_ref.shape[0]):
        weight_ref[pair] = weight_term


SMEM_SPEC = pl.BlockSpec(memory_space=pltpu.SMEM)
VMEM_SPEC = pl.BlockSpec(memory_space=pltpu.VMEM)


def in_vmem(array):
    return pltpu.with_memory_space_constraint(array, pltpu.VMEM)


def call(kernel, scalars, arrays, out_shapes, scratch=()):
    return pl.pallas_call(
        kernel,
        out_shape=out_shapes,
        in_specs=[SMEM_SPEC] * len(scalars) + [VMEM_SPEC] * len(arrays),
        out_specs=jax.tree.map(lambda _: VMEM_SPEC, out_shapes),
        scratch_shapes=scratch,
        compiler_params=pltpu.CompilerParams(vmem_limit_bytes=VMEM_LIMIT),
    )(*scalars, *(in_vmem(array) for array in arrays))


def tile_call(kernel, scalars, adjacency, arrays, out_shapes, scratch):
    return pl.pallas_call(
        kernel,
        out_shape=out_shapes,
        in_specs=[SMEM_SPEC] * len(scalars)
        + [pl.BlockSpec(memory_space=pltpu.HBM)]
        + [VMEM_SPEC] * len(arrays),
        out_specs=jax.tree.map(lambda _: VMEM_SPEC, out_shapes),
        scratch_shapes=[
            *scratch,
            pltpu.VMEM(adjacency.shape, adjacency.dtype),
            pltpu.SemaphoreType.DMA((adjacency.shape[0] // CHUNK,)),
        ],
        compiler_params=pltpu.CompilerParams(vmem_limit_bytes=VMEM_LIMIT),
    )(
        *scalars,
        pltpu.with_memory_space_constraint(adjacency, pltpu.HBM),
        *(in_vmem(array) for array in arrays),
    )


def local(features, weight, grad_out, adjacency, tile_rows, tile_cols, tile_count):
    nodes, width = features.shape
    extent = adjacency.shape[1]
    rings, near, feats = (lax.axis_size(name) for name in ("ring", "near", "feat"))
    full = feats * width
    blocks = nodes // extent
    owners = near * feats
    swap = [(0, 1), (1, 0)]
    core, side, near_index = (
        lax.axis_index(name).astype(jnp.int32) for name in ("core", "side", "near")
    )
    scalars = (jnp.stack([core, side]), tile_rows, tile_cols, tile_count)
    bf16, f32 = jnp.bfloat16, jnp.float32

    def spread(value):
        copies = call(spread_kernel, (), (value,), pltpu.VMEM((rings, width, nodes), bf16))
        return lax.all_to_all(copies, "ring", 0, 0, tiled=False)

    own = features.T
    partner = lax.ppermute(own, "side", swap)
    same = spread(own)
    same, partner = lax.optimization_barrier((same, partner))
    far = spread(partner)

    half = jax.ShapeDtypeStruct((near, feats, width, extent), f32)
    keep, send = tile_call(
        forward_kernel,
        scalars,
        adjacency,
        (same, far),
        (half, half),
        [pltpu.VMEM((CORES * owners, width, extent), f32)],
    )
    received = lax.ppermute(send, "core", swap)
    flat = (owners, width, extent)
    terms = call(
        combine_kernel,
        (near_index.reshape(1),),
        (keep.reshape(flat), received.reshape(flat), weight),
        pltpu.VMEM((owners, width + PIECE, extent), bf16),
    )
    terms = lax.all_to_all(terms, ("near", "feat"), 0, 0, tiled=False)
    outgoing, activated = call(
        dense_kernel,
        (),
        (terms.reshape(near, feats, width + PIECE, extent), grad_out),
        (
            pltpu.VMEM((owners, width + PIECE, extent), bf16),
            jax.ShapeDtypeStruct((extent, full), bf16),
        ),
        [pltpu.VMEM((full, full), bf16)],
    )

    mine = lax.all_to_all(outgoing, ("near", "feat"), 0, 0, tiled=False)
    other = lax.ppermute(mine, "core", swap)
    far, same = tile_call(
        backward_kernel,
        scalars,
        adjacency,
        (mine, other),
        (
            pltpu.VMEM((rings, blocks * width + PIECE, extent), bf16),
            pltpu.VMEM((rings, blocks * width, extent), bf16),
        ),
        [
            pltpu.VMEM((near, CORES, feats, width, extent), bf16),
            pltpu.VMEM((rings * SIDES * blocks, width, extent), f32),
        ],
    )
    far = lax.all_to_all(far, "ring", 0, 0, tiled=False)
    summed = call(
        reduce_kernel,
        (),
        (far,),
        jax.ShapeDtypeStruct((blocks * width + PIECE, extent), f32),
    )
    swapped = lax.ppermute(summed, "side", swap)
    same, summed = lax.optimization_barrier((same, summed))
    same = lax.all_to_all(same, "ring", 0, 0, tiled=False)
    scale = 1.0 / math.sqrt(nodes * rings * SIDES * near * CORES)
    feature_grad, weight_piece = call(
        lambda *refs: final_kernel(scale, *refs),
        (),
        (same, swapped, summed),
        (
            jax.ShapeDtypeStruct((width, nodes), f32),
            pltpu.VMEM((near, PIECE, extent), f32),
        ),
    )
    weight_grad = lax.all_to_all(weight_piece, "near", 0, 0, tiled=False)
    weight_grad = weight_grad.reshape(width // PIECE, full // extent, PIECE, extent)
    weight_grad = weight_grad.transpose(0, 2, 1, 3).reshape(width, full)
    return (activated, weight_grad, feature_grad.T)


def solution(mesh):
    rows, cols, feats = (mesh.shape[name] for name in ("row", "col", "feat"))
    fine = jax.sharding.Mesh(
        mesh.devices.reshape(rows // SIDES, SIDES, cols // CORES, CORES, feats),
        ("ring", "side", "near", "core", "feat"),
    )
    pair = P(("ring", "side", "near", "core"))
    owner = P(("ring", "side", "near", "core", "feat"), None)
    by_column = P(("near", "core", "ring", "side"), "feat")
    return jax.shard_map(
        local,
        mesh=fine,
        in_specs=(by_column, P("feat", None), owner, pair, pair, pair, pair),
        out_specs=(owner, P("feat", None), by_column),
        check_vma=False,
    )
```

time: 180 us -> 173 us (0.961)
  waiting for transfers between devices: 45.4 us -> 23.8 us
  blocking collectives: 61 us -> 75 us
  starting transfers between devices: 43.2 us -> 55.8 us
  Pallas kernels: 19 us -> 13.4 us
  local copies, waits for them, and re-layouts: 6.93 us -> 2.84 us
    all_to_all x3, waiting for transfers between devices: 43.9 us -> 16.7 us  [the longest x2 11.2 us: spread(): return lax.all_to_all(copies, 'ring', 0, 0, tiled=False)]
    ppermute x0 -> x2, starting transfers between devices: none -> 24.4 us  [the longest x1 14.4 us: local(): partner = lax.ppermute(own, 'side', swap)]
    all_to_all x3, starting transfers between devices: 34.2 us -> 18.5 us  [the longest x2 15 us: spread(): return lax.all_to_all(copies, 'ring', 0, 0, tiled=False)]
    all_to_all x1 -> x3, blocking collectives: 42 us -> 56 us  [the longest x1 26 us: local(): terms = lax.all_to_all(terms, ('near', 'feat'), 0, 0, tiled=False)]
    pallas_call x6, Pallas kernels: 13.4 us -> 3.44 us  [call(): pl.pallas_call(kernel, out_shape=out_shapes, in_specs=[SMEM_SPEC] * len(s...]
    pallas_call x2, Pallas kernels: 5.62 us -> 9.95 us  [tile_call(): pl.pallas_call(kernel, out_shape=out_shapes, in_specs=[SMEM_SPEC] * len(s...]
    ppermute x0 -> x2, waiting for transfers between devices: none -> 4.28 us  [the longest x1 2.43 us: local(): swapped = lax.ppermute(summed, 'side', swap)]
    unnamed x15, local copies, waits for them, and re-layouts: 6.92 us -> 2.83 us
  transfers between devices with their start and end apart: 5 -> 7, of which waited for: 4 -> 6; matrix products, arithmetic and copies ran while one was open for 0% -> 0% of each run, Pallas kernels for 3% -> 0%
where the time goes in v5:
time: 173 us; the launch traced here: 172 us
  blocking collectives  75 us (43%)
  starting transfers between devices  55.8 us (32%)
  waiting for transfers between devices  23.8 us (14%)
  Pallas kernels  13.4 us (8%)
  local copies, waits for them, and re-layouts  2.84 us (2%)
    all_to_all x1, blocking collectives, local(): terms = lax.all_to_all(terms, ('near', 'feat'), 0, 0, tiled=False)  26 us
    all_to_all x1, blocking collectives, local(): far = lax.all_to_all(far, 'ring', 0, 0, tiled=False)  21.3 us
    all_to_all x1, blocking collectives, local(): mine = lax.all_to_all(outgoing, ('near', 'feat'), 0, 0, tiled=False)  19 us
    all_to_all x2, starting transfers between devices, spread(): return lax.all_to_all(copies, 'ring', 0, 0, tiled=False)  15 us
    ppermute x1, starting transfers between devices, local(): partner = lax.ppermute(own, 'side', swap)  14.4 us
    all_to_all x2, waiting for transfers between devices, spread(): return lax.all_to_all(copies, 'ring', 0, 0, tiled=False)  11.2 us
    ppermute x1, starting transfers between devices, local(): swapped = lax.ppermute(summed, 'side', swap)  9.97 us
    pallas_call x2, Pallas kernels, tile_call(): pl.pallas_call(kernel, out_shape=out_shapes, in_specs=[SMEM_SPEC] * len(s...  9.95 us
  transfers between devices with their start and end apart: 7, of which 6 were waited for; matrix products, arithmetic and copies ran while one was open for 0% of the time, Pallas kernels for 0%

profile of v5, /device:TPU:1, one launch (start us, length us, event | category | flops | bytes accessed | tf_op | source)
XLA Modules:
  0.0 172.3 jit_solution(16656890066827956604)
XLA Ops:
  0.6 0.0 copy-start
  0.6 0.8 copy-done
  1.5 0.0 copy-start.2
  1.5 0.8 shard_map.94
  2.3 0.0 copy-start.1
  2.3 8.2 %all-to-all-start = ((bf16[8,32,1024]{2,1,0:T(8,128)(2,1)}), bf16[8,32,1024]{2,1,0:T(8,128)(2,1)S(1)}, u32[]{:S(2)}, u32[]{:S(2)}) async-start(bf16[8,32,1024]{2,1,0:T(8,128)(2,1)} %shard_map.94), calls=%async_computation | async-start | bytes 1048576 | tf_op jit(solution)/shard_map/all_to_all | solution.py:230
  10.5 0.0 copy-start.4
  10.5 0.0 copy-start.6
  10.6 14.4 %collective-permute-start = (bf16[32,1024]{1,0:T(8,128)(2,1)}, bf16[32,1024]{1,0:T(8,128)(2,1)S(1)}, u32[]{:S(2)}, u32[]{:S(2)}) collective-permute-start(bf16[32,1024]{1,0:T(8,128)(2,1)} %bitcast.19), channel_id=1, source_target_pairs={{0,64},{64,0},{1,65},{65,1},{2,66},{66,2},{3,67},{67,3},{4,68},{68... | collective-permute-start | bytes 196616 | tf_op jit(solution)/shard_map/ppermute | solution.py:233
  25.0 1.9 %collective-permute-done.value_ref = bf16[32,1024]{1,0:T(8,128)(2,1)S(1)} collective-permute-done((bf16[32,1024]{1,0:T(8,128)(2,1)}, bf16[32,1024]{1,0:T(8,128)(2,1)S(1)}, u32[]{:S(2)}, u32[]{:S(2)}) %collective-permute-start) | collective-permute-done | bytes 65568 | tf_op jit(solution)/shard_map/ppermute | solution.py:233
  26.8 0.0 all-to-all-done.same_ref
  26.8 0.8 shard_map.95
  27.7 6.7 %all-to-all-start.1 = ((bf16[8,32,1024]{2,1,0:T(8,128)(2,1)}), bf16[8,32,1024]{2,1,0:T(8,128)(2,1)S(1)}, u32[]{:S(2)}, u32[]{:S(2)}) async-start(bf16[8,32,1024]{2,1,0:T(8,128)(2,1)} %shard_map.95), calls=%async_computation.1 | async-start | bytes 1048576 | tf_op jit(solution)/shard_map/all_to_all | solution.py:230
  35.0 0.1 pad_add_fusion.place
  35.1 11.2 %all-to-all-done.1.far_ref = bf16[8,32,1024]{2,1,0:T(8,128)(2,1)S(1)} async-done(((bf16[8,32,1024]{2,1,0:T(8,128)(2,1)}), bf16[8,32,1024]{2,1,0:T(8,128)(2,1)S(1)}, u32[]{:S(2)}, u32[]{:S(2)}) %all-to-all-start.1) | async-done | bytes 524320 | tf_op jit(solution)/shard_map/all_to_all | solution.py:230
  46.3 0.0 copy-start.3
  46.3 0.7 copy-done.3
  47.0 0.0 copy-start.5
  47.0 0.7 copy-done.5
  47.6 4.8 %shard_map.96 = (f32[4,8,32,128]{3,2,1,0:T(8,128)S(1)}, f32[4,8,32,128]{3,2,1,0:T(8,128)S(1)}) custom-call(s32[2]{0:T(128)S(1)} %pad_add_fusion.place, s32[192]{0:T(256)S(1)} %copy-done.3, s32[192]{0:T(256)S(1)} %copy-done.5, s32[1]{0:T(128)S(6)} %copy.14.count, bf16[192,128,128]{2,1,0:T(8,128)(2,1)} %adj_ref.3, ...), custom_call_target="tpu_custom_call" | custom-call | tf_op jit(solution)/shard_map/pallas_call | solution.py:194
  52.4 8.0 %collective-permute-start.1 = (f32[4,8,32,128]{3,2,1,0:T(8,128)S(1)}, f32[4,8,32,128]{3,2,1,0:T(8,128)S(1)}, u32[]{:S(2)}, u32[]{:S(2)}) collective-permute-start(f32[4,8,32,128]{3,2,1,0:T(8,128)S(1)} %get-tuple-element.18), channel_id=1, source_target_pairs={{0,8},{8,0},{1,9},{9,1},{2,10},{10,2},{3,11},{11,3},{4,12},{12,4},... | collective-permute-start | bytes 1572872 | tf_op jit(solution)/shard_map/ppermute | solution.py:247
  60.4 1.5 collective-permute-done.1
  61.9 0.0 copy-done.2
  61.9 0.1 shard_map.97
  62.0 26.0 %all_to_all.35 = bf16[32,48,128]{2,1,0:T(8,128)(2,1)S(1)} all-to-all(bf16[32,48,128]{2,1,0:T(8,128)(2,1)S(1)} %shard_map.97), channel_id=1, replica_groups=mesh['ring'=8,'side'=2,'near'=4,'core'=2,'feat'=8] {'near','feat'}, dimensions={0} | all-to-all | bytes 786432 | tf_op jit(solution)/shard_map/all_to_all | solution.py:255
  88.0 0.0 copy-done.1
  88.0 0.9 shard_map.98
  88.9 19.0 %all_to_all.36.mine_ref = bf16[32,48,128]{2,1,0:T(8,128)(2,1)S(1)} all-to-all(bf16[32,48,128]{2,1,0:T(8,128)(2,1)S(1)} %get-tuple-element.20), channel_id=1, replica_groups=mesh['ring'=8,'side'=2,'near'=4,'core'=2,'feat'=8] {'near','feat'}, dimensions={0} | all-to-all | bytes 786432 | tf_op jit(solution)/shard_map/all_to_all | solution.py:267
  108.0 5.0 %collective-permute-start.2 = (bf16[32,48,128]{2,1,0:T(8,128)(2,1)S(1)}, bf16[32,48,128]{2,1,0:T(8,128)(2,1)S(1)}, u32[]{:S(2)}, u32[]{:S(2)}) collective-permute-start(bf16[32,48,128]{2,1,0:T(8,128)(2,1)S(1)} %all_to_all.36.mine_ref), channel_id=1, source_target_pairs={{0,8},{8,0},{1,9},{9,1},{2,10},{10,2},{3,11},{11,3},{4,12},{12,4},... | collective-permute-start | bytes 1179656 | tf_op jit(solution)/shard_map/ppermute | solution.py:268
  112.9 1.3 collective-permute-done.2.other_ref
  114.3 0.0 copy-done.4
  114.3 0.0 copy-done.6
  114.3 5.2 %shard_map.99 = (bf16[8,272,128]{2,1,0:T(8,128)(2,1)S(1)}, bf16[8,256,128]{2,1,0:T(8,128)(2,1)}) custom-call(s32[2]{0:T(128)S(1)} %pad_add_fusion.place, s32[192]{0:T(256)S(1)} %copy-done.4, s32[192]{0:T(256)S(1)} %copy-done.6, s32[1]{0:T(128)S(6)} %copy.14.count, bf16[192,128,128]{2,1,0:T(8,128)(2,1)} %adj_ref.3, ...), custom_call_target="tpu_custom_call" | custom-call | tf_op jit(solution)/shard_map/pallas_call | solution.py:194
  119.5 21.3 %all_to_all.37.pieces_ref = bf16[8,272,128]{2,1,0:T(8,128)(2,1)S(1)} all-to-all(bf16[8,272,128]{2,1,0:T(8,128)(2,1)S(1)} %get-tuple-element.22), channel_id=1, replica_groups=mesh['ring'=8,'side'=2,'near'=4,'core'=2,'feat'=8] {'ring'}, dimensions={0} | all-to-all | bytes 1114112 | tf_op jit(solution)/shard_map/all_to_all | solution.py:283
  140.7 0.1 shard_map.100.refs_2_
  140.8 3.5 %all-to-all-start.5 = ((bf16[8,256,128]{2,1,0:T(8,128)(2,1)}), bf16[8,256,128]{2,1,0:T(8,128)(2,1)S(1)}, u32[]{:S(2)}, u32[]{:S(2)}) async-start(bf16[8,256,128]{2,1,0:T(8,128)(2,1)} %get-tuple-element.23), calls=%async_computation.5 | async-start | bytes 1048576 | tf_op jit(solution)/shard_map/all_to_all | solution.py:292
  144.3 10.0 %collective-permute-start.3 = (f32[272,128]{1,0:T(8,128)S(1)}, f32[272,128]{1,0:T(8,128)S(1)}, u32[]{:S(2)}, u32[]{:S(2)}) collective-permute-start(f32[272,128]{1,0:T(8,128)S(1)} %shard_map.100.refs_2_), channel_id=1, source_target_pairs={{0,64},{64,0},{1,65},{65,1},{2,66},{66,2},{3,67},{67,3},{4,68},{68... | collective-permute-start | bytes 417800 | tf_op jit(solution)/shard_map/ppermute | solution.py:290
  154.3 2.4 %collective-permute-done.3.refs_1_ = f32[272,128]{1,0:T(8,128)S(1)} collective-permute-done((f32[272,128]{1,0:T(8,128)S(1)}, f32[272,128]{1,0:T(8,128)S(1)}, u32[]{:S(2)}, u32[]{:S(2)}) %collective-permute-start.3) | collective-permute-done | bytes 139296 | tf_op jit(solution)/shard_map/ppermute | solution.py:290
  156.7 5.5 %all-to-all-done.5.refs_0_ = bf16[8,256,128]{2,1,0:T(8,128)(2,1)S(1)} async-done(((bf16[8,256,128]{2,1,0:T(8,128)(2,1)}), bf16[8,256,128]{2,1,0:T(8,128)(2,1)S(1)}, u32[]{:S(2)}, u32[]{:S(2)}) %all-to-all-start.5) | async-done | bytes 524320 | tf_op jit(solution)/shard_map/all_to_all | solution.py:292
  162.2 0.7 shard_map.101
  163.0 8.7 %all_to_all.38 = f32[4,16,128]{2,1,0:T(8,128)S(1)} all-to-all(f32[4,16,128]{2,1,0:T(8,128)S(1)} %get-tuple-element.25), channel_id=1, replica_groups=mesh['ring'=8,'side'=2,'near'=4,'core'=2,'feat'=8] {'near'}, dimensions={0} | all-to-all | bytes 65536 | tf_op jit(solution)/shard_map/all_to_all | solution.py:303
  171.7 0.6 copy.13
  (1 shorter events, 0.0 us)
Async XLA Ops:
  0.6 0.8 copy-start
  1.5 60.4 %copy-start.2 = (bf16[32,256]{1,0:T(8,128)(2,1)S(1)}, bf16[32,256]{1,0:T(8,128)(2,1)}, u32[]{:S(2)}) copy-start(bf16[32,256]{1,0:T(8,128)(2,1)} %weight_ref.1) | copy-start | bytes 49156
  2.3 85.7 %copy-start.1 = (bf16[128,256]{1,0:T(8,128)(2,1)S(1)}, bf16[128,256]{1,0:T(8,128)(2,1)}, u32[]{:S(2)}) copy-start(bf16[128,256]{1,0:T(8,128)(2,1)} %grad_ref.1) | copy-start | bytes 196612
  2.3 24.5 %all-to-all-start = ((bf16[8,32,1024]{2,1,0:T(8,128)(2,1)}), bf16[8,32,1024]{2,1,0:T(8,128)(2,1)S(1)}, u32[]{:S(2)}, u32[]{:S(2)}) async-start(bf16[8,32,1024]{2,1,0:T(8,128)(2,1)} %shard_map.94), calls=%async_computation | async-start | bytes 1048576 | tf_op jit(solution)/shard_map/all_to_all | solution.py:230
  10.5 103.7 %copy-start.4 = (s32[192]{0:T(256)S(1)}, s32[192]{0:T(256)}, u32[]{:S(2)}) copy-start(s32[192]{0:T(256)} %rows.3) | copy-start | bytes 2308
  10.5 103.7 %copy-start.6 = (s32[192]{0:T(256)S(1)}, s32[192]{0:T(256)}, u32[]{:S(2)}) copy-start(s32[192]{0:T(256)} %cols.3) | copy-start | bytes 2308
  10.6 16.3 %collective-permute-start = (bf16[32,1024]{1,0:T(8,128)(2,1)}, bf16[32,1024]{1,0:T(8,128)(2,1)S(1)}, u32[]{:S(2)}, u32[]{:S(2)}) collective-permute-start(bf16[32,1024]{1,0:T(8,128)(2,1)} %bitcast.19), channel_id=1, source_target_pairs={{0,64},{64,0},{1,65},{65,1},{2,66},{66,2},{3,67},{67,3},{4,68},{68... | collective-permute-start | bytes 196616 | tf_op jit(solution)/shard_map/ppermute | solution.py:233
  27.7 18.6 %all-to-all-start.1 = ((bf16[8,32,1024]{2,1,0:T(8,128)(2,1)}), bf16[8,32,1024]{2,1,0:T(8,128)(2,1)S(1)}, u32[]{:S(2)}, u32[]{:S(2)}) async-start(bf16[8,32,1024]{2,1,0:T(8,128)(2,1)} %shard_map.95), calls=%async_computation.1 | async-start | bytes 1048576 | tf_op jit(solution)/shard_map/all_to_all | solution.py:230
  46.3 0.7 copy-start.3
  47.0 0.7 copy-start.5
  52.4 9.5 %collective-permute-start.1 = (f32[4,8,32,128]{3,2,1,0:T(8,128)S(1)}, f32[4,8,32,128]{3,2,1,0:T(8,128)S(1)}, u32[]{:S(2)}, u32[]{:S(2)}) collective-permute-start(f32[4,8,32,128]{3,2,1,0:T(8,128)S(1)} %get-tuple-element.18), channel_id=1, source_target_pairs={{0,8},{8,0},{1,9},{9,1},{2,10},{10,2},{3,11},{11,3},{4,12},{12,4},... | collective-permute-start | bytes 1572872 | tf_op jit(solution)/shard_map/ppermute | solution.py:247
  108.0 6.3 %collective-permute-start.2 = (bf16[32,48,128]{2,1,0:T(8,128)(2,1)S(1)}, bf16[32,48,128]{2,1,0:T(8,128)(2,1)S(1)}, u32[]{:S(2)}, u32[]{:S(2)}) collective-permute-start(bf16[32,48,128]{2,1,0:T(8,128)(2,1)S(1)} %all_to_all.36.mine_ref), channel_id=1, source_target_pairs={{0,8},{8,0},{1,9},{9,1},{2,10},{10,2},{3,11},{11,3},{4,12},{12,4},... | collective-permute-start | bytes 1179656 | tf_op jit(solution)/shard_map/ppermute | solution.py:268
  140.8 21.5 %all-to-all-start.5 = ((bf16[8,256,128]{2,1,0:T(8,128)(2,1)}), bf16[8,256,128]{2,1,0:T(8,128)(2,1)S(1)}, u32[]{:S(2)}, u32[]{:S(2)}) async-start(bf16[8,256,128]{2,1,0:T(8,128)(2,1)} %get-tuple-element.23), calls=%async_computation.5 | async-start | bytes 1048576 | tf_op jit(solution)/shard_map/all_to_all | solution.py:292
  144.3 12.4 %collective-permute-start.3 = (f32[272,128]{1,0:T(8,128)S(1)}, f32[272,128]{1,0:T(8,128)S(1)}, u32[]{:S(2)}, u32[]{:S(2)}) collective-permute-start(f32[272,128]{1,0:T(8,128)S(1)} %shard_map.100.refs_2_), channel_id=1, source_target_pairs={{0,64},{64,0},{1,65},{65,1},{2,66},{66,2},{3,67},{67,3},{4,68},{68... | collective-permute-start | bytes 417800 | tf_op jit(solution)/shard_map/ppermute | solution.py:290

commit v6 on v5

--- a/solution.py
+++ b/solution.py
@@ -12,6 +12,7 @@
 PIECE = 16
 CORES = 2
 SIDES = 2
+HEAD = 3
 VMEM_LIMIT = 24 * 1024 * 1024
 NT = (((1,), (1,)), ((), ()))
 NN = (((1,), (0,)), ((), ()))
@@ -52,23 +53,22 @@
                     acc_ref[target] += terms[u]
 
 
-def forward_kernel(
-    place, rows, cols, count, adj_ref, same_ref, far_ref, keep_ref, send_ref, acc_ref, *tiles
-):
-    core, side = place[0], place[1]
-    extent = adj_ref.shape[1]
-    blocks = same_ref.shape[2] // extent
+def slots_of(table, slots):
+    return lambda s: table[HEAD + s], lambda s: table[HEAD + slots + s]
+
+
+def forward_kernel(table, adj_ref, feat_ref, keep_ref, send_ref, acc_ref, *tiles):
+    core, count = table[0], table[2]
+    slots, extent, _ = adj_ref.shape
+    blocks = feat_ref.shape[2] // extent
+    row_of, col_of = slots_of(table, slots)
 
     def source(slot):
-        col = cols[slot]
-        row_device = col // blocks
+        col = col_of(slot)
         nodes = pl.ds(pl.multiple_of((col % blocks) * extent, extent), extent)
-        ring = row_device // SIDES
-        return jnp.where(
-            row_device % SIDES == side, same_ref[ring, :, nodes], far_ref[ring, :, nodes]
-        )
-
-    accumulate_tiles(count[0], source, adj_ref, *tiles, acc_ref, lambda s: rows[s], NT)
+        return feat_ref[col // blocks, :, nodes]
+
+    accumulate_tiles(count, source, adj_ref, *tiles, acc_ref, row_of, NT)
     near, feats = keep_ref.shape[:2]
     for pair in range(near):
         keep_ref[pair] = acc_ref[pl.ds((pair * CORES + core) * feats, feats)]
@@ -114,18 +114,20 @@
     weight_term = (dot(high, grad_pre, NN) + dot(low, grad_pre, NN)).astype(out_ref.dtype)
     for pair in range(near):
         for feat in range(feats):
-            top = feat * width + (pair // halves) * PIECE
-            left = (pair % halves) * extent
             out_ref[pair * feats + feat, :width] = projected[feat * width : (feat + 1) * width]
-            out_ref[pair * feats + feat, width:] = weight_term[
-                top : top + PIECE, left : left + extent
-            ]
+            for part in range((out_ref.shape[1] - width) // PIECE):
+                top = feat * width + (part // halves) * PIECE
+                left = (part % halves) * extent
+                out_ref[
+                    pair * feats + feat, width + part * PIECE : width + (part + 1) * PIECE
+                ] = weight_term[top : top + PIECE, left : left + extent]
 
 
 def backward_kernel(
-    place, rows, cols, count, adj_ref, mine_ref, other_ref, far_ref, same_ref, proj_ref, acc_ref, *tiles
+    table, adj_ref, mine_ref, other_ref, far_ref, same_ref, proj_ref, acc_ref, *tiles
 ):
-    core, side = place[0], place[1]
+    core, side, count = table[0], table[1], table[2]
+    row_of, col_of = slots_of(table, adj_ref.shape[0])
     rings = far_ref.shape[0]
     width = acc_ref.shape[1]
     blocks = acc_ref.shape[0] // (rings * SIDES)
@@ -136,10 +138,10 @@
         proj_ref[pair, 1 - core] = other_ref[part, :width]
 
     def source(slot):
-        row = rows[slot]
+        row = row_of(slot)
         return proj_ref[row // (CORES * feats), (row // feats) % CORES, row % feats]
 
-    accumulate_tiles(count[0], source, adj_ref, *tiles, acc_ref, lambda s: cols[s], NN)
+    accumulate_tiles(count, source, adj_ref, *tiles, acc_ref, col_of, NN)
     weight_term = jnp.sum(mine_ref[:, width:].astype(jnp.float32), axis=0) + jnp.sum(
         other_ref[:, width:].astype(jnp.float32), axis=0
     )
@@ -165,10 +167,14 @@
         grad_ref[:, block * extent : (block + 1) * extent] = swapped_ref[part] + jnp.sum(
             same_ref[:, part].astype(jnp.float32), axis=0
         )
-    rest = slice(nodes // extent * width, None)
-    weight_term = (summed_ref[rest] + swapped_ref[rest]) * scale
-    for pair in range(weight_ref.shape[0]):
-        weight_ref[pair] = weight_term
+    halves = weight_ref.shape[1] // extent
+    for part in range(width // PIECE * halves):
+        start = nodes // extent * width + part * PIECE
+        rest = slice(start, start + PIECE)
+        top, left = (part // halves) * PIECE, (part % halves) * extent
+        weight_ref[top : top + PIECE, left : left + extent] = (
+            summed_ref[rest] + swapped_ref[rest]
+        ) * scale
 
 
 SMEM_SPEC = pl.BlockSpec(memory_space=pltpu.SMEM)
@@ -222,25 +228,21 @@
     core, side, near_index = (
         lax.axis_index(name).astype(jnp.int32) for name in ("core", "side", "near")
     )
-    scalars = (jnp.stack([core, side]), tile_rows, tile_cols, tile_count)
+    table = jnp.concatenate([jnp.stack([core, side]), tile_count, tile_rows, tile_cols])
+    parts = full // extent * width // PIECE
     bf16, f32 = jnp.bfloat16, jnp.float32
 
-    def spread(value):
-        copies = call(spread_kernel, (), (value,), pltpu.VMEM((rings, width, nodes), bf16))
-        return lax.all_to_all(copies, "ring", 0, 0, tiled=False)
-
-    own = features.T
-    partner = lax.ppermute(own, "side", swap)
-    same = spread(own)
-    same, partner = lax.optimization_barrier((same, partner))
-    far = spread(partner)
+    own = call(
+        spread_kernel, (), (features.T,), pltpu.VMEM((rings * SIDES, width, nodes), bf16)
+    )
+    gathered = lax.all_to_all(own, ("ring", "side"), 0, 0, tiled=False)
 
     half = jax.ShapeDtypeStruct((near, feats, width, extent), f32)
     keep, send = tile_call(
         forward_kernel,
-        scalars,
+        (table,),
         adjacency,
-        (same, far),
+        (gathered,),
         (half, half),
         [pltpu.VMEM((CORES * owners, width, extent), f32)],
     )
@@ -258,7 +260,7 @@
         (),
         (terms.reshape(near, feats, width + PIECE, extent), grad_out),
         (
-            pltpu.VMEM((owners, width + PIECE, extent), bf16),
+            pltpu.VMEM((owners, width + parts * PIECE, extent), bf16),
             jax.ShapeDtypeStruct((extent, full), bf16),
         ),
         [pltpu.VMEM((full, full), bf16)],
@@ -268,11 +270,11 @@
     other = lax.ppermute(mine, "core", swap)
     far, same = tile_call(
         backward_kernel,
-        scalars,
+        (table,),
         adjacency,
         (mine, other),
         (
-            pltpu.VMEM((rings, blocks * width + PIECE, extent), bf16),
+            pltpu.VMEM((rings, blocks * width + parts * PIECE, extent), bf16),
             pltpu.VMEM((rings, blocks * width, extent), bf16),
         ),
         [
@@ -285,24 +287,21 @@
         reduce_kernel,
         (),
         (far,),
-        jax.ShapeDtypeStruct((blocks * width + PIECE, extent), f32),
+        jax.ShapeDtypeStruct((blocks * width + parts * PIECE, extent), f32),
     )
     swapped = lax.ppermute(summed, "side", swap)
     same, summed = lax.optimization_barrier((same, summed))
     same = lax.all_to_all(same, "ring", 0, 0, tiled=False)
     scale = 1.0 / math.sqrt(nodes * rings * SIDES * near * CORES)
-    feature_grad, weight_piece = call(
+    feature_grad, weight_grad = call(
         lambda *refs: final_kernel(scale, *refs),
         (),
         (same, swapped, summed),
         (
             jax.ShapeDtypeStruct((width, nodes), f32),
-            pltpu.VMEM((near, PIECE, extent), f32),
+            jax.ShapeDtypeStruct((width, full), f32),
         ),
     )
-    weight_grad = lax.all_to_all(weight_piece, "near", 0, 0, tiled=False)
-    weight_grad = weight_grad.reshape(width // PIECE, full // extent, PIECE, extent)
-    weight_grad = weight_grad.transpose(0, 2, 1, 3).reshape(width, full)
     return (activated, weight_grad, feature_grad.T)
 
 

time: 173 us -> 178 us (1.029)
  the two profiles are of different devices: /device:TPU:1 before, /device:TPU:16 now
where the time goes in v6:
time: 178 us; the launch traced here: 177 us
  blocking collectives  76.8 us (43%)
  waiting for transfers between devices  49.1 us (28%)
  starting transfers between devices  33.3 us (19%)
  Pallas kernels  15.4 us (9%)
    all_to_all x1, waiting for transfers between devices, local(): gathered = lax.all_to_all(own, ('ring', 'side'), 0, 0, tiled=False)  35.3 us
    all_to_all x1, blocking collectives, local(): mine = lax.all_to_all(outgoing, ('near', 'feat'), 0, 0, tiled=False)  28.7 us
    all_to_all x1, blocking collectives, local(): far = lax.all_to_all(far, 'ring', 0, 0, tiled=False)  25.1 us
    all_to_all x1, blocking collectives, local(): terms = lax.all_to_all(terms, ('near', 'feat'), 0, 0, tiled=False)  23 us
    all_to_all x1, starting transfers between devices, local(): gathered = lax.all_to_all(own, ('ring', 'side'), 0, 0, tiled=False)  20 us
    pallas_call x2, Pallas kernels, tile_call(): pl.pallas_call(kernel, out_shape=out_shapes, in_specs=[SMEM_SPEC] * len(s...  12.6 us
    ppermute x1, waiting for transfers between devices, local(): swapped = lax.ppermute(summed, 'side', swap)  9.58 us
    all_to_all x1, starting transfers between devices, local(): same = lax.all_to_all(same, 'ring', 0, 0, tiled=False)  4.87 us
  transfers between devices with their start and end apart: 5, of which 4 were waited for; matrix products, arithmetic and copies ran while one was open for 0% of the time, Pallas kernels for 0%

profile of v6, /device:TPU:16, one launch (start us, length us, event | category | flops | bytes accessed | tf_op | source)
XLA Modules:
  0.0 177.5 jit_solution(16759768623081523023)
XLA Ops:
  0.6 0.0 copy-start
  0.6 0.8 copy-done
  1.5 0.0 copy-start.2
  1.5 0.0 copy-start.1
  1.5 1.0 shard_map.94
  2.5 20.0 %all-to-all-start = ((bf16[16,32,1024]{2,1,0:T(8,128)(2,1)}), bf16[16,32,1024]{2,1,0:T(8,128)(2,1)S(1)}, u32[]{:S(2)}, u32[]{:S(2)}) async-start(bf16[16,32,1024]{2,1,0:T(8,128)(2,1)} %shard_map.94), calls=%async_computation | async-start | bytes 2097152 | tf_op jit(solution)/shard_map/all_to_all | solution.py:238
  23.2 0.8 concatenate.3.table
  23.9 35.3 %all-to-all-done.feat_ref = bf16[16,32,1024]{2,1,0:T(8,128)(2,1)S(1)} async-done(((bf16[16,32,1024]{2,1,0:T(8,128)(2,1)}), bf16[16,32,1024]{2,1,0:T(8,128)(2,1)S(1)}, u32[]{:S(2)}, u32[]{:S(2)}) %all-to-all-start) | async-done | bytes 1048608 | tf_op jit(solution)/shard_map/all_to_all | solution.py:238
  59.3 6.2 %shard_map.95 = (f32[4,8,32,128]{3,2,1,0:T(8,128)S(1)}, f32[4,8,32,128]{3,2,1,0:T(8,128)S(1)}) custom-call(s32[387]{0:T(512)S(1)} %concatenate.3.table, bf16[192,128,128]{2,1,0:T(8,128)(2,1)} %adj_ref.3, bf16[16,32,1024]{2,1,0:T(8,128)(2,1)S(1)} %all-to-all-done.feat_ref), custom_call_target="tpu_custom_call" | custom-call | tf_op jit(solution)/shard_map/pallas_call | solution.py:200
  65.5 1.9 %collective-permute-start = (f32[4,8,32,128]{3,2,1,0:T(8,128)S(1)}, f32[4,8,32,128]{3,2,1,0:T(8,128)S(1)}, u32[]{:S(2)}, u32[]{:S(2)}) collective-permute-start(f32[4,8,32,128]{3,2,1,0:T(8,128)S(1)} %get-tuple-element.14), channel_id=1, source_target_pairs={{0,8},{8,0},{1,9},{9,1},{2,10},{10,2},{3,11},{11,3},{4,12},{12,4},... | collective-permute-start | bytes 1572872 | tf_op jit(solution)/shard_map/ppermute | solution.py:249
  67.4 1.9 %collective-permute-done = f32[4,8,32,128]{3,2,1,0:T(8,128)S(1)} collective-permute-done((f32[4,8,32,128]{3,2,1,0:T(8,128)S(1)}, f32[4,8,32,128]{3,2,1,0:T(8,128)S(1)}, u32[]{:S(2)}, u32[]{:S(2)}) %collective-permute-start) | collective-permute-done | bytes 524320 | tf_op jit(solution)/shard_map/ppermute | solution.py:249
  69.3 0.0 copy-done.2
  69.3 0.1 shard_map.96
  69.4 23.0 %all_to_all.25 = bf16[32,48,128]{2,1,0:T(8,128)(2,1)S(1)} all-to-all(bf16[32,48,128]{2,1,0:T(8,128)(2,1)S(1)} %shard_map.96), channel_id=1, replica_groups=mesh['ring'=8,'side'=2,'near'=4,'core'=2,'feat'=8] {'near','feat'}, dimensions={0} | all-to-all | bytes 786432 | tf_op jit(solution)/shard_map/all_to_all | solution.py:257
  92.4 0.0 copy-done.1
  92.4 0.9 shard_map.97
  93.3 28.7 %all_to_all.26.mine_ref = bf16[32,96,128]{2,1,0:T(8,128)(2,1)S(1)} all-to-all(bf16[32,96,128]{2,1,0:T(8,128)(2,1)S(1)} %get-tuple-element.16), channel_id=1, replica_groups=mesh['ring'=8,'side'=2,'near'=4,'core'=2,'feat'=8] {'near','feat'}, dimensions={0} | all-to-all | bytes 1572864 | tf_op jit(solution)/shard_map/all_to_all | solution.py:269
  122.0 1.9 %collective-permute-start.1 = (bf16[32,96,128]{2,1,0:T(8,128)(2,1)S(1)}, bf16[32,96,128]{2,1,0:T(8,128)(2,1)S(1)}, u32[]{:S(2)}, u32[]{:S(2)}) collective-permute-start(bf16[32,96,128]{2,1,0:T(8,128)(2,1)S(1)} %all_to_all.26.mine_ref), channel_id=1, source_target_pairs={{0,8},{8,0},{1,9},{9,1},{2,10},{10,2},{3,11},{11,3},{4,12},{12,4},... | collective-permute-start | bytes 2359304 | tf_op jit(solution)/shard_map/ppermute | solution.py:270
  123.9 2.3 %collective-permute-done.1.other_ref = bf16[32,96,128]{2,1,0:T(8,128)(2,1)S(1)} collective-permute-done((bf16[32,96,128]{2,1,0:T(8,128)(2,1)S(1)}, bf16[32,96,128]{2,1,0:T(8,128)(2,1)S(1)}, u32[]{:S(2)}, u32[]{:S(2)}) %collective-permute-start.1) | collective-permute-done | bytes 786464 | tf_op jit(solution)/shard_map/ppermute | solution.py:270
  126.2 6.4 %shard_map.98 = (bf16[8,320,128]{2,1,0:T(8,128)(2,1)S(1)}, bf16[8,256,128]{2,1,0:T(8,128)(2,1)}) custom-call(s32[387]{0:T(512)S(1)} %concatenate.3.table, bf16[192,128,128]{2,1,0:T(8,128)(2,1)} %adj_ref.3, bf16[32,96,128]{2,1,0:T(8,128)(2,1)S(1)} %all_to_all.26.mine_ref, bf16[32,96,128]{2,1,0:T(8,128)(2,1)S(1)} %collective-permute-done.1.other_ref), custom_call_target="tpu_custom_call" | custom-call | tf_op jit(solution)/shard_map/pallas_call | solution.py:200
  132.5 25.1 %all_to_all.27.pieces_ref = bf16[8,320,128]{2,1,0:T(8,128)(2,1)S(1)} all-to-all(bf16[8,320,128]{2,1,0:T(8,128)(2,1)S(1)} %get-tuple-element.18), channel_id=1, replica_groups=mesh['ring'=8,'side'=2,'near'=4,'core'=2,'feat'=8] {'ring'}, dimensions={0} | all-to-all | bytes 1310720 | tf_op jit(solution)/shard_map/all_to_all | solution.py:285
  157.6 0.1 shard_map.99.refs_2_
  157.7 4.9 %all-to-all-start.4 = ((bf16[8,256,128]{2,1,0:T(8,128)(2,1)}), bf16[8,256,128]{2,1,0:T(8,128)(2,1)S(1)}, u32[]{:S(2)}, u32[]{:S(2)}) async-start(bf16[8,256,128]{2,1,0:T(8,128)(2,1)} %get-tuple-element.19), calls=%async_computation.4 | async-start | bytes 1048576 | tf_op jit(solution)/shard_map/all_to_all | solution.py:294
  162.6 4.6 %collective-permute-start.2 = (f32[320,128]{1,0:T(8,128)S(1)}, f32[320,128]{1,0:T(8,128)S(1)}, u32[]{:S(2)}, u32[]{:S(2)}) collective-permute-start(f32[320,128]{1,0:T(8,128)S(1)} %shard_map.99.refs_2_), channel_id=1, source_target_pairs={{0,64},{64,0},{1,65},{65,1},{2,66},{66,2},{3,67},{67,3},{4,68},{68... | collective-permute-start | bytes 491528 | tf_op jit(solution)/shard_map/ppermute | solution.py:292
  167.2 9.6 %collective-permute-done.2.refs_1_ = f32[320,128]{1,0:T(8,128)S(1)} collective-permute-done((f32[320,128]{1,0:T(8,128)S(1)}, f32[320,128]{1,0:T(8,128)S(1)}, u32[]{:S(2)}, u32[]{:S(2)}) %collective-permute-start.2) | collective-permute-done | bytes 163872 | tf_op jit(solution)/shard_map/ppermute | solution.py:292
  176.7 0.0 all-to-all-done.4.refs_0_
  176.7 0.7 shard_map.100
Async XLA Ops:
  0.6 0.8 copy-start
  1.5 67.8 %copy-start.2 = (bf16[32,256]{1,0:T(8,128)(2,1)S(1)}, bf16[32,256]{1,0:T(8,128)(2,1)}, u32[]{:S(2)}) copy-start(bf16[32,256]{1,0:T(8,128)(2,1)} %weight_ref.1) | copy-start | bytes 49156
  1.5 90.9 %copy-start.1 = (bf16[128,256]{1,0:T(8,128)(2,1)S(1)}, bf16[128,256]{1,0:T(8,128)(2,1)}, u32[]{:S(2)}) copy-start(bf16[128,256]{1,0:T(8,128)(2,1)} %grad_ref.1) | copy-start | bytes 196612
  2.5 56.8 %all-to-all-start = ((bf16[16,32,1024]{2,1,0:T(8,128)(2,1)}), bf16[16,32,1024]{2,1,0:T(8,128)(2,1)S(1)}, u32[]{:S(2)}, u32[]{:S(2)}) async-start(bf16[16,32,1024]{2,1,0:T(8,128)(2,1)} %shard_map.94), calls=%async_computation | async-start | bytes 2097152 | tf_op jit(solution)/shard_map/all_to_all | solution.py:238
  65.5 3.8 %collective-permute-start = (f32[4,8,32,128]{3,2,1,0:T(8,128)S(1)}, f32[4,8,32,128]{3,2,1,0:T(8,128)S(1)}, u32[]{:S(2)}, u32[]{:S(2)}) collective-permute-start(f32[4,8,32,128]{3,2,1,0:T(8,128)S(1)} %get-tuple-element.14), channel_id=1, source_target_pairs={{0,8},{8,0},{1,9},{9,1},{2,10},{10,2},{3,11},{11,3},{4,12},{12,4},... | collective-permute-start | bytes 1572872 | tf_op jit(solution)/shard_map/ppermute | solution.py:249
  122.0 4.2 %collective-permute-start.1 = (bf16[32,96,128]{2,1,0:T(8,128)(2,1)S(1)}, bf16[32,96,128]{2,1,0:T(8,128)(2,1)S(1)}, u32[]{:S(2)}, u32[]{:S(2)}) collective-permute-start(bf16[32,96,128]{2,1,0:T(8,128)(2,1)S(1)} %all_to_all.26.mine_ref), channel_id=1, source_target_pairs={{0,8},{8,0},{1,9},{9,1},{2,10},{10,2},{3,11},{11,3},{4,12},{12,4},... | collective-permute-start | bytes 2359304 | tf_op jit(solution)/shard_map/ppermute | solution.py:270
  157.7 19.1 %all-to-all-start.4 = ((bf16[8,256,128]{2,1,0:T(8,128)(2,1)}), bf16[8,256,128]{2,1,0:T(8,128)(2,1)S(1)}, u32[]{:S(2)}, u32[]{:S(2)}) async-start(bf16[8,256,128]{2,1,0:T(8,128)(2,1)} %get-tuple-element.19), calls=%async_computation.4 | async-start | bytes 1048576 | tf_op jit(solution)/shard_map/all_to_all | solution.py:294
  162.6 14.2 %collective-permute-start.2 = (f32[320,128]{1,0:T(8,128)S(1)}, f32[320,128]{1,0:T(8,128)S(1)}, u32[]{:S(2)}, u32[]{:S(2)}) collective-permute-start(f32[320,128]{1,0:T(8,128)S(1)} %shard_map.99.refs_2_), channel_id=1, source_target_pairs={{0,64},{64,0},{1,65},{65,1},{2,66},{66,2},{3,67},{67,3},{4,68},{68... | collective-permute-start | bytes 491528 | tf_op jit(solution)/shard_map/ppermute | solution.py:292

commit v7 on v6

--- a/solution.py
+++ b/solution.py
@@ -57,16 +57,20 @@
     return lambda s: table[HEAD + s], lambda s: table[HEAD + slots + s]
 
 
-def forward_kernel(table, adj_ref, feat_ref, keep_ref, send_ref, acc_ref, *tiles):
-    core, count = table[0], table[2]
+def forward_kernel(table, adj_ref, same_ref, far_ref, keep_ref, send_ref, acc_ref, *tiles):
+    core, side, count = table[0], table[1], table[2]
     slots, extent, _ = adj_ref.shape
-    blocks = feat_ref.shape[2] // extent
+    blocks = same_ref.shape[2] // extent
     row_of, col_of = slots_of(table, slots)
 
     def source(slot):
         col = col_of(slot)
+        row_device = col // blocks
         nodes = pl.ds(pl.multiple_of((col % blocks) * extent, extent), extent)
-        return feat_ref[col // blocks, :, nodes]
+        ring = row_device // SIDES
+        return jnp.where(
+            row_device % SIDES == side, same_ref[ring, :, nodes], far_ref[ring, :, nodes]
+        )
 
     accumulate_tiles(count, source, adj_ref, *tiles, acc_ref, row_of, NT)
     near, feats = keep_ref.shape[:2]
@@ -114,13 +118,12 @@
     weight_term = (dot(high, grad_pre, NN) + dot(low, grad_pre, NN)).astype(out_ref.dtype)
     for pair in range(near):
         for feat in range(feats):
+            top = feat * width + (pair // halves) * PIECE
+            left = (pair % halves) * extent
             out_ref[pair * feats + feat, :width] = projected[feat * width : (feat + 1) * width]
-            for part in range((out_ref.shape[1] - width) // PIECE):
-                top = feat * width + (part // halves) * PIECE
-                left = (part % halves) * extent
-                out_ref[
-                    pair * feats + feat, width + part * PIECE : width + (part + 1) * PIECE
-                ] = weight_term[top : top + PIECE, left : left + extent]
+            out_ref[pair * feats + feat, width:] = weight_term[
+                top : top + PIECE, left : left + extent
+            ]
 
 
 def backward_kernel(
@@ -155,11 +158,17 @@
         far_ref[ring, blocks * width :] = weight_term.astype(far_ref.dtype)
 
 
-def reduce_kernel(pieces_ref, out_ref):
-    out_ref[...] = jnp.sum(pieces_ref[...].astype(jnp.float32), axis=0)
-
-
-def final_kernel(scale, same_ref, swapped_ref, summed_ref, grad_ref, weight_ref):
+def reduce_kernel(pieces_ref, grad_ref, weight_ref):
+    rows = grad_ref.shape[0]
+    grad_ref[...] = jnp.sum(pieces_ref[:, :rows].astype(jnp.float32), axis=0)
+    weight_term = jnp.sum(pieces_ref[:, rows:].astype(jnp.float32), axis=0)
+    for pair in range(weight_ref.shape[0]):
+        weight_ref[pair] = weight_term
+
+
+def final_kernel(
+    scale, same_ref, swapped_ref, near_ref, far_near_ref, grad_ref, weight_ref
+):
     width, nodes = grad_ref.shape
     extent = same_ref.shape[2]
     for block in range(nodes // extent):
@@ -168,12 +177,10 @@
             same_ref[:, part].astype(jnp.float32), axis=0
         )
     halves = weight_ref.shape[1] // extent
-    for part in range(width // PIECE * halves):
-        start = nodes // extent * width + part * PIECE
-        rest = slice(start, start + PIECE)
-        top, left = (part // halves) * PIECE, (part % halves) * extent
+    for pair in range(near_ref.shape[0]):
+        top, left = (pair // halves) * PIECE, (pair % halves) * extent
         weight_ref[top : top + PIECE, left : left + extent] = (
-            summed_ref[rest] + swapped_ref[rest]
+            near_ref[pair] + far_near_ref[pair]
         ) * scale
 
 
@@ -229,20 +236,24 @@
         lax.axis_index(name).astype(jnp.int32) for name in ("core", "side", "near")
     )
     table = jnp.concatenate([jnp.stack([core, side]), tile_count, tile_rows, tile_cols])
-    parts = full // extent * width // PIECE
     bf16, f32 = jnp.bfloat16, jnp.float32
 
-    own = call(
-        spread_kernel, (), (features.T,), pltpu.VMEM((rings * SIDES, width, nodes), bf16)
-    )
-    gathered = lax.all_to_all(own, ("ring", "side"), 0, 0, tiled=False)
+    def spread(value):
+        copies = call(spread_kernel, (), (value,), pltpu.VMEM((rings, width, nodes), bf16))
+        return lax.all_to_all(copies, "ring", 0, 0, tiled=False)
+
+    own = features.T
+    partner = lax.ppermute(own, "side", swap)
+    same = spread(own)
+    same, partner = lax.optimization_barrier((same, partner))
+    far = spread(partner)
 
     half = jax.ShapeDtypeStruct((near, feats, width, extent), f32)
     keep, send = tile_call(
         forward_kernel,
         (table,),
         adjacency,
-        (gathered,),
+        (same, far),
         (half, half),
         [pltpu.VMEM((CORES * owners, width, extent), f32)],
     )
@@ -260,7 +271,7 @@
         (),
         (terms.reshape(near, feats, width + PIECE, extent), grad_out),
         (
-            pltpu.VMEM((owners, width + parts * PIECE, extent), bf16),
+            pltpu.VMEM((owners, width + PIECE, extent), bf16),
             jax.ShapeDtypeStruct((extent, full), bf16),
         ),
         [pltpu.VMEM((full, full), bf16)],
@@ -274,7 +285,7 @@
         adjacency,
         (mine, other),
         (
-            pltpu.VMEM((rings, blocks * width + parts * PIECE, extent), bf16),
+            pltpu.VMEM((rings, blocks * width + PIECE, extent), bf16),
             pltpu.VMEM((rings, blocks * width, extent), bf16),
         ),
         [
@@ -283,20 +294,25 @@
         ],
     )
     far = lax.all_to_all(far, "ring", 0, 0, tiled=False)
-    summed = call(
+    summed, weight_piece = call(
         reduce_kernel,
         (),
         (far,),
-        jax.ShapeDtypeStruct((blocks * width + parts * PIECE, extent), f32),
+        (
+            jax.ShapeDtypeStruct((blocks * width, extent), f32),
+            pltpu.VMEM((near, PIECE, extent), f32),
+        ),
     )
     swapped = lax.ppermute(summed, "side", swap)
-    same, summed = lax.optimization_barrier((same, summed))
+    same, weight_piece = lax.optimization_barrier((same, weight_piece))
     same = lax.all_to_all(same, "ring", 0, 0, tiled=False)
+    weight_piece = lax.all_to_all(weight_piece, "near", 0, 0, tiled=False)
+    far_weight_piece = lax.ppermute(weight_piece, "side", swap)
     scale = 1.0 / math.sqrt(nodes * rings * SIDES * near * CORES)
     feature_grad, weight_grad = call(
         lambda *refs: final_kernel(scale, *refs),
         (),
-        (same, swapped, summed),
+        (same, swapped, weight_piece, far_weight_piece),
         (
             jax.ShapeDtypeStruct((width, nodes), f32),
             jax.ShapeDtypeStruct((width, full), f32),

time: 178 us -> 175 us (0.983)
  the two profiles are of different devices: /device:TPU:16 before, /device:TPU:18 now
where the time goes in v7:
time: 175 us; the launch traced here: 174 us
  blocking collectives  79.5 us (45%)
  starting transfers between devices  50.7 us (29%)
  waiting for transfers between devices  27.5 us (16%)
  Pallas kernels  13.4 us (8%)
    all_to_all x1, blocking collectives, local(): terms = lax.all_to_all(terms, ('near', 'feat'), 0, 0, tiled=False)  32 us
    all_to_all x1, blocking collectives, local(): far = lax.all_to_all(far, 'ring', 0, 0, tiled=False)  19.3 us
    all_to_all x1, blocking collectives, local(): mine = lax.all_to_all(outgoing, ('near', 'feat'), 0, 0, tiled=False)  19.2 us
    all_to_all x2, starting transfers between devices, spread(): return lax.all_to_all(copies, 'ring', 0, 0, tiled=False)  15.2 us
    ppermute x1, starting transfers between devices, local(): partner = lax.ppermute(own, 'side', swap)  14.5 us
    all_to_all x2, waiting for transfers between devices, spread(): return lax.all_to_all(copies, 'ring', 0, 0, tiled=False)  12.8 us
    ppermute x1, starting transfers between devices, local(): swapped = lax.ppermute(summed, 'side', swap)  10.3 us
    pallas_call x2, Pallas kernels, tile_call(): pl.pallas_call(kernel, out_shape=out_shapes, in_specs=[SMEM_SPEC] * len(s...  9.96 us
  transfers between devices with their start and end apart: 8, of which 5 were waited for; matrix products, arithmetic and copies ran while one was open for 0% of the time, Pallas kernels for 0%

profile of v7, /device:TPU:18, one launch (start us, length us, event | category | flops | bytes accessed | tf_op | source)
XLA Modules:
  0.0 174.1 jit_solution(9737124089593477752)
XLA Ops:
  0.6 0.0 copy-start
  0.6 0.8 copy-done
  1.5 0.0 copy-start.2
  1.5 0.8 shard_map.94
  2.3 0.0 copy-start.1
  2.3 8.0 %all-to-all-start = ((bf16[8,32,1024]{2,1,0:T(8,128)(2,1)}), bf16[8,32,1024]{2,1,0:T(8,128)(2,1)S(1)}, u32[]{:S(2)}, u32[]{:S(2)}) async-start(bf16[8,32,1024]{2,1,0:T(8,128)(2,1)} %shard_map.94), calls=%async_computation | async-start | bytes 1048576 | tf_op jit(solution)/shard_map/all_to_all | solution.py:243
  10.3 14.5 %collective-permute-start = (bf16[32,1024]{1,0:T(8,128)(2,1)}, bf16[32,1024]{1,0:T(8,128)(2,1)S(1)}, u32[]{:S(2)}, u32[]{:S(2)}) collective-permute-start(bf16[32,1024]{1,0:T(8,128)(2,1)} %bitcast.11), channel_id=1, source_target_pairs={{0,64},{64,0},{1,65},{65,1},{2,66},{66,2},{3,67},{67,3},{4,68},{68... | collective-permute-start | bytes 196616 | tf_op jit(solution)/shard_map/ppermute | solution.py:246
  24.9 2.8 %collective-permute-done.value_ref = bf16[32,1024]{1,0:T(8,128)(2,1)S(1)} collective-permute-done((bf16[32,1024]{1,0:T(8,128)(2,1)}, bf16[32,1024]{1,0:T(8,128)(2,1)S(1)}, u32[]{:S(2)}, u32[]{:S(2)}) %collective-permute-start) | collective-permute-done | bytes 65568 | tf_op jit(solution)/shard_map/ppermute | solution.py:246
  27.7 0.0 all-to-all-done.same_ref
  27.7 0.8 shard_map.95
  28.5 7.2 %all-to-all-start.1 = ((bf16[8,32,1024]{2,1,0:T(8,128)(2,1)}), bf16[8,32,1024]{2,1,0:T(8,128)(2,1)S(1)}, u32[]{:S(2)}, u32[]{:S(2)}) async-start(bf16[8,32,1024]{2,1,0:T(8,128)(2,1)} %shard_map.95), calls=%async_computation.1 | async-start | bytes 1048576 | tf_op jit(solution)/shard_map/all_to_all | solution.py:243
  36.4 0.8 concatenate.3.table
  37.2 12.8 %all-to-all-done.1.far_ref = bf16[8,32,1024]{2,1,0:T(8,128)(2,1)S(1)} async-done(((bf16[8,32,1024]{2,1,0:T(8,128)(2,1)}), bf16[8,32,1024]{2,1,0:T(8,128)(2,1)S(1)}, u32[]{:S(2)}, u32[]{:S(2)}) %all-to-all-start.1) | async-done | bytes 524320 | tf_op jit(solution)/shard_map/all_to_all | solution.py:243
  50.0 4.8 %shard_map.96 = (f32[4,8,32,128]{3,2,1,0:T(8,128)S(1)}, f32[4,8,32,128]{3,2,1,0:T(8,128)S(1)}) custom-call(s32[387]{0:T(512)S(1)} %concatenate.3.table, bf16[192,128,128]{2,1,0:T(8,128)(2,1)} %adj_ref.3, bf16[8,32,1024]{2,1,0:T(8,128)(2,1)S(1)} %all-to-all-done.same_ref, bf16[8,32,1024]{2,1,0:T(8,128)(2,1)S(1)} %all-to-all-done.1.far_ref), custom_call_target="tpu_custom_call" | custom-call | tf_op jit(solution)/shard_map/pallas_call | solution.py:207
  54.8 1.9 %collective-permute-start.1 = (f32[4,8,32,128]{3,2,1,0:T(8,128)S(1)}, f32[4,8,32,128]{3,2,1,0:T(8,128)S(1)}, u32[]{:S(2)}, u32[]{:S(2)}) collective-permute-start(f32[4,8,32,128]{3,2,1,0:T(8,128)S(1)} %get-tuple-element.20), channel_id=1, source_target_pairs={{0,8},{8,0},{1,9},{9,1},{2,10},{10,2},{3,11},{11,3},{4,12},{12,4},... | collective-permute-start | bytes 1572872 | tf_op jit(solution)/shard_map/ppermute | solution.py:260
  56.7 1.9 %collective-permute-done.1 = f32[4,8,32,128]{3,2,1,0:T(8,128)S(1)} collective-permute-done((f32[4,8,32,128]{3,2,1,0:T(8,128)S(1)}, f32[4,8,32,128]{3,2,1,0:T(8,128)S(1)}, u32[]{:S(2)}, u32[]{:S(2)}) %collective-permute-start.1) | collective-permute-done | bytes 524320 | tf_op jit(solution)/shard_map/ppermute | solution.py:260
  58.6 0.0 copy-done.2
  58.6 0.1 shard_map.97
  58.6 32.0 %all_to_all.35 = bf16[32,48,128]{2,1,0:T(8,128)(2,1)S(1)} all-to-all(bf16[32,48,128]{2,1,0:T(8,128)(2,1)S(1)} %shard_map.97), channel_id=1, replica_groups=mesh['ring'=8,'side'=2,'near'=4,'core'=2,'feat'=8] {'near','feat'}, dimensions={0} | all-to-all | bytes 786432 | tf_op jit(solution)/shard_map/all_to_all | solution.py:268
  90.6 0.0 copy-done.1
  90.6 0.9 shard_map.98
  91.6 19.2 %all_to_all.36.mine_ref = bf16[32,48,128]{2,1,0:T(8,128)(2,1)S(1)} all-to-all(bf16[32,48,128]{2,1,0:T(8,128)(2,1)S(1)} %get-tuple-element.22), channel_id=1, replica_groups=mesh['ring'=8,'side'=2,'near'=4,'core'=2,'feat'=8] {'near','feat'}, dimensions={0} | all-to-all | bytes 786432 | tf_op jit(solution)/shard_map/all_to_all | solution.py:280
  110.8 1.9 %collective-permute-start.2 = (bf16[32,48,128]{2,1,0:T(8,128)(2,1)S(1)}, bf16[32,48,128]{2,1,0:T(8,128)(2,1)S(1)}, u32[]{:S(2)}, u32[]{:S(2)}) collective-permute-start(bf16[32,48,128]{2,1,0:T(8,128)(2,1)S(1)} %all_to_all.36.mine_ref), channel_id=1, source_target_pairs={{0,8},{8,0},{1,9},{9,1},{2,10},{10,2},{3,11},{11,3},{4,12},{12,4},... | collective-permute-start | bytes 1179656 | tf_op jit(solution)/shard_map/ppermute | solution.py:281
  112.7 1.7 collective-permute-done.2.other_ref
  114.4 5.2 %shard_map.99 = (bf16[8,272,128]{2,1,0:T(8,128)(2,1)S(1)}, bf16[8,256,128]{2,1,0:T(8,128)(2,1)}) custom-call(s32[387]{0:T(512)S(1)} %concatenate.3.table, bf16[192,128,128]{2,1,0:T(8,128)(2,1)} %adj_ref.3, bf16[32,48,128]{2,1,0:T(8,128)(2,1)S(1)} %all_to_all.36.mine_ref, bf16[32,48,128]{2,1,0:T(8,128)(2,1)S(1)} %collective-permute-done.2.other_ref), custom_call_target="tpu_custom_call" | custom-call | tf_op jit(solution)/shard_map/pallas_call | solution.py:207
  119.6 19.3 %all_to_all.37.pieces_ref = bf16[8,272,128]{2,1,0:T(8,128)(2,1)S(1)} all-to-all(bf16[8,272,128]{2,1,0:T(8,128)(2,1)S(1)} %get-tuple-element.24), channel_id=1, replica_groups=mesh['ring'=8,'side'=2,'near'=4,'core'=2,'feat'=8] {'ring'}, dimensions={0} | all-to-all | bytes 1114112 | tf_op jit(solution)/shard_map/all_to_all | solution.py:296
  138.9 0.1 shard_map.100
  139.0 8.9 %all_to_all.38.refs_2_ = f32[4,16,128]{2,1,0:T(8,128)S(1)} all-to-all(f32[4,16,128]{2,1,0:T(8,128)S(1)} %get-tuple-element.28), channel_id=1, replica_groups=mesh['ring'=8,'side'=2,'near'=4,'core'=2,'feat'=8] {'near'}, dimensions={0} | all-to-all | bytes 65536 | tf_op jit(solution)/shard_map/all_to_all | solution.py:309
  147.9 4.9 %all-to-all-start.5 = ((bf16[8,256,128]{2,1,0:T(8,128)(2,1)}), bf16[8,256,128]{2,1,0:T(8,128)(2,1)S(1)}, u32[]{:S(2)}, u32[]{:S(2)}) async-start(bf16[8,256,128]{2,1,0:T(8,128)(2,1)} %get-tuple-element.26), calls=%async_computation.5 | async-start | bytes 1048576 | tf_op jit(solution)/shard_map/all_to_all | solution.py:308
  152.8 10.3 %collective-permute-start.3 = (f32[256,128]{1,0:T(8,128)S(1)}, f32[256,128]{1,0:T(8,128)S(1)}, u32[]{:S(2)}, u32[]{:S(2)}) collective-permute-start(f32[256,128]{1,0:T(8,128)S(1)} %get-tuple-element.27), channel_id=1, source_target_pairs={{0,64},{64,0},{1,65},{65,1},{2,66},{66,2},{3,67},{67,3},{4,68},{68... | collective-permute-start | bytes 393224 | tf_op jit(solution)/shard_map/ppermute | solution.py:306
  163.1 1.9 %collective-permute-start.4 = (f32[4,16,128]{2,1,0:T(8,128)S(1)}, f32[4,16,128]{2,1,0:T(8,128)S(1)}, u32[]{:S(2)}, u32[]{:S(2)}) collective-permute-start(f32[4,16,128]{2,1,0:T(8,128)S(1)} %all_to_all.38.refs_2_), channel_id=1, source_target_pairs={{0,64},{64,0},{1,65},{65,1},{2,66},{66,2},{3,67},{67,3},{4,68},{68... | collective-permute-start | bytes 98312 | tf_op jit(solution)/shard_map/ppermute | solution.py:310
  165.0 8.3 %collective-permute-done.4.refs_3_ = f32[4,16,128]{2,1,0:T(8,128)S(1)} collective-permute-done((f32[4,16,128]{2,1,0:T(8,128)S(1)}, f32[4,16,128]{2,1,0:T(8,128)S(1)}, u32[]{:S(2)}, u32[]{:S(2)}) %collective-permute-start.4) | collective-permute-done | bytes 32800 | tf_op jit(solution)/shard_map/ppermute | solution.py:310
  173.4 0.0 collective-permute-done.3.refs_1_
  173.4 0.0 all-to-all-done.5.refs_0_
  173.4 0.7 shard_map.101
Async XLA Ops:
  0.6 0.8 copy-start
  1.5 57.1 %copy-start.2 = (bf16[32,256]{1,0:T(8,128)(2,1)S(1)}, bf16[32,256]{1,0:T(8,128)(2,1)}, u32[]{:S(2)}) copy-start(bf16[32,256]{1,0:T(8,128)(2,1)} %weight_ref.1) | copy-start | bytes 49156
  2.3 88.3 %copy-start.1 = (bf16[128,256]{1,0:T(8,128)(2,1)S(1)}, bf16[128,256]{1,0:T(8,128)(2,1)}, u32[]{:S(2)}) copy-start(bf16[128,256]{1,0:T(8,128)(2,1)} %grad_ref.1) | copy-start | bytes 196612
  2.3 25.4 %all-to-all-start = ((bf16[8,32,1024]{2,1,0:T(8,128)(2,1)}), bf16[8,32,1024]{2,1,0:T(8,128)(2,1)S(1)}, u32[]{:S(2)}, u32[]{:S(2)}) async-start(bf16[8,32,1024]{2,1,0:T(8,128)(2,1)} %shard_map.94), calls=%async_computation | async-start | bytes 1048576 | tf_op jit(solution)/shard_map/all_to_all | solution.py:243
  10.3 17.4 %collective-permute-start = (bf16[32,1024]{1,0:T(8,128)(2,1)}, bf16[32,1024]{1,0:T(8,128)(2,1)S(1)}, u32[]{:S(2)}, u32[]{:S(2)}) collective-permute-start(bf16[32,1024]{1,0:T(8,128)(2,1)} %bitcast.11), channel_id=1, source_target_pairs={{0,64},{64,0},{1,65},{65,1},{2,66},{66,2},{3,67},{67,3},{4,68},{68... | collective-permute-start | bytes 196616 | tf_op jit(solution)/shard_map/ppermute | solution.py:246
  28.5 21.5 %all-to-all-start.1 = ((bf16[8,32,1024]{2,1,0:T(8,128)(2,1)}), bf16[8,32,1024]{2,1,0:T(8,128)(2,1)S(1)}, u32[]{:S(2)}, u32[]{:S(2)}) async-start(bf16[8,32,1024]{2,1,0:T(8,128)(2,1)} %shard_map.95), calls=%async_computation.1 | async-start | bytes 1048576 | tf_op jit(solution)/shard_map/all_to_all | solution.py:243
  54.8 3.8 %collective-permute-start.1 = (f32[4,8,32,128]{3,2,1,0:T(8,128)S(1)}, f32[4,8,32,128]{3,2,1,0:T(8,128)S(1)}, u32[]{:S(2)}, u32[]{:S(2)}) collective-permute-start(f32[4,8,32,128]{3,2,1,0:T(8,128)S(1)} %get-tuple-element.20), channel_id=1, source_target_pairs={{0,8},{8,0},{1,9},{9,1},{2,10},{10,2},{3,11},{11,3},{4,12},{12,4},... | collective-permute-start | bytes 1572872 | tf_op jit(solution)/shard_map/ppermute | solution.py:260
  110.8 3.6 %collective-permute-start.2 = (bf16[32,48,128]{2,1,0:T(8,128)(2,1)S(1)}, bf16[32,48,128]{2,1,0:T(8,128)(2,1)S(1)}, u32[]{:S(2)}, u32[]{:S(2)}) collective-permute-start(bf16[32,48,128]{2,1,0:T(8,128)(2,1)S(1)} %all_to_all.36.mine_ref), channel_id=1, source_target_pairs={{0,8},{8,0},{1,9},{9,1},{2,10},{10,2},{3,11},{11,3},{4,12},{12,4},... | collective-permute-start | bytes 1179656 | tf_op jit(solution)/shard_map/ppermute | solution.py:281
  147.9 25.5 %all-to-all-start.5 = ((bf16[8,256,128]{2,1,0:T(8,128)(2,1)}), bf16[8,256,128]{2,1,0:T(8,128)(2,1)S(1)}, u32[]{:S(2)}, u32[]{:S(2)}) async-start(bf16[8,256,128]{2,1,0:T(8,128)(2,1)} %get-tuple-element.26), calls=%async_computation.5 | async-start | bytes 1048576 | tf_op jit(solution)/shard_map/all_to_all | solution.py:308
  152.8 20.6 %collective-permute-start.3 = (f32[256,128]{1,0:T(8,128)S(1)}, f32[256,128]{1,0:T(8,128)S(1)}, u32[]{:S(2)}, u32[]{:S(2)}) collective-permute-start(f32[256,128]{1,0:T(8,128)S(1)} %get-tuple-element.27), channel_id=1, source_target_pairs={{0,64},{64,0},{1,65},{65,1},{2,66},{66,2},{3,67},{67,3},{4,68},{68... | collective-permute-start | bytes 393224 | tf_op jit(solution)/shard_map/ppermute | solution.py:306
  163.1 10.3 %collective-permute-start.4 = (f32[4,16,128]{2,1,0:T(8,128)S(1)}, f32[4,16,128]{2,1,0:T(8,128)S(1)}, u32[]{:S(2)}, u32[]{:S(2)}) collective-permute-start(f32[4,16,128]{2,1,0:T(8,128)S(1)} %all_to_all.38.refs_2_), channel_id=1, source_target_pairs={{0,64},{64,0},{1,65},{65,1},{2,66},{66,2},{3,67},{67,3},{4,68},{68... | collective-permute-start | bytes 98312 | tf_op jit(solution)/shard_map/ppermute | solution.py:310

commit v8 on v5

--- a/solution.py
+++ b/solution.py
@@ -7,11 +7,11 @@
 from jax.experimental.pallas import tpu as pltpu
 from jax.sharding import PartitionSpec as P
 
-UNROLL = 8
-CHUNK = 16
+CHUNK = 32
 PIECE = 16
 CORES = 2
 SIDES = 2
+HEAD = 3
 VMEM_LIMIT = 24 * 1024 * 1024
 NT = (((1,), (1,)), ((), ()))
 NN = (((1,), (0,)), ((), ()))
@@ -23,7 +23,7 @@
 
 
 def accumulate_tiles(count, source, adj_ref, tiles_ref, done, acc_ref, target_of, dims):
-    chunks = adj_ref.shape[0] // CHUNK
+    chunks, extent = adj_ref.shape[0] // CHUNK, adj_ref.shape[1]
 
     def load(chunk):
         part = pl.ds(chunk * CHUNK, CHUNK)
@@ -33,34 +33,44 @@
         load(chunk).start()
     acc_ref[...] = jnp.zeros_like(acc_ref)
 
+    def product(slot):
+        one, two = source(slot), source(slot + 1)
+        zero = jnp.zeros_like(one)
+        left = jnp.concatenate(
+            [jnp.concatenate([one, zero], axis=1), jnp.concatenate([zero, two], axis=1)], axis=0
+        )
+        if dims is NN:
+            right = tiles_ref[pl.ds(slot, 2)].reshape(2 * extent, extent)
+        else:
+            right = jnp.concatenate([tiles_ref[slot], tiles_ref[slot + 1]], axis=1)
+        both = dot(left, right, dims)
+        return both[: one.shape[0]], both[one.shape[0] :]
+
     @pl.loop(0, chunks)
     def _(chunk):
         load(chunk).wait()
-
-        @pl.loop(0, CHUNK // UNROLL)
-        def _(group):
-            first = chunk * CHUNK + group * UNROLL
-
-            @pl.when(first < count)
-            def _():
-                terms = []
-                for u in range(UNROLL):
-                    term = dot(source(first + u), tiles_ref[first + u], dims)
-                    terms.append(jnp.where(first + u < count, term, 0.0))
-                for u in range(UNROLL):
-                    target = target_of(first + u)
-                    acc_ref[target] += terms[u]
-
-
-def forward_kernel(
-    place, rows, cols, count, adj_ref, same_ref, far_ref, keep_ref, send_ref, acc_ref, *tiles
-):
-    core, side = place[0], place[1]
-    extent = adj_ref.shape[1]
+        first = chunk * CHUNK
+
+        @pl.when(first < count)
+        def _():
+            terms = [term for u in range(0, CHUNK, 2) for term in product(first + u)]
+            for u, term in enumerate(terms):
+                target = target_of(first + u)
+                acc_ref[target] += jnp.where(first + u < count, term, 0.0)
+
+
+def slots_of(table, slots):
+    return lambda s: table[HEAD + s], lambda s: table[HEAD + slots + s]
+
+
+def forward_kernel(table, adj_ref, same_ref, far_ref, keep_ref, send_ref, acc_ref, *tiles):
+    core, side, count = table[0], table[1], table[2]
+    slots, extent, _ = adj_ref.shape
     blocks = same_ref.shape[2] // extent
+    row_of, col_of = slots_of(table, slots)
 
     def source(slot):
-        col = cols[slot]
+        col = col_of(slot)
         row_device = col // blocks
         nodes = pl.ds(pl.multiple_of((col % blocks) * extent, extent), extent)
         ring = row_device // SIDES
@@ -68,7 +78,7 @@
             row_device % SIDES == side, same_ref[ring, :, nodes], far_ref[ring, :, nodes]
         )
 
-    accumulate_tiles(count[0], source, adj_ref, *tiles, acc_ref, lambda s: rows[s], NT)
+    accumulate_tiles(count, source, adj_ref, *tiles, acc_ref, row_of, NT)
     near, feats = keep_ref.shape[:2]
     for pair in range(near):
         keep_ref[pair] = acc_ref[pl.ds((pair * CORES + core) * feats, feats)]
@@ -123,12 +133,13 @@
 
 
 def backward_kernel(
-    place, rows, cols, count, adj_ref, mine_ref, other_ref, far_ref, same_ref, proj_ref, acc_ref, *tiles
+    table, adj_ref, mine_ref, other_ref, out_ref, proj_ref, acc_ref, *tiles
 ):
-    core, side = place[0], place[1]
-    rings = far_ref.shape[0]
+    core, count = table[0], table[2]
+    row_of, col_of = slots_of(table, adj_ref.shape[0])
+    rows = out_ref.shape[0]
     width = acc_ref.shape[1]
-    blocks = acc_ref.shape[0] // (rings * SIDES)
+    blocks = acc_ref.shape[0] // rows
     feats = proj_ref.shape[2]
     for pair in range(proj_ref.shape[0]):
         part = slice(pair * feats, (pair + 1) * feats)
@@ -136,37 +147,30 @@
         proj_ref[pair, 1 - core] = other_ref[part, :width]
 
     def source(slot):
-        row = rows[slot]
+        row = row_of(slot)
         return proj_ref[row // (CORES * feats), (row // feats) % CORES, row % feats]
 
-    accumulate_tiles(count[0], source, adj_ref, *tiles, acc_ref, lambda s: cols[s], NN)
+    accumulate_tiles(count, source, adj_ref, *tiles, acc_ref, col_of, NN)
     weight_term = jnp.sum(mine_ref[:, width:].astype(jnp.float32), axis=0) + jnp.sum(
         other_ref[:, width:].astype(jnp.float32), axis=0
     )
-    for ring in range(rings):
-        for out_ref, out_side in ((far_ref, 1 - side), (same_ref, side)):
-            start = (ring * SIDES + out_side) * blocks
-            for block in range(blocks):
-                out_ref[ring, block * width : (block + 1) * width] = acc_ref[start + block].astype(
-                    out_ref.dtype
-                )
-        far_ref[ring, blocks * width :] = weight_term.astype(far_ref.dtype)
-
-
-def reduce_kernel(pieces_ref, out_ref):
-    out_ref[...] = jnp.sum(pieces_ref[...].astype(jnp.float32), axis=0)
-
-
-def final_kernel(scale, same_ref, swapped_ref, summed_ref, grad_ref, weight_ref):
+    for row in range(rows):
+        for block in range(blocks):
+            out_ref[row, block * width : (block + 1) * width] = acc_ref[
+                row * blocks + block
+            ].astype(out_ref.dtype)
+        out_ref[row, blocks * width :] = weight_term.astype(out_ref.dtype)
+
+
+def final_kernel(scale, pieces_ref, grad_ref, weight_ref):
     width, nodes = grad_ref.shape
-    extent = same_ref.shape[2]
+    extent = pieces_ref.shape[2]
     for block in range(nodes // extent):
-        part = slice(block * width, (block + 1) * width)
-        grad_ref[:, block * extent : (block + 1) * extent] = swapped_ref[part] + jnp.sum(
-            same_ref[:, part].astype(jnp.float32), axis=0
+        grad_ref[:, block * extent : (block + 1) * extent] = jnp.sum(
+            pieces_ref[:, block * width : (block + 1) * width].astype(jnp.float32), axis=0
         )
-    rest = slice(nodes // extent * width, None)
-    weight_term = (summed_ref[rest] + swapped_ref[rest]) * scale
+    rest = pieces_ref[:, nodes // extent * width :].astype(jnp.float32)
+    weight_term = jnp.sum(rest, axis=0) * scale
     for pair in range(weight_ref.shape[0]):
         weight_ref[pair] = weight_term
 
@@ -222,7 +226,7 @@
     core, side, near_index = (
         lax.axis_index(name).astype(jnp.int32) for name in ("core", "side", "near")
     )
-    scalars = (jnp.stack([core, side]), tile_rows, tile_cols, tile_count)
+    table = jnp.concatenate([jnp.stack([core, side]), tile_count, tile_rows, tile_cols])
     bf16, f32 = jnp.bfloat16, jnp.float32
 
     def spread(value):
@@ -238,7 +242,7 @@
     half = jax.ShapeDtypeStruct((near, feats, width, extent), f32)
     keep, send = tile_call(
         forward_kernel,
-        scalars,
+        (table,),
         adjacency,
         (same, far),
         (half, half),
@@ -266,35 +270,23 @@
 
     mine = lax.all_to_all(outgoing, ("near", "feat"), 0, 0, tiled=False)
     other = lax.ppermute(mine, "core", swap)
-    far, same = tile_call(
+    pieces = tile_call(
         backward_kernel,
-        scalars,
+        (table,),
         adjacency,
         (mine, other),
-        (
-            pltpu.VMEM((rings, blocks * width + PIECE, extent), bf16),
-            pltpu.VMEM((rings, blocks * width, extent), bf16),
-        ),
+        pltpu.VMEM((rings * SIDES, blocks * width + PIECE, extent), bf16),
         [
             pltpu.VMEM((near, CORES, feats, width, extent), bf16),
             pltpu.VMEM((rings * SIDES * blocks, width, extent), f32),
         ],
     )
-    far = lax.all_to_all(far, "ring", 0, 0, tiled=False)
-    summed = call(
-        reduce_kernel,
-        (),
-        (far,),
-        jax.ShapeDtypeStruct((blocks * width + PIECE, extent), f32),
-    )
-    swapped = lax.ppermute(summed, "side", swap)
-    same, summed = lax.optimization_barrier((same, summed))
-    same = lax.all_to_all(same, "ring", 0, 0, tiled=False)
+    pieces = lax.all_to_all(pieces, ("ring", "side"), 0, 0, tiled=False)
     scale = 1.0 / math.sqrt(nodes * rings * SIDES * near * CORES)
     feature_grad, weight_piece = call(
         lambda *refs: final_kernel(scale, *refs),
         (),
-        (same, swapped, summed),
+        (pieces,),
         (
             jax.ShapeDtypeStruct((width, nodes), f32),
             pltpu.VMEM((near, PIECE, extent), f32),

time: 173 us -> 172 us (level)
  blocking collectives: 75 us -> 96.1 us
  starting transfers between devices: 55.8 us -> 45.2 us
  waiting for transfers between devices: 23.8 us -> 15.4 us
  Pallas kernels: 13.4 us -> 10.5 us
    all_to_all x1, blocking collectives: 21.3 us -> 44.3 us  [local(): pieces = lax.all_to_all(pieces, ('ring', 'side'), 0, 0, tiled=False)]
    ppermute x1 -> x0, starting transfers between devices: 9.97 us -> none  [local(): swapped = lax.ppermute(summed, 'side', swap)]
    all_to_all x1 -> x0, waiting for transfers between devices: 5.54 us -> none  [local(): same = lax.all_to_all(same, 'ring', 0, 0, tiled=False)]
    all_to_all x1 -> x0, starting transfers between devices: 3.5 us -> none  [local(): same = lax.all_to_all(same, 'ring', 0, 0, tiled=False)]
    pallas_call x2, Pallas kernels: 9.95 us -> 7.03 us  [tile_call(): pl.pallas_call(kernel, out_shape=out_shapes, in_specs=[SMEM_SPEC] * len(s...]
    ppermute x1, starting transfers between devices: 7.97 us -> 10.8 us  [local(): received = lax.ppermute(send, 'core', swap)]
    ppermute x1 -> x0, waiting for transfers between devices: 2.43 us -> none  [local(): swapped = lax.ppermute(summed, 'side', swap)]
    all_to_all x1, blocking collectives: 26 us -> 23.8 us  [local(): terms = lax.all_to_all(terms, ('near', 'feat'), 0, 0, tiled=False)]
  transfers between devices with their start and end apart: 7 -> 5, of which waited for: 6 -> 4; matrix products, arithmetic and copies ran while one was open for 0% -> 0% of each run, Pallas kernels for 0% -> 0%
where the time goes in v8:
time: 172 us; the launch traced here: 170 us
  blocking collectives  96.1 us (56%)
  starting transfers between devices  45.2 us (26%)
  waiting for transfers between devices  15.4 us (9%)
  Pallas kernels  10.5 us (6%)
    all_to_all x1, blocking collectives, local(): pieces = lax.all_to_all(pieces, ('ring', 'side'), 0, 0, tiled=False)  44.3 us
    all_to_all x1, blocking collectives, local(): terms = lax.all_to_all(terms, ('near', 'feat'), 0, 0, tiled=False)  23.8 us
    all_to_all x1, blocking collectives, local(): mine = lax.all_to_all(outgoing, ('near', 'feat'), 0, 0, tiled=False)  19 us
    all_to_all x2, starting transfers between devices, spread(): return lax.all_to_all(copies, 'ring', 0, 0, tiled=False)  15.2 us
    ppermute x1, starting transfers between devices, local(): partner = lax.ppermute(own, 'side', swap)  14.3 us
    all_to_all x2, waiting for transfers between devices, spread(): return lax.all_to_all(copies, 'ring', 0, 0, tiled=False)  10.9 us
    ppermute x1, starting transfers between devices, local(): received = lax.ppermute(send, 'core', swap)  10.8 us
    all_to_all x1, blocking collectives, local(): weight_grad = lax.all_to_all(weight_piece, 'near', 0, 0, tiled=False)  9.03 us
  transfers between devices with their start and end apart: 5, of which 4 were waited for; matrix products, arithmetic and copies ran while one was open for 0% of the time, Pallas kernels for 0%

profile of v8, /device:TPU:1, one launch (start us, length us, event | category | flops | bytes accessed | tf_op | source)
XLA Modules:
  0.0 170.1 jit_solution(4875742356674163383)
XLA Ops:
  0.6 0.0 copy-start
  0.6 0.8 copy-done
  1.5 0.0 copy-start.1
  1.5 0.8 shard_map.94
  2.3 0.0 copy-start.4
  2.3 0.0 copy-start.5
  2.3 8.2 %all-to-all-start = ((bf16[8,32,1024]{2,1,0:T(8,128)(2,1)}), bf16[8,32,1024]{2,1,0:T(8,128)(2,1)S(1)}, u32[]{:S(2)}, u32[]{:S(2)}) async-start(bf16[8,32,1024]{2,1,0:T(8,128)(2,1)} %shard_map.94), calls=%async_computation | async-start | bytes 1048576 | tf_op jit(solution)/shard_map/all_to_all | solution.py:234
  10.5 0.0 copy-done.1
  10.5 14.3 %collective-permute-start = (bf16[32,1024]{1,0:T(8,128)(2,1)S(1)}, bf16[32,1024]{1,0:T(8,128)(2,1)S(1)}, u32[]{:S(2)}, u32[]{:S(2)}) collective-permute-start(bf16[32,1024]{1,0:T(8,128)(2,1)S(1)} %bitcast.20), channel_id=1, source_target_pairs={{0,64},{64,0},{1,65},{65,1},{2,66},{66,2},{3,67},{67,3},{4,68},{68... | collective-permute-start | bytes 196616 | tf_op jit(solution)/shard_map/ppermute | solution.py:237
  24.8 1.6 collective-permute-done.value_ref
  26.5 0.0 all-to-all-done.same_ref
  26.5 0.8 shard_map.95
  27.3 6.9 %all-to-all-start.1 = ((bf16[8,32,1024]{2,1,0:T(8,128)(2,1)}), bf16[8,32,1024]{2,1,0:T(8,128)(2,1)S(1)}, u32[]{:S(2)}, u32[]{:S(2)}) async-start(bf16[8,32,1024]{2,1,0:T(8,128)(2,1)} %shard_map.95), calls=%async_computation.1 | async-start | bytes 1048576 | tf_op jit(solution)/shard_map/all_to_all | solution.py:234
  34.9 0.0 copy-done.4
  34.9 0.0 copy-done.5
  34.9 0.1 concatenate.3.table
  35.0 0.0 copy-start.3
  35.0 10.9 %all-to-all-done.1.far_ref = bf16[8,32,1024]{2,1,0:T(8,128)(2,1)S(1)} async-done(((bf16[8,32,1024]{2,1,0:T(8,128)(2,1)}), bf16[8,32,1024]{2,1,0:T(8,128)(2,1)S(1)}, u32[]{:S(2)}, u32[]{:S(2)}) %all-to-all-start.1) | async-done | bytes 524320 | tf_op jit(solution)/shard_map/all_to_all | solution.py:234
  45.9 3.5 %shard_map.96 = (f32[4,8,32,128]{3,2,1,0:T(8,128)S(1)}, f32[4,8,32,128]{3,2,1,0:T(8,128)S(1)}) custom-call(s32[387]{0:T(512)S(1)} %concatenate.3.table, bf16[192,128,128]{2,1,0:T(8,128)(2,1)} %adj_ref.3, bf16[8,32,1024]{2,1,0:T(8,128)(2,1)S(1)} %all-to-all-done.same_ref, bf16[8,32,1024]{2,1,0:T(8,128)(2,1)S(1)} %all-to-all-done.1.far_ref), custom_call_target="tpu_custom_call" | custom-call | tf_op jit(solution)/shard_map/pallas_call | solution.py:198
  49.4 10.8 %collective-permute-start.1 = (f32[4,8,32,128]{3,2,1,0:T(8,128)S(1)}, f32[4,8,32,128]{3,2,1,0:T(8,128)S(1)}, u32[]{:S(2)}, u32[]{:S(2)}) collective-permute-start(f32[4,8,32,128]{3,2,1,0:T(8,128)S(1)} %get-tuple-element.14), channel_id=1, source_target_pairs={{0,8},{8,0},{1,9},{9,1},{2,10},{10,2},{3,11},{11,3},{4,12},{12,4},... | collective-permute-start | bytes 1572872 | tf_op jit(solution)/shard_map/ppermute | solution.py:251
  60.2 1.5 collective-permute-done.1
  61.7 0.0 copy-done.3
  61.7 0.0 copy-start.2
  61.7 0.1 shard_map.97
  61.8 23.8 %all_to_all.30 = bf16[32,48,128]{2,1,0:T(8,128)(2,1)S(1)} all-to-all(bf16[32,48,128]{2,1,0:T(8,128)(2,1)S(1)} %shard_map.97), channel_id=1, replica_groups=mesh['ring'=8,'side'=2,'near'=4,'core'=2,'feat'=8] {'near','feat'}, dimensions={0} | all-to-all | bytes 786432 | tf_op jit(solution)/shard_map/all_to_all | solution.py:259
  85.6 0.0 copy-done.2
  85.6 0.9 shard_map.98
  86.5 19.0 %all_to_all.31.mine_ref = bf16[32,48,128]{2,1,0:T(8,128)(2,1)S(1)} all-to-all(bf16[32,48,128]{2,1,0:T(8,128)(2,1)S(1)} %get-tuple-element.16), channel_id=1, replica_groups=mesh['ring'=8,'side'=2,'near'=4,'core'=2,'feat'=8] {'near','feat'}, dimensions={0} | all-to-all | bytes 786432 | tf_op jit(solution)/shard_map/all_to_all | solution.py:271
  105.6 5.0 %collective-permute-start.2 = (bf16[32,48,128]{2,1,0:T(8,128)(2,1)S(1)}, bf16[32,48,128]{2,1,0:T(8,128)(2,1)S(1)}, u32[]{:S(2)}, u32[]{:S(2)}) collective-permute-start(bf16[32,48,128]{2,1,0:T(8,128)(2,1)S(1)} %all_to_all.31.mine_ref), channel_id=1, source_target_pairs={{0,8},{8,0},{1,9},{9,1},{2,10},{10,2},{3,11},{11,3},{4,12},{12,4},... | collective-permute-start | bytes 1179656 | tf_op jit(solution)/shard_map/ppermute | solution.py:272
  110.5 1.3 collective-permute-done.2.other_ref
  111.9 3.5 %shard_map.99 = bf16[16,272,128]{2,1,0:T(8,128)(2,1)S(1)} custom-call(s32[387]{0:T(512)S(1)} %concatenate.3.table, bf16[192,128,128]{2,1,0:T(8,128)(2,1)} %adj_ref.3, bf16[32,48,128]{2,1,0:T(8,128)(2,1)S(1)} %all_to_all.31.mine_ref, bf16[32,48,128]{2,1,0:T(8,128)(2,1)S(1)} %collective-permute-done.2.other_ref), custom_call_target="tpu_custom_call" | custom-call | tf_op jit(solution)/shard_map/pallas_call | solution.py:198
  115.4 44.3 %all_to_all.32.refs_0_ = bf16[16,272,128]{2,1,0:T(8,128)(2,1)S(1)} all-to-all(bf16[16,272,128]{2,1,0:T(8,128)(2,1)S(1)} %shard_map.99), channel_id=1, replica_groups=mesh['ring'=8,'side'=2,'near'=4,'core'=2,'feat'=8] {'ring','side'}, dimensions={0} | all-to-all | bytes 2228224 | tf_op jit(solution)/shard_map/all_to_all | solution.py:284
  159.7 0.8 shard_map.100
  160.5 9.0 %all_to_all.33 = f32[4,16,128]{2,1,0:T(8,128)S(1)} all-to-all(f32[4,16,128]{2,1,0:T(8,128)S(1)} %get-tuple-element.17), channel_id=1, replica_groups=mesh['ring'=8,'side'=2,'near'=4,'core'=2,'feat'=8] {'near'}, dimensions={0} | all-to-all | bytes 65536 | tf_op jit(solution)/shard_map/all_to_all | solution.py:295
  169.5 0.6 copy.13
  (1 shorter events, 0.0 us)
Async XLA Ops:
  0.6 0.8 copy-start
  1.5 9.1 %copy-start.1 = (bf16[1024,32]{0,1:T(8,128)(2,1)S(1)}, bf16[1024,32]{0,1:T(8,128)(2,1)}, u32[]{:S(2)}) copy-start(bf16[1024,32]{0,1:T(8,128)(2,1)} %param.7) | copy-start | bytes 196612
  2.3 32.6 %copy-start.4 = (s32[192]{0:T(256)S(1)}, s32[192]{0:T(256)}, u32[]{:S(2)}) copy-start(s32[192]{0:T(256)} %param.11) | copy-start | bytes 2308
  2.3 32.6 %copy-start.5 = (s32[192]{0:T(256)S(1)}, s32[192]{0:T(256)}, u32[]{:S(2)}) copy-start(s32[192]{0:T(256)} %param.12) | copy-start | bytes 2308
  2.3 24.2 %all-to-all-start = ((bf16[8,32,1024]{2,1,0:T(8,128)(2,1)}), bf16[8,32,1024]{2,1,0:T(8,128)(2,1)S(1)}, u32[]{:S(2)}, u32[]{:S(2)}) async-start(bf16[8,32,1024]{2,1,0:T(8,128)(2,1)} %shard_map.94), calls=%async_computation | async-start | bytes 1048576 | tf_op jit(solution)/shard_map/all_to_all | solution.py:234
  10.5 15.9 %collective-permute-start = (bf16[32,1024]{1,0:T(8,128)(2,1)S(1)}, bf16[32,1024]{1,0:T(8,128)(2,1)S(1)}, u32[]{:S(2)}, u32[]{:S(2)}) collective-permute-start(bf16[32,1024]{1,0:T(8,128)(2,1)S(1)} %bitcast.20), channel_id=1, source_target_pairs={{0,64},{64,0},{1,65},{65,1},{2,66},{66,2},{3,67},{67,3},{4,68},{68... | collective-permute-start | bytes 196616 | tf_op jit(solution)/shard_map/ppermute | solution.py:237
  27.3 18.6 %all-to-all-start.1 = ((bf16[8,32,1024]{2,1,0:T(8,128)(2,1)}), bf16[8,32,1024]{2,1,0:T(8,128)(2,1)S(1)}, u32[]{:S(2)}, u32[]{:S(2)}) async-start(bf16[8,32,1024]{2,1,0:T(8,128)(2,1)} %shard_map.95), calls=%async_computation.1 | async-start | bytes 1048576 | tf_op jit(solution)/shard_map/all_to_all | solution.py:234
  35.0 26.7 %copy-start.3 = (bf16[32,256]{1,0:T(8,128)(2,1)S(1)}, bf16[32,256]{1,0:T(8,128)(2,1)}, u32[]{:S(2)}) copy-start(bf16[32,256]{1,0:T(8,128)(2,1)} %weight_ref.1) | copy-start | bytes 49156
  49.4 12.4 %collective-permute-start.1 = (f32[4,8,32,128]{3,2,1,0:T(8,128)S(1)}, f32[4,8,32,128]{3,2,1,0:T(8,128)S(1)}, u32[]{:S(2)}, u32[]{:S(2)}) collective-permute-start(f32[4,8,32,128]{3,2,1,0:T(8,128)S(1)} %get-tuple-element.14), channel_id=1, source_target_pairs={{0,8},{8,0},{1,9},{9,1},{2,10},{10,2},{3,11},{11,3},{4,12},{12,4},... | collective-permute-start | bytes 1572872 | tf_op jit(solution)/shard_map/ppermute | solution.py:251
  61.7 23.9 %copy-start.2 = (bf16[128,256]{1,0:T(8,128)(2,1)S(1)}, bf16[128,256]{1,0:T(8,128)(2,1)}, u32[]{:S(2)}) copy-start(bf16[128,256]{1,0:T(8,128)(2,1)} %grad_ref.1) | copy-start | bytes 196612
  105.6 6.3 %collective-permute-start.2 = (bf16[32,48,128]{2,1,0:T(8,128)(2,1)S(1)}, bf16[32,48,128]{2,1,0:T(8,128)(2,1)S(1)}, u32[]{:S(2)}, u32[]{:S(2)}) collective-permute-start(bf16[32,48,128]{2,1,0:T(8,128)(2,1)S(1)} %all_to_all.31.mine_ref), channel_id=1, source_target_pairs={{0,8},{8,0},{1,9},{9,1},{2,10},{10,2},{3,11},{11,3},{4,12},{12,4},... | collective-permute-start | bytes 1179656 | tf_op jit(solution)/shard_map/ppermute | solution.py:272

commit v9 on v8

--- a/solution.py
+++ b/solution.py
@@ -135,11 +135,11 @@
 def backward_kernel(
     table, adj_ref, mine_ref, other_ref, out_ref, proj_ref, acc_ref, *tiles
 ):
-    core, count = table[0], table[2]
+    core, side, count = table[0], table[1], table[2]
     row_of, col_of = slots_of(table, adj_ref.shape[0])
-    rows = out_ref.shape[0]
+    rings = out_ref.shape[0]
     width = acc_ref.shape[1]
-    blocks = acc_ref.shape[0] // rows
+    blocks = acc_ref.shape[0] // (rings * SIDES)
     feats = proj_ref.shape[2]
     for pair in range(proj_ref.shape[0]):
         part = slice(pair * feats, (pair + 1) * feats)
@@ -154,25 +154,37 @@
     weight_term = jnp.sum(mine_ref[:, width:].astype(jnp.float32), axis=0) + jnp.sum(
         other_ref[:, width:].astype(jnp.float32), axis=0
     )
-    for row in range(rows):
-        for block in range(blocks):
-            out_ref[row, block * width : (block + 1) * width] = acc_ref[
-                row * blocks + block
-            ].astype(out_ref.dtype)
-        out_ref[row, blocks * width :] = weight_term.astype(out_ref.dtype)
-
-
-def final_kernel(scale, pieces_ref, grad_ref, weight_ref):
+    for ring in range(rings):
+        for part, out_side in enumerate((1 - side, side)):
+            start = (ring * SIDES + out_side) * blocks
+            for block in range(blocks):
+                top = (part * blocks + block) * width
+                out_ref[ring, top : top + width] = acc_ref[start + block].astype(out_ref.dtype)
+        out_ref[ring, SIDES * blocks * width :] = weight_term.astype(out_ref.dtype)
+
+
+def reduce_kernel(pieces_ref, far_ref, same_ref, weight_ref):
+    rows = far_ref.shape[0]
+    far_ref[...] = jnp.sum(pieces_ref[:, :rows].astype(jnp.float32), axis=0)
+    same_ref[...] = jnp.sum(pieces_ref[:, rows : 2 * rows].astype(jnp.float32), axis=0)
+    weight_term = jnp.sum(pieces_ref[:, 2 * rows :].astype(jnp.float32), axis=0)
+    for copy in range(weight_ref.shape[0]):
+        weight_ref[copy] = weight_term
+
+
+def final_kernel(scale, same_ref, swapped_ref, terms_ref, grad_ref, weight_ref):
     width, nodes = grad_ref.shape
-    extent = pieces_ref.shape[2]
+    extent = same_ref.shape[1]
     for block in range(nodes // extent):
-        grad_ref[:, block * extent : (block + 1) * extent] = jnp.sum(
-            pieces_ref[:, block * width : (block + 1) * width].astype(jnp.float32), axis=0
-        )
-    rest = pieces_ref[:, nodes // extent * width :].astype(jnp.float32)
-    weight_term = jnp.sum(rest, axis=0) * scale
-    for pair in range(weight_ref.shape[0]):
-        weight_ref[pair] = weight_term
+        part = slice(block * width, (block + 1) * width)
+        grad_ref[:, block * extent : (block + 1) * extent] = same_ref[part] + swapped_ref[part]
+    halves = weight_ref.shape[1] // extent
+    near = terms_ref.shape[0] // SIDES
+    for pair in range(near):
+        top, left = (pair // halves) * PIECE, (pair % halves) * extent
+        weight_ref[top : top + PIECE, left : left + extent] = (
+            terms_ref[pair] + terms_ref[near + pair]
+        ) * scale
 
 
 SMEM_SPEC = pl.BlockSpec(memory_space=pltpu.SMEM)
@@ -275,26 +287,32 @@
         (table,),
         adjacency,
         (mine, other),
-        pltpu.VMEM((rings * SIDES, blocks * width + PIECE, extent), bf16),
+        pltpu.VMEM((rings, SIDES * blocks * width + PIECE, extent), bf16),
         [
             pltpu.VMEM((near, CORES, feats, width, extent), bf16),
             pltpu.VMEM((rings * SIDES * blocks, width, extent), f32),
         ],
     )
-    pieces = lax.all_to_all(pieces, ("ring", "side"), 0, 0, tiled=False)
+    pieces = lax.all_to_all(pieces, "ring", 0, 0, tiled=False)
+    block_sum = jax.ShapeDtypeStruct((blocks * width, extent), f32)
+    other_side, this_side, weight_piece = call(
+        reduce_kernel,
+        (),
+        (pieces,),
+        (block_sum, block_sum, pltpu.VMEM((SIDES * near, PIECE, extent), f32)),
+    )
+    swapped = lax.ppermute(other_side, "side", swap)
+    weight_terms = lax.all_to_all(weight_piece, ("side", "near"), 0, 0, tiled=False)
     scale = 1.0 / math.sqrt(nodes * rings * SIDES * near * CORES)
-    feature_grad, weight_piece = call(
+    feature_grad, weight_grad = call(
         lambda *refs: final_kernel(scale, *refs),
         (),
-        (pieces,),
+        (this_side, swapped, weight_terms),
         (
             jax.ShapeDtypeStruct((width, nodes), f32),
-            pltpu.VMEM((near, PIECE, extent), f32),
+            jax.ShapeDtypeStruct((width, full), f32),
         ),
     )
-    weight_grad = lax.all_to_all(weight_piece, "near", 0, 0, tiled=False)
-    weight_grad = weight_grad.reshape(width // PIECE, full // extent, PIECE, extent)
-    weight_grad = weight_grad.transpose(0, 2, 1, 3).reshape(width, full)
     return (activated, weight_grad, feature_grad.T)
 
 

time: 172 us -> 173 us (level)
  starting transfers between devices: 45.2 us -> 56.4 us
  blocking collectives: 96.1 us -> 86.7 us
    ppermute x0 -> x1, starting transfers between devices: none -> 12.2 us  [local(): swapped = lax.ppermute(other_side, 'side', swap)]
    all_to_all x2, blocking collectives: 53.3 us -> 43.3 us  [the longest x1 31.4 us: local(): pieces = lax.all_to_all(pieces, 'ring', 0, 0, tiled=False)]
  transfers between devices with their start and end apart: 5 -> 6, of which waited for: 4 -> 4; matrix products, arithmetic and copies ran while one was open for 0% -> 0% of each run, Pallas kernels for 0% -> 0%
where the time goes in v9:
time: 173 us; the launch traced here: 172 us
  blocking collectives  86.7 us (50%)
  starting transfers between devices  56.4 us (33%)
  waiting for transfers between devices  15.3 us (9%)
  Pallas kernels  10.8 us (6%)
    all_to_all x1, blocking collectives, local(): pieces = lax.all_to_all(pieces, 'ring', 0, 0, tiled=False)  31.4 us
    all_to_all x1, blocking collectives, local(): terms = lax.all_to_all(terms, ('near', 'feat'), 0, 0, tiled=False)  24.4 us
    all_to_all x1, blocking collectives, local(): mine = lax.all_to_all(outgoing, ('near', 'feat'), 0, 0, tiled=False)  19 us
    all_to_all x2, starting transfers between devices, spread(): return lax.all_to_all(copies, 'ring', 0, 0, tiled=False)  15 us
    ppermute x1, starting transfers between devices, local(): partner = lax.ppermute(own, 'side', swap)  14.3 us
    ppermute x1, starting transfers between devices, local(): swapped = lax.ppermute(other_side, 'side', swap)  12.2 us
    all_to_all x1, blocking collectives, local(): lax.all_to_all(weight_piece, ('side', 'near'), 0, 0, tiled=False)  11.9 us
    all_to_all x2, waiting for transfers between devices, spread(): return lax.all_to_all(copies, 'ring', 0, 0, tiled=False)  10.9 us
  transfers between devices with their start and end apart: 6, of which 4 were waited for; matrix products, arithmetic and copies ran while one was open for 0% of the time, Pallas kernels for 0%

profile of v9, /device:TPU:1, one launch (start us, length us, event | category | flops | bytes accessed | tf_op | source)
XLA Modules:
  0.0 171.7 jit_solution(9765434256209966308)
XLA Ops:
  0.6 0.0 copy-start
  0.6 0.8 copy-done
  1.5 0.0 copy-start.1
  1.5 0.8 shard_map.94
  2.3 8.1 %all-to-all-start = ((bf16[8,32,1024]{2,1,0:T(8,128)(2,1)}), bf16[8,32,1024]{2,1,0:T(8,128)(2,1)S(1)}, u32[]{:S(2)}, u32[]{:S(2)}) async-start(bf16[8,32,1024]{2,1,0:T(8,128)(2,1)} %shard_map.94), calls=%async_computation | async-start | bytes 1048576 | tf_op jit(solution)/shard_map/all_to_all | solution.py:246
  10.4 0.0 copy-done.1
  10.4 0.0 copy-start.4
  10.4 0.0 copy-start.5
  10.4 14.3 %collective-permute-start = (bf16[32,1024]{1,0:T(8,128)(2,1)S(1)}, bf16[32,1024]{1,0:T(8,128)(2,1)S(1)}, u32[]{:S(2)}, u32[]{:S(2)}) collective-permute-start(bf16[32,1024]{1,0:T(8,128)(2,1)S(1)} %bitcast.12), channel_id=1, source_target_pairs={{0,64},{64,0},{1,65},{65,1},{2,66},{66,2},{3,67},{67,3},{4,68},{68... | collective-permute-start | bytes 196616 | tf_op jit(solution)/shard_map/ppermute | solution.py:249
  24.7 1.6 collective-permute-done.value_ref
  26.4 0.0 all-to-all-done.same_ref
  26.4 0.8 shard_map.95
  27.2 6.9 %all-to-all-start.1 = ((bf16[8,32,1024]{2,1,0:T(8,128)(2,1)}), bf16[8,32,1024]{2,1,0:T(8,128)(2,1)S(1)}, u32[]{:S(2)}, u32[]{:S(2)}) async-start(bf16[8,32,1024]{2,1,0:T(8,128)(2,1)} %shard_map.95), calls=%async_computation.1 | async-start | bytes 1048576 | tf_op jit(solution)/shard_map/all_to_all | solution.py:246
  34.8 0.0 copy-done.4
  34.8 0.0 copy-done.5
  34.8 0.1 concatenate.3.table
  34.9 0.0 copy-start.3
  34.9 10.9 %all-to-all-done.1.far_ref = bf16[8,32,1024]{2,1,0:T(8,128)(2,1)S(1)} async-done(((bf16[8,32,1024]{2,1,0:T(8,128)(2,1)}), bf16[8,32,1024]{2,1,0:T(8,128)(2,1)S(1)}, u32[]{:S(2)}, u32[]{:S(2)}) %all-to-all-start.1) | async-done | bytes 524320 | tf_op jit(solution)/shard_map/all_to_all | solution.py:246
  45.7 3.7 %shard_map.96 = (f32[4,8,32,128]{3,2,1,0:T(8,128)S(1)}, f32[4,8,32,128]{3,2,1,0:T(8,128)S(1)}) custom-call(s32[387]{0:T(512)S(1)} %concatenate.3.table, bf16[192,128,128]{2,1,0:T(8,128)(2,1)} %adj_ref.3, bf16[8,32,1024]{2,1,0:T(8,128)(2,1)S(1)} %all-to-all-done.same_ref, bf16[8,32,1024]{2,1,0:T(8,128)(2,1)S(1)} %all-to-all-done.1.far_ref), custom_call_target="tpu_custom_call" | custom-call | tf_op jit(solution)/shard_map/pallas_call | solution.py:210
  49.5 10.0 %collective-permute-start.1 = (f32[4,8,32,128]{3,2,1,0:T(8,128)S(1)}, f32[4,8,32,128]{3,2,1,0:T(8,128)S(1)}, u32[]{:S(2)}, u32[]{:S(2)}) collective-permute-start(f32[4,8,32,128]{3,2,1,0:T(8,128)S(1)} %get-tuple-element.17), channel_id=1, source_target_pairs={{0,8},{8,0},{1,9},{9,1},{2,10},{10,2},{3,11},{11,3},{4,12},{12,4},... | collective-permute-start | bytes 1572872 | tf_op jit(solution)/shard_map/ppermute | solution.py:263
  59.5 1.5 collective-permute-done.1
  61.0 0.0 copy-done.3
  61.0 0.0 copy-start.2
  61.0 0.1 shard_map.97
  61.1 24.4 %all_to_all.30 = bf16[32,48,128]{2,1,0:T(8,128)(2,1)S(1)} all-to-all(bf16[32,48,128]{2,1,0:T(8,128)(2,1)S(1)} %shard_map.97), channel_id=1, replica_groups=mesh['ring'=8,'side'=2,'near'=4,'core'=2,'feat'=8] {'near','feat'}, dimensions={0} | all-to-all | bytes 786432 | tf_op jit(solution)/shard_map/all_to_all | solution.py:271
  85.5 0.0 copy-done.2
  85.5 0.9 shard_map.98
  86.4 19.0 %all_to_all.31.mine_ref = bf16[32,48,128]{2,1,0:T(8,128)(2,1)S(1)} all-to-all(bf16[32,48,128]{2,1,0:T(8,128)(2,1)S(1)} %get-tuple-element.19), channel_id=1, replica_groups=mesh['ring'=8,'side'=2,'near'=4,'core'=2,'feat'=8] {'near','feat'}, dimensions={0} | all-to-all | bytes 786432 | tf_op jit(solution)/shard_map/all_to_all | solution.py:283
  105.4 5.0 %collective-permute-start.2 = (bf16[32,48,128]{2,1,0:T(8,128)(2,1)S(1)}, bf16[32,48,128]{2,1,0:T(8,128)(2,1)S(1)}, u32[]{:S(2)}, u32[]{:S(2)}) collective-permute-start(bf16[32,48,128]{2,1,0:T(8,128)(2,1)S(1)} %all_to_all.31.mine_ref), channel_id=1, source_target_pairs={{0,8},{8,0},{1,9},{9,1},{2,10},{10,2},{3,11},{11,3},{4,12},{12,4},... | collective-permute-start | bytes 1179656 | tf_op jit(solution)/shard_map/ppermute | solution.py:284
  110.4 1.3 collective-permute-done.2.other_ref
  111.7 3.7 %shard_map.99 = bf16[8,528,128]{2,1,0:T(8,128)(2,1)S(1)} custom-call(s32[387]{0:T(512)S(1)} %concatenate.3.table, bf16[192,128,128]{2,1,0:T(8,128)(2,1)} %adj_ref.3, bf16[32,48,128]{2,1,0:T(8,128)(2,1)S(1)} %all_to_all.31.mine_ref, bf16[32,48,128]{2,1,0:T(8,128)(2,1)S(1)} %collective-permute-done.2.other_ref), custom_call_target="tpu_custom_call" | custom-call | tf_op jit(solution)/shard_map/pallas_call | solution.py:210
  115.4 31.4 %all_to_all.32.pieces_ref = bf16[8,528,128]{2,1,0:T(8,128)(2,1)S(1)} all-to-all(bf16[8,528,128]{2,1,0:T(8,128)(2,1)S(1)} %shard_map.99), channel_id=1, replica_groups=mesh['ring'=8,'side'=2,'near'=4,'core'=2,'feat'=8] {'ring'}, dimensions={0} | all-to-all | bytes 2162688 | tf_op jit(solution)/shard_map/all_to_all | solution.py:296
  146.8 0.1 shard_map.100
  147.0 12.2 %collective-permute-start.3 = (f32[256,128]{1,0:T(8,128)S(1)}, f32[256,128]{1,0:T(8,128)S(1)}, u32[]{:S(2)}, u32[]{:S(2)}) collective-permute-start(f32[256,128]{1,0:T(8,128)S(1)} %get-tuple-element.21), channel_id=1, source_target_pairs={{0,64},{64,0},{1,65},{65,1},{2,66},{66,2},{3,67},{67,3},{4,68},{68... | collective-permute-start | bytes 393224 | tf_op jit(solution)/shard_map/ppermute | solution.py:304
  159.1 11.9 %all_to_all.33.refs_2_ = f32[8,16,128]{2,1,0:T(8,128)S(1)} all-to-all(f32[8,16,128]{2,1,0:T(8,128)S(1)} %get-tuple-element.22), channel_id=1, replica_groups=mesh['ring'=8,'side'=2,'near'=4,'core'=2,'feat'=8] {'side','near'}, dimensions={0} | all-to-all | bytes 131072 | tf_op jit(solution)/shard_map/all_to_all | solution.py:305
  171.0 0.0 collective-permute-done.3.refs_1_
  171.0 0.7 shard_map.101
Async XLA Ops:
  0.6 0.8 copy-start
  1.5 8.9 %copy-start.1 = (bf16[1024,32]{0,1:T(8,128)(2,1)S(1)}, bf16[1024,32]{0,1:T(8,128)(2,1)}, u32[]{:S(2)}) copy-start(bf16[1024,32]{0,1:T(8,128)(2,1)} %param.7) | copy-start | bytes 196612
  2.3 24.1 %all-to-all-start = ((bf16[8,32,1024]{2,1,0:T(8,128)(2,1)}), bf16[8,32,1024]{2,1,0:T(8,128)(2,1)S(1)}, u32[]{:S(2)}, u32[]{:S(2)}) async-start(bf16[8,32,1024]{2,1,0:T(8,128)(2,1)} %shard_map.94), calls=%async_computation | async-start | bytes 1048576 | tf_op jit(solution)/shard_map/all_to_all | solution.py:246
  10.4 24.4 %copy-start.4 = (s32[192]{0:T(256)S(1)}, s32[192]{0:T(256)}, u32[]{:S(2)}) copy-start(s32[192]{0:T(256)} %param.11) | copy-start | bytes 2308
  10.4 24.4 %copy-start.5 = (s32[192]{0:T(256)S(1)}, s32[192]{0:T(256)}, u32[]{:S(2)}) copy-start(s32[192]{0:T(256)} %param.12) | copy-start | bytes 2308
  10.4 15.9 %collective-permute-start = (bf16[32,1024]{1,0:T(8,128)(2,1)S(1)}, bf16[32,1024]{1,0:T(8,128)(2,1)S(1)}, u32[]{:S(2)}, u32[]{:S(2)}) collective-permute-start(bf16[32,1024]{1,0:T(8,128)(2,1)S(1)} %bitcast.12), channel_id=1, source_target_pairs={{0,64},{64,0},{1,65},{65,1},{2,66},{66,2},{3,67},{67,3},{4,68},{68... | collective-permute-start | bytes 196616 | tf_op jit(solution)/shard_map/ppermute | solution.py:249
  27.2 18.5 %all-to-all-start.1 = ((bf16[8,32,1024]{2,1,0:T(8,128)(2,1)}), bf16[8,32,1024]{2,1,0:T(8,128)(2,1)S(1)}, u32[]{:S(2)}, u32[]{:S(2)}) async-start(bf16[8,32,1024]{2,1,0:T(8,128)(2,1)} %shard_map.95), calls=%async_computation.1 | async-start | bytes 1048576 | tf_op jit(solution)/shard_map/all_to_all | solution.py:246
  34.9 26.1 %copy-start.3 = (bf16[32,256]{1,0:T(8,128)(2,1)S(1)}, bf16[32,256]{1,0:T(8,128)(2,1)}, u32[]{:S(2)}) copy-start(bf16[32,256]{1,0:T(8,128)(2,1)} %weight_ref.1) | copy-start | bytes 49156
  49.5 11.5 %collective-permute-start.1 = (f32[4,8,32,128]{3,2,1,0:T(8,128)S(1)}, f32[4,8,32,128]{3,2,1,0:T(8,128)S(1)}, u32[]{:S(2)}, u32[]{:S(2)}) collective-permute-start(f32[4,8,32,128]{3,2,1,0:T(8,128)S(1)} %get-tuple-element.17), channel_id=1, source_target_pairs={{0,8},{8,0},{1,9},{9,1},{2,10},{10,2},{3,11},{11,3},{4,12},{12,4},... | collective-permute-start | bytes 1572872 | tf_op jit(solution)/shard_map/ppermute | solution.py:263
  61.0 24.5 %copy-start.2 = (bf16[128,256]{1,0:T(8,128)(2,1)S(1)}, bf16[128,256]{1,0:T(8,128)(2,1)}, u32[]{:S(2)}) copy-start(bf16[128,256]{1,0:T(8,128)(2,1)} %grad_ref.1) | copy-start | bytes 196612
  105.4 6.3 %collective-permute-start.2 = (bf16[32,48,128]{2,1,0:T(8,128)(2,1)S(1)}, bf16[32,48,128]{2,1,0:T(8,128)(2,1)S(1)}, u32[]{:S(2)}, u32[]{:S(2)}) collective-permute-start(bf16[32,48,128]{2,1,0:T(8,128)(2,1)S(1)} %all_to_all.31.mine_ref), channel_id=1, source_target_pairs={{0,8},{8,0},{1,9},{9,1},{2,10},{10,2},{3,11},{11,3},{4,12},{12,4},... | collective-permute-start | bytes 1179656 | tf_op jit(solution)/shard_map/ppermute | solution.py:284
  147.0 24.1 %collective-permute-start.3 = (f32[256,128]{1,0:T(8,128)S(1)}, f32[256,128]{1,0:T(8,128)S(1)}, u32[]{:S(2)}, u32[]{:S(2)}) collective-permute-start(f32[256,128]{1,0:T(8,128)S(1)} %get-tuple-element.21), channel_id=1, source_target_pairs={{0,64},{64,0},{1,65},{65,1},{2,66},{66,2},{3,67},{67,3},{4,68},{68... | collective-permute-start | bytes 393224 | tf_op jit(solution)/shard_map/ppermute | solution.py:304

commit v10 on v9

--- a/solution.py
+++ b/solution.py
@@ -165,7 +165,7 @@
 
 def reduce_kernel(pieces_ref, far_ref, same_ref, weight_ref):
     rows = far_ref.shape[0]
-    far_ref[...] = jnp.sum(pieces_ref[:, :rows].astype(jnp.float32), axis=0)
+    far_ref[...] = jnp.sum(pieces_ref[:, :rows].astype(jnp.float32), axis=0).astype(far_ref.dtype)
     same_ref[...] = jnp.sum(pieces_ref[:, rows : 2 * rows].astype(jnp.float32), axis=0)
     weight_term = jnp.sum(pieces_ref[:, 2 * rows :].astype(jnp.float32), axis=0)
     for copy in range(weight_ref.shape[0]):
@@ -177,7 +177,9 @@
     extent = same_ref.shape[1]
     for block in range(nodes // extent):
         part = slice(block * width, (block + 1) * width)
-        grad_ref[:, block * extent : (block + 1) * extent] = same_ref[part] + swapped_ref[part]
+        grad_ref[:, block * extent : (block + 1) * extent] = same_ref[part] + swapped_ref[
+            part
+        ].astype(jnp.float32)
     halves = weight_ref.shape[1] // extent
     near = terms_ref.shape[0] // SIDES
     for pair in range(near):
@@ -248,7 +250,7 @@
     own = features.T
     partner = lax.ppermute(own, "side", swap)
     same = spread(own)
-    same, partner = lax.optimization_barrier((same, partner))
+    same, partner, table = lax.optimization_barrier((same, partner, table))
     far = spread(partner)
 
     half = jax.ShapeDtypeStruct((near, feats, width, extent), f32)
@@ -294,12 +296,16 @@
         ],
     )
     pieces = lax.all_to_all(pieces, "ring", 0, 0, tiled=False)
-    block_sum = jax.ShapeDtypeStruct((blocks * width, extent), f32)
+    block_sum = (blocks * width, extent)
     other_side, this_side, weight_piece = call(
         reduce_kernel,
         (),
         (pieces,),
-        (block_sum, block_sum, pltpu.VMEM((SIDES * near, PIECE, extent), f32)),
+        (
+            pltpu.VMEM(block_sum, bf16),
+            jax.ShapeDtypeStruct(block_sum, f32),
+            pltpu.VMEM((SIDES * near, PIECE, extent), f32),
+        ),
     )
     swapped = lax.ppermute(other_side, "side", swap)
     weight_terms = lax.all_to_all(weight_piece, ("side", "near"), 0, 0, tiled=False)

time: 173 us -> 170 us (0.983)
  waiting for transfers between devices: 15.3 us -> 6.08 us
  blocking collectives: 86.7 us -> 93.6 us
    all_to_all x0 -> x1, starting transfers between devices: none -> 14.2 us  [local(): lax.all_to_all(weight_piece, ('side', 'near'), 0, 0, tiled=False)]
    all_to_all x2 -> x1, waiting for transfers between devices: 10.9 us -> 0.01 us  [spread(): return lax.all_to_all(copies, 'ring', 0, 0, tiled=False)]
    all_to_all x1, blocking collectives: 11.9 us -> 19.1 us  [spread(): return lax.all_to_all(copies, 'ring', 0, 0, tiled=False)]
    all_to_all x2 -> x1, starting transfers between devices: 15 us -> 8.11 us  [spread(): return lax.all_to_all(copies, 'ring', 0, 0, tiled=False)]
    ppermute x1, starting transfers between devices: 12.2 us -> 7.27 us  [local(): swapped = lax.ppermute(other_side, 'side', swap)]
    ppermute x1, waiting for transfers between devices: 0.01 us -> 2.35 us  [local(): swapped = lax.ppermute(other_side, 'side', swap)]
    ppermute x1, starting transfers between devices: 10 us -> 7.97 us  [local(): received = lax.ppermute(send, 'core', swap)]
where the time goes in v10:
time: 170 us; the launch traced here: 169 us
  blocking collectives  93.6 us (55%)
  starting transfers between devices  56.8 us (33%)
  Pallas kernels  10.2 us (6%)
  waiting for transfers between devices  6.08 us (4%)
    all_to_all x1, blocking collectives, local(): pieces = lax.all_to_all(pieces, 'ring', 0, 0, tiled=False)  30.3 us
    all_to_all x1, blocking collectives, local(): terms = lax.all_to_all(terms, ('near', 'feat'), 0, 0, tiled=False)  25.1 us
    all_to_all x1, blocking collectives, spread(): return lax.all_to_all(copies, 'ring', 0, 0, tiled=False)  19.1 us
    all_to_all x1, blocking collectives, local(): mine = lax.all_to_all(outgoing, ('near', 'feat'), 0, 0, tiled=False)  19 us
    ppermute x1, starting transfers between devices, local(): partner = lax.ppermute(own, 'side', swap)  14.3 us
    all_to_all x1, starting transfers between devices, local(): lax.all_to_all(weight_piece, ('side', 'near'), 0, 0, tiled=False)  14.2 us
    all_to_all x1, starting transfers between devices, spread(): return lax.all_to_all(copies, 'ring', 0, 0, tiled=False)  8.11 us
    ppermute x1, starting transfers between devices, local(): received = lax.ppermute(send, 'core', swap)  7.97 us
  transfers between devices with their start and end apart: 6, of which 4 were waited for; matrix products, arithmetic and copies ran while one was open for 0% of the time, Pallas kernels for 0%

profile of v10, /device:TPU:1, one launch (start us, length us, event | category | flops | bytes accessed | tf_op | source)
XLA Modules:
  0.0 169.0 jit_solution(9456154176246533039)
XLA Ops:
  0.6 0.0 copy-start.4
  0.6 0.0 copy-start
  0.7 0.8 copy-done
  1.5 0.0 copy-start.1
  1.5 0.0 copy-start.5
  1.5 0.8 shard_map.94
  2.3 8.1 %all-to-all-start = ((bf16[8,32,1024]{2,1,0:T(8,128)(2,1)}), bf16[8,32,1024]{2,1,0:T(8,128)(2,1)S(1)}, u32[]{:S(2)}, u32[]{:S(2)}) async-start(bf16[8,32,1024]{2,1,0:T(8,128)(2,1)} %shard_map.94), calls=%async_computation | async-start | bytes 1048576 | tf_op jit(solution)/shard_map/all_to_all | solution.py:248
  10.4 0.0 copy-done.1
  10.4 14.3 %collective-permute-start = (bf16[32,1024]{1,0:T(8,128)(2,1)S(1)}, bf16[32,1024]{1,0:T(8,128)(2,1)S(1)}, u32[]{:S(2)}, u32[]{:S(2)}) collective-permute-start(bf16[32,1024]{1,0:T(8,128)(2,1)S(1)} %bitcast.12), channel_id=1, source_target_pairs={{0,64},{64,0},{1,65},{65,1},{2,66},{66,2},{3,67},{67,3},{4,68},{68... | collective-permute-start | bytes 196616 | tf_op jit(solution)/shard_map/ppermute | solution.py:251
  25.4 0.0 copy-done.4
  25.4 0.0 copy-done.5
  25.4 0.1 concatenate.3.table
  25.5 0.9 collective-permute-done.value_ref
  26.3 0.0 all-to-all-done.same_ref
  26.4 19.1 %all_to_all.30.far_ref = bf16[8,32,1024]{2,1,0:T(8,128)(2,1)S(1)} all-to-all(bf16[8,32,1024]{2,1,0:T(8,128)(2,1)S(1)} %shard_map.95), channel_id=1, replica_groups=mesh['ring'=8,'side'=2,'near'=4,'core'=2,'feat'=8] {'ring'}, dimensions={0} | all-to-all | bytes 1048576 | tf_op jit(solution)/shard_map/all_to_all | solution.py:248
  45.5 0.0 copy-start.3
  45.5 3.5 %shard_map.96 = (f32[4,8,32,128]{3,2,1,0:T(8,128)S(1)}, f32[4,8,32,128]{3,2,1,0:T(8,128)S(1)}) custom-call(s32[387]{0:T(512)S(1)} %concatenate.3.table, bf16[192,128,128]{2,1,0:T(8,128)(2,1)} %adj_ref.3, bf16[8,32,1024]{2,1,0:T(8,128)(2,1)S(1)} %all-to-all-done.same_ref, bf16[8,32,1024]{2,1,0:T(8,128)(2,1)S(1)} %all_to_all.30.far_ref), custom_call_target="tpu_custom_call" | custom-call | tf_op jit(solution)/shard_map/pallas_call | solution.py:212
  49.0 8.0 %collective-permute-start.1 = (f32[4,8,32,128]{3,2,1,0:T(8,128)S(1)}, f32[4,8,32,128]{3,2,1,0:T(8,128)S(1)}, u32[]{:S(2)}, u32[]{:S(2)}) collective-permute-start(f32[4,8,32,128]{3,2,1,0:T(8,128)S(1)} %get-tuple-element.19), channel_id=1, source_target_pairs={{0,8},{8,0},{1,9},{9,1},{2,10},{10,2},{3,11},{11,3},{4,12},{12,4},... | collective-permute-start | bytes 1572872 | tf_op jit(solution)/shard_map/ppermute | solution.py:265
  57.0 1.5 collective-permute-done.1
  58.5 0.0 copy-done.3
  58.5 0.0 copy-start.2
  58.5 0.1 shard_map.97
  58.6 25.1 %all_to_all.31 = bf16[32,48,128]{2,1,0:T(8,128)(2,1)S(1)} all-to-all(bf16[32,48,128]{2,1,0:T(8,128)(2,1)S(1)} %shard_map.97), channel_id=1, replica_groups=mesh['ring'=8,'side'=2,'near'=4,'core'=2,'feat'=8] {'near','feat'}, dimensions={0} | all-to-all | bytes 786432 | tf_op jit(solution)/shard_map/all_to_all | solution.py:273
  83.7 0.0 copy-done.2
  83.7 0.9 shard_map.98
  84.6 19.0 %all_to_all.32.mine_ref = bf16[32,48,128]{2,1,0:T(8,128)(2,1)S(1)} all-to-all(bf16[32,48,128]{2,1,0:T(8,128)(2,1)S(1)} %get-tuple-element.21), channel_id=1, replica_groups=mesh['ring'=8,'side'=2,'near'=4,'core'=2,'feat'=8] {'near','feat'}, dimensions={0} | all-to-all | bytes 786432 | tf_op jit(solution)/shard_map/all_to_all | solution.py:285
  103.7 5.0 %collective-permute-start.2 = (bf16[32,48,128]{2,1,0:T(8,128)(2,1)S(1)}, bf16[32,48,128]{2,1,0:T(8,128)(2,1)S(1)}, u32[]{:S(2)}, u32[]{:S(2)}) collective-permute-start(bf16[32,48,128]{2,1,0:T(8,128)(2,1)S(1)} %all_to_all.32.mine_ref), channel_id=1, source_target_pairs={{0,8},{8,0},{1,9},{9,1},{2,10},{10,2},{3,11},{11,3},{4,12},{12,4},... | collective-permute-start | bytes 1179656 | tf_op jit(solution)/shard_map/ppermute | solution.py:286
  108.6 1.3 collective-permute-done.2.other_ref
  110.0 3.5 %shard_map.99 = bf16[8,528,128]{2,1,0:T(8,128)(2,1)S(1)} custom-call(s32[387]{0:T(512)S(1)} %concatenate.3.table, bf16[192,128,128]{2,1,0:T(8,128)(2,1)} %adj_ref.3, bf16[32,48,128]{2,1,0:T(8,128)(2,1)S(1)} %all_to_all.32.mine_ref, bf16[32,48,128]{2,1,0:T(8,128)(2,1)S(1)} %collective-permute-done.2.other_ref), custom_call_target="tpu_custom_call" | custom-call | tf_op jit(solution)/shard_map/pallas_call | solution.py:212
  113.5 30.3 %all_to_all.33.pieces_ref = bf16[8,528,128]{2,1,0:T(8,128)(2,1)S(1)} all-to-all(bf16[8,528,128]{2,1,0:T(8,128)(2,1)S(1)} %shard_map.99), channel_id=1, replica_groups=mesh['ring'=8,'side'=2,'near'=4,'core'=2,'feat'=8] {'ring'}, dimensions={0} | all-to-all | bytes 2162688 | tf_op jit(solution)/shard_map/all_to_all | solution.py:298
  143.8 0.7 shard_map.100
  144.5 14.2 %all-to-all-start.5 = ((f32[8,16,128]{2,1,0:T(8,128)}), f32[8,16,128]{2,1,0:T(8,128)S(1)}, u32[]{:S(2)}, u32[]{:S(2)}) async-start(f32[8,16,128]{2,1,0:T(8,128)} %get-tuple-element.24), calls=%async_computation.5 | async-start | bytes 131072 | tf_op jit(solution)/shard_map/all_to_all | solution.py:311
  158.7 7.3 %collective-permute-start.3 = (bf16[256,128]{1,0:T(8,128)(2,1)S(1)}, bf16[256,128]{1,0:T(8,128)(2,1)S(1)}, u32[]{:S(2)}, u32[]{:S(2)}) collective-permute-start(bf16[256,128]{1,0:T(8,128)(2,1)S(1)} %get-tuple-element.23), channel_id=1, source_target_pairs={{0,64},{64,0},{1,65},{65,1},{2,66},{66,2},{3,67},{67,3},{4,68},{68... | collective-permute-start | bytes 196616 | tf_op jit(solution)/shard_map/ppermute | solution.py:310
  166.0 2.4 %collective-permute-done.3.refs_1_ = bf16[256,128]{1,0:T(8,128)(2,1)S(1)} collective-permute-done((bf16[256,128]{1,0:T(8,128)(2,1)S(1)}, bf16[256,128]{1,0:T(8,128)(2,1)S(1)}, u32[]{:S(2)}, u32[]{:S(2)}) %collective-permute-start.3) | collective-permute-done | bytes 65568 | tf_op jit(solution)/shard_map/ppermute | solution.py:310
  168.3 0.0 all-to-all-done.5.refs_2_
  168.4 0.7 shard_map.101
  (1 shorter events, 0.0 us)
Async XLA Ops:
  0.6 24.7 %copy-start.4 = (s32[192]{0:T(256)S(1)}, s32[192]{0:T(256)}, u32[]{:S(2)}) copy-start(s32[192]{0:T(256)} %param.11) | copy-start | bytes 2308
  0.6 0.8 copy-start
  1.5 8.9 %copy-start.1 = (bf16[1024,32]{0,1:T(8,128)(2,1)S(1)}, bf16[1024,32]{0,1:T(8,128)(2,1)}, u32[]{:S(2)}) copy-start(bf16[1024,32]{0,1:T(8,128)(2,1)} %param.7) | copy-start | bytes 196612
  1.5 23.9 %copy-start.5 = (s32[192]{0:T(256)S(1)}, s32[192]{0:T(256)}, u32[]{:S(2)}) copy-start(s32[192]{0:T(256)} %param.12) | copy-start | bytes 2308
  2.3 24.0 %all-to-all-start = ((bf16[8,32,1024]{2,1,0:T(8,128)(2,1)}), bf16[8,32,1024]{2,1,0:T(8,128)(2,1)S(1)}, u32[]{:S(2)}, u32[]{:S(2)}) async-start(bf16[8,32,1024]{2,1,0:T(8,128)(2,1)} %shard_map.94), calls=%async_computation | async-start | bytes 1048576 | tf_op jit(solution)/shard_map/all_to_all | solution.py:248
  10.4 15.9 %collective-permute-start = (bf16[32,1024]{1,0:T(8,128)(2,1)S(1)}, bf16[32,1024]{1,0:T(8,128)(2,1)S(1)}, u32[]{:S(2)}, u32[]{:S(2)}) collective-permute-start(bf16[32,1024]{1,0:T(8,128)(2,1)S(1)} %bitcast.12), channel_id=1, source_target_pairs={{0,64},{64,0},{1,65},{65,1},{2,66},{66,2},{3,67},{67,3},{4,68},{68... | collective-permute-start | bytes 196616 | tf_op jit(solution)/shard_map/ppermute | solution.py:251
  45.5 13.0 %copy-start.3 = (bf16[32,256]{1,0:T(8,128)(2,1)S(1)}, bf16[32,256]{1,0:T(8,128)(2,1)}, u32[]{:S(2)}) copy-start(bf16[32,256]{1,0:T(8,128)(2,1)} %weight_ref.1) | copy-start | bytes 49156
  49.0 9.5 %collective-permute-start.1 = (f32[4,8,32,128]{3,2,1,0:T(8,128)S(1)}, f32[4,8,32,128]{3,2,1,0:T(8,128)S(1)}, u32[]{:S(2)}, u32[]{:S(2)}) collective-permute-start(f32[4,8,32,128]{3,2,1,0:T(8,128)S(1)} %get-tuple-element.19), channel_id=1, source_target_pairs={{0,8},{8,0},{1,9},{9,1},{2,10},{10,2},{3,11},{11,3},{4,12},{12,4},... | collective-permute-start | bytes 1572872 | tf_op jit(solution)/shard_map/ppermute | solution.py:265
  58.5 25.2 %copy-start.2 = (bf16[128,256]{1,0:T(8,128)(2,1)S(1)}, bf16[128,256]{1,0:T(8,128)(2,1)}, u32[]{:S(2)}) copy-start(bf16[128,256]{1,0:T(8,128)(2,1)} %grad_ref.1) | copy-start | bytes 196612
  103.7 6.3 %collective-permute-start.2 = (bf16[32,48,128]{2,1,0:T(8,128)(2,1)S(1)}, bf16[32,48,128]{2,1,0:T(8,128)(2,1)S(1)}, u32[]{:S(2)}, u32[]{:S(2)}) collective-permute-start(bf16[32,48,128]{2,1,0:T(8,128)(2,1)S(1)} %all_to_all.32.mine_ref), channel_id=1, source_target_pairs={{0,8},{8,0},{1,9},{9,1},{2,10},{10,2},{3,11},{11,3},{4,12},{12,4},... | collective-permute-start | bytes 1179656 | tf_op jit(solution)/shard_map/ppermute | solution.py:286
  144.5 23.9 %all-to-all-start.5 = ((f32[8,16,128]{2,1,0:T(8,128)}), f32[8,16,128]{2,1,0:T(8,128)S(1)}, u32[]{:S(2)}, u32[]{:S(2)}) async-start(f32[8,16,128]{2,1,0:T(8,128)} %get-tuple-element.24), calls=%async_computation.5 | async-start | bytes 131072 | tf_op jit(solution)/shard_map/all_to_all | solution.py:311
  158.7 9.6 %collective-permute-start.3 = (bf16[256,128]{1,0:T(8,128)(2,1)S(1)}, bf16[256,128]{1,0:T(8,128)(2,1)S(1)}, u32[]{:S(2)}, u32[]{:S(2)}) collective-permute-start(bf16[256,128]{1,0:T(8,128)(2,1)S(1)} %get-tuple-element.23), channel_id=1, source_target_pairs={{0,64},{64,0},{1,65},{65,1},{2,66},{66,2},{3,67},{67,3},{4,68},{68... | collective-permute-start | bytes 196616 | tf_op jit(solution)/shard_map/ppermute | solution.py:310

commit v11 on v10

--- a/solution.py
+++ b/solution.py
@@ -22,15 +22,24 @@
     return lax.dot_general(a, b, dims, preferred_element_type=jnp.float32)
 
 
-def accumulate_tiles(count, source, adj_ref, tiles_ref, done, acc_ref, target_of, dims):
-    chunks, extent = adj_ref.shape[0] // CHUNK, adj_ref.shape[1]
-
+def stage_kernel(source_ref, out_ref, done):
+    copy = pltpu.make_async_copy(source_ref, out_ref, done)
+    copy.start()
+    copy.wait()
+
+
+def start_copies(adj_ref, tiles_ref, done):
     def load(chunk):
         part = pl.ds(chunk * CHUNK, CHUNK)
         return pltpu.make_async_copy(adj_ref.at[part], tiles_ref.at[part], done.at[chunk])
 
-    for chunk in range(chunks):
+    for chunk in range(adj_ref.shape[0] // CHUNK):
         load(chunk).start()
+    return lambda chunk: load(chunk).wait()
+
+
+def accumulate_tiles(count, source, tiles_ref, wait, acc_ref, target_of, dims):
+    chunks, extent = tiles_ref.shape[0] // CHUNK, tiles_ref.shape[1]
     acc_ref[...] = jnp.zeros_like(acc_ref)
 
     def product(slot):
@@ -48,7 +57,7 @@
 
     @pl.loop(0, chunks)
     def _(chunk):
-        load(chunk).wait()
+        wait(chunk)
         first = chunk * CHUNK
 
         @pl.when(first < count)
@@ -63,8 +72,11 @@
     return lambda s: table[HEAD + s], lambda s: table[HEAD + slots + s]
 
 
-def forward_kernel(table, adj_ref, same_ref, far_ref, keep_ref, send_ref, acc_ref, *tiles):
+def forward_kernel(
+    table, adj_ref, same_ref, far_ref, keep_ref, send_ref, acc_ref, tiles_ref, done
+):
     core, side, count = table[0], table[1], table[2]
+    wait = start_copies(adj_ref, tiles_ref, done)
     slots, extent, _ = adj_ref.shape
     blocks = same_ref.shape[2] // extent
     row_of, col_of = slots_of(table, slots)
@@ -78,7 +90,7 @@
             row_device % SIDES == side, same_ref[ring, :, nodes], far_ref[ring, :, nodes]
         )
 
-    accumulate_tiles(count, source, adj_ref, *tiles, acc_ref, row_of, NT)
+    accumulate_tiles(count, source, tiles_ref, wait, acc_ref, row_of, NT)
     near, feats = keep_ref.shape[:2]
     for pair in range(near):
         keep_ref[pair] = acc_ref[pl.ds((pair * CORES + core) * feats, feats)]
@@ -133,10 +145,10 @@
 
 
 def backward_kernel(
-    table, adj_ref, mine_ref, other_ref, out_ref, proj_ref, acc_ref, *tiles
+    table, tiles_ref, mine_ref, other_ref, out_ref, proj_ref, acc_ref
 ):
     core, side, count = table[0], table[1], table[2]
-    row_of, col_of = slots_of(table, adj_ref.shape[0])
+    row_of, col_of = slots_of(table, tiles_ref.shape[0])
     rings = out_ref.shape[0]
     width = acc_ref.shape[1]
     blocks = acc_ref.shape[0] // (rings * SIDES)
@@ -150,7 +162,7 @@
         row = row_of(slot)
         return proj_ref[row // (CORES * feats), (row // feats) % CORES, row % feats]
 
-    accumulate_tiles(count, source, adj_ref, *tiles, acc_ref, col_of, NN)
+    accumulate_tiles(count, source, tiles_ref, lambda chunk: None, acc_ref, col_of, NN)
     weight_term = jnp.sum(mine_ref[:, width:].astype(jnp.float32), axis=0) + jnp.sum(
         other_ref[:, width:].astype(jnp.float32), axis=0
     )
@@ -160,16 +172,17 @@
             for block in range(blocks):
                 top = (part * blocks + block) * width
                 out_ref[ring, top : top + width] = acc_ref[start + block].astype(out_ref.dtype)
-        out_ref[ring, SIDES * blocks * width :] = weight_term.astype(out_ref.dtype)
+        for top in range(SIDES * blocks * width, out_ref.shape[1], PIECE):
+            out_ref[ring, top : top + PIECE] = weight_term.astype(out_ref.dtype)
 
 
 def reduce_kernel(pieces_ref, far_ref, same_ref, weight_ref):
     rows = far_ref.shape[0]
     far_ref[...] = jnp.sum(pieces_ref[:, :rows].astype(jnp.float32), axis=0).astype(far_ref.dtype)
     same_ref[...] = jnp.sum(pieces_ref[:, rows : 2 * rows].astype(jnp.float32), axis=0)
-    weight_term = jnp.sum(pieces_ref[:, 2 * rows :].astype(jnp.float32), axis=0)
-    for copy in range(weight_ref.shape[0]):
-        weight_ref[copy] = weight_term
+    weight_ref[...] = jnp.sum(
+        pieces_ref[:, 2 * rows : 2 * rows + PIECE].astype(jnp.float32), axis=0
+    )
 
 
 def final_kernel(scale, same_ref, swapped_ref, terms_ref, grad_ref, weight_ref):
@@ -206,6 +219,17 @@
         scratch_shapes=scratch,
         compiler_params=pltpu.CompilerParams(vmem_limit_bytes=VMEM_LIMIT),
     )(*scalars, *(in_vmem(array) for array in arrays))
+
+
+def stage(array):
+    return pl.pallas_call(
+        stage_kernel,
+        out_shape=pltpu.VMEM(array.shape, array.dtype),
+        in_specs=[pl.BlockSpec(memory_space=pltpu.HBM)],
+        out_specs=VMEM_SPEC,
+        scratch_shapes=[pltpu.SemaphoreType.DMA],
+        compiler_params=pltpu.CompilerParams(vmem_limit_bytes=VMEM_LIMIT),
+    )(pltpu.with_memory_space_constraint(array, pltpu.HBM))
 
 
 def tile_call(kernel, scalars, adjacency, arrays, out_shapes, scratch):
@@ -283,13 +307,13 @@
     )
 
     mine = lax.all_to_all(outgoing, ("near", "feat"), 0, 0, tiled=False)
+    mine, adjacency = lax.optimization_barrier((mine, adjacency))
     other = lax.ppermute(mine, "core", swap)
-    pieces = tile_call(
+    pieces = call(
         backward_kernel,
         (table,),
-        adjacency,
-        (mine, other),
-        pltpu.VMEM((rings, SIDES * blocks * width + PIECE, extent), bf16),
+        (stage(adjacency), mine, other),
+        pltpu.VMEM((rings, SIDES * blocks * width + 2 * PIECE, extent), bf16),
         [
             pltpu.VMEM((near, CORES, feats, width, extent), bf16),
             pltpu.VMEM((rings * SIDES * blocks, width, extent), f32),
@@ -304,8 +328,11 @@
         (
             pltpu.VMEM(block_sum, bf16),
             jax.ShapeDtypeStruct(block_sum, f32),
-            pltpu.VMEM((SIDES * near, PIECE, extent), f32),
+            pltpu.VMEM((PIECE, extent), f32),
         ),
+    )
+    weight_piece = call(
+        spread_kernel, (), (weight_piece,), pltpu.VMEM((SIDES * near, PIECE, extent), f32)
     )
     swapped = lax.ppermute(other_side, "side", swap)
     weight_terms = lax.all_to_all(weight_piece, ("side", "near"), 0, 0, tiled=False)

time: 170 us -> 172 us (1.012)
  blocking collectives: 93.6 us -> 96.6 us
  starting transfers between devices: 56.8 us -> 54.1 us
  waiting for transfers between devices: 6.08 us -> 3.79 us
  Pallas kernels: 10.2 us -> 12.4 us
    all_to_all x1, blocking collectives: 30.3 us -> 34 us  [local(): pieces = lax.all_to_all(pieces, 'ring', 0, 0, tiled=False)]
    pallas_call x2 -> x1, Pallas kernels: 7.03 us -> 3.74 us  [tile_call(): pl.pallas_call(kernel, out_shape=out_shapes, in_specs=[SMEM_SPEC] * len(s...]
    pallas_call x0 -> x1, Pallas kernels: none -> 2.8 us  [stage(): pl.pallas_call(stage_kernel, out_shape=pltpu.VMEM(array.shape, array.dtyp...]
    all_to_all x1, starting transfers between devices: 14.2 us -> 11.4 us  [local(): lax.all_to_all(weight_piece, ('side', 'near'), 0, 0, tiled=False)]
    pallas_call x6 -> x8, Pallas kernels: 3.18 us -> 5.85 us  [call(): pl.pallas_call(kernel, out_shape=out_shapes, in_specs=[SMEM_SPEC] * len(s...]
  transfers between devices with their start and end apart: 6 -> 6, of which waited for: 4 -> 3; matrix products, arithmetic and copies ran while one was open for 0% -> 0% of each run, Pallas kernels for 0% -> 2%
where the time goes in v11:
time: 172 us; the launch traced here: 170 us
  blocking collectives  96.6 us (56%)
  starting transfers between devices  54.1 us (31%)
  Pallas kernels  12.4 us (7%)
  waiting for transfers between devices  3.79 us (2%)
    all_to_all x1, blocking collectives, local(): pieces = lax.all_to_all(pieces, 'ring', 0, 0, tiled=False)  34 us
    all_to_all x1, blocking collectives, local(): terms = lax.all_to_all(terms, ('near', 'feat'), 0, 0, tiled=False)  24.5 us
    all_to_all x1, blocking collectives, spread(): return lax.all_to_all(copies, 'ring', 0, 0, tiled=False)  19.1 us
    all_to_all x1, blocking collectives, local(): mine = lax.all_to_all(outgoing, ('near', 'feat'), 0, 0, tiled=False)  19 us
    ppermute x1, starting transfers between devices, local(): partner = lax.ppermute(own, 'side', swap)  14.3 us
    all_to_all x1, starting transfers between devices, local(): lax.all_to_all(weight_piece, ('side', 'near'), 0, 0, tiled=False)  11.4 us
    all_to_all x1, starting transfers between devices, spread(): return lax.all_to_all(copies, 'ring', 0, 0, tiled=False)  8.24 us
    ppermute x1, starting transfers between devices, local(): received = lax.ppermute(send, 'core', swap)  7.95 us
  transfers between devices with their start and end apart: 6, of which 3 were waited for; matrix products, arithmetic and copies ran while one was open for 0% of the time, Pallas kernels for 2%

profile of v11, /device:TPU:1, one launch (start us, length us, event | category | flops | bytes accessed | tf_op | source)
XLA Modules:
  0.0 169.9 jit_solution(2333372843072796628)
XLA Ops:
  0.6 0.0 copy-start
  0.6 0.8 copy-done
  1.5 0.0 copy-start.2
  1.5 0.8 shard_map.94
  2.3 0.0 copy-start.1
  2.3 8.2 %all-to-all-start = ((bf16[8,32,1024]{2,1,0:T(8,128)(2,1)}), bf16[8,32,1024]{2,1,0:T(8,128)(2,1)S(1)}, u32[]{:S(2)}, u32[]{:S(2)}) async-start(bf16[8,32,1024]{2,1,0:T(8,128)(2,1)} %shard_map.94), calls=%async_computation | async-start | bytes 1048576 | tf_op jit(solution)/shard_map/all_to_all | solution.py:272
  10.5 14.3 %collective-permute-start = (bf16[32,1024]{1,0:T(8,128)(2,1)}, bf16[32,1024]{1,0:T(8,128)(2,1)S(1)}, u32[]{:S(2)}, u32[]{:S(2)}) collective-permute-start(bf16[32,1024]{1,0:T(8,128)(2,1)} %bitcast.11), channel_id=1, source_target_pairs={{0,64},{64,0},{1,65},{65,1},{2,66},{66,2},{3,67},{67,3},{4,68},{68... | collective-permute-start | bytes 196616 | tf_op jit(solution)/shard_map/ppermute | solution.py:275
  25.5 0.8 concatenate.3.table
  26.2 0.4 collective-permute-done.value_ref
  26.7 0.0 all-to-all-done.same_ref
  26.7 19.1 %all_to_all.30.far_ref = bf16[8,32,1024]{2,1,0:T(8,128)(2,1)S(1)} all-to-all(bf16[8,32,1024]{2,1,0:T(8,128)(2,1)S(1)} %shard_map.95), channel_id=1, replica_groups=mesh['ring'=8,'side'=2,'near'=4,'core'=2,'feat'=8] {'ring'}, dimensions={0} | all-to-all | bytes 1048576 | tf_op jit(solution)/shard_map/all_to_all | solution.py:272
  45.8 3.7 %shard_map.96 = (f32[4,8,32,128]{3,2,1,0:T(8,128)S(1)}, f32[4,8,32,128]{3,2,1,0:T(8,128)S(1)}) custom-call(s32[387]{0:T(512)S(1)} %concatenate.3.table, bf16[192,128,128]{2,1,0:T(8,128)(2,1)} %source_ref, bf16[8,32,1024]{2,1,0:T(8,128)(2,1)S(1)} %all-to-all-done.same_ref, bf16[8,32,1024]{2,1,0:T(8,128)(2,1)S(1)} %all_to_all.30.far_ref), custom_call_target="tpu_custom_call" | custom-call | tf_op jit(solution)/shard_map/pallas_call | solution.py:236
  49.6 7.9 %collective-permute-start.1 = (f32[4,8,32,128]{3,2,1,0:T(8,128)S(1)}, f32[4,8,32,128]{3,2,1,0:T(8,128)S(1)}, u32[]{:S(2)}, u32[]{:S(2)}) collective-permute-start(f32[4,8,32,128]{3,2,1,0:T(8,128)S(1)} %get-tuple-element.21), channel_id=1, source_target_pairs={{0,8},{8,0},{1,9},{9,1},{2,10},{10,2},{3,11},{11,3},{4,12},{12,4},... | collective-permute-start | bytes 1572872 | tf_op jit(solution)/shard_map/ppermute | solution.py:289
  57.5 1.5 collective-permute-done.1
  59.0 0.0 copy-done.2
  59.0 0.1 shard_map.97
  59.1 24.5 %all_to_all.31 = bf16[32,48,128]{2,1,0:T(8,128)(2,1)S(1)} all-to-all(bf16[32,48,128]{2,1,0:T(8,128)(2,1)S(1)} %shard_map.97), channel_id=1, replica_groups=mesh['ring'=8,'side'=2,'near'=4,'core'=2,'feat'=8] {'near','feat'}, dimensions={0} | all-to-all | bytes 786432 | tf_op jit(solution)/shard_map/all_to_all | solution.py:297
  83.6 0.0 copy-done.1
  83.6 0.9 shard_map.98
  84.5 19.0 %all_to_all.32.mine_ref = bf16[32,48,128]{2,1,0:T(8,128)(2,1)S(1)} all-to-all(bf16[32,48,128]{2,1,0:T(8,128)(2,1)S(1)} %get-tuple-element.23), channel_id=1, replica_groups=mesh['ring'=8,'side'=2,'near'=4,'core'=2,'feat'=8] {'near','feat'}, dimensions={0} | all-to-all | bytes 786432 | tf_op jit(solution)/shard_map/all_to_all | solution.py:309
  103.5 5.0 %collective-permute-start.2 = (bf16[32,48,128]{2,1,0:T(8,128)(2,1)S(1)}, bf16[32,48,128]{2,1,0:T(8,128)(2,1)S(1)}, u32[]{:S(2)}, u32[]{:S(2)}) collective-permute-start(bf16[32,48,128]{2,1,0:T(8,128)(2,1)S(1)} %all_to_all.32.mine_ref), channel_id=1, source_target_pairs={{0,8},{8,0},{1,9},{9,1},{2,10},{10,2},{3,11},{11,3},{4,12},{12,4},... | collective-permute-start | bytes 1179656 | tf_op jit(solution)/shard_map/ppermute | solution.py:311
  108.5 2.8 %shard_map.99.tiles_ref = bf16[192,128,128]{2,1,0:T(8,128)(2,1)S(1)} custom-call(bf16[192,128,128]{2,1,0:T(8,128)(2,1)} %source_ref), custom_call_target="tpu_custom_call" | custom-call | tf_op jit(solution)/shard_map/pallas_call | solution.py:225
  111.3 0.0 collective-permute-done.2.other_ref
  111.3 2.6 %shard_map.100 = bf16[8,544,128]{2,1,0:T(8,128)(2,1)S(1)} custom-call(s32[387]{0:T(512)S(1)} %concatenate.3.table, bf16[192,128,128]{2,1,0:T(8,128)(2,1)S(1)} %shard_map.99.tiles_ref, bf16[32,48,128]{2,1,0:T(8,128)(2,1)S(1)} %all_to_all.32.mine_ref, bf16[32,48,128]{2,1,0:T(8,128)(2,1)S(1)} %collective-permute-done.2.other_ref), custom_call_target="tpu_custom_call" | custom-call | tf_op jit(solution)/shard_map/pallas_call | solution.py:214
  113.9 34.0 %all_to_all.33.pieces_ref = bf16[8,544,128]{2,1,0:T(8,128)(2,1)S(1)} all-to-all(bf16[8,544,128]{2,1,0:T(8,128)(2,1)S(1)} %shard_map.100), channel_id=1, replica_groups=mesh['ring'=8,'side'=2,'near'=4,'core'=2,'feat'=8] {'ring'}, dimensions={0} | all-to-all | bytes 2228224 | tf_op jit(solution)/shard_map/all_to_all | solution.py:322
  147.9 0.1 shard_map.101
  148.0 0.6 shard_map.102
  148.7 11.4 %all-to-all-start.5 = ((f32[8,16,128]{2,1,0:T(8,128)}), f32[8,16,128]{2,1,0:T(8,128)S(1)}, u32[]{:S(2)}, u32[]{:S(2)}) async-start(f32[8,16,128]{2,1,0:T(8,128)} %shard_map.102), calls=%async_computation.5 | async-start | bytes 131072 | tf_op jit(solution)/shard_map/all_to_all | solution.py:338
  160.1 7.3 %collective-permute-start.3 = (bf16[256,128]{1,0:T(8,128)(2,1)S(1)}, bf16[256,128]{1,0:T(8,128)(2,1)S(1)}, u32[]{:S(2)}, u32[]{:S(2)}) collective-permute-start(bf16[256,128]{1,0:T(8,128)(2,1)S(1)} %get-tuple-element.27), channel_id=1, source_target_pairs={{0,64},{64,0},{1,65},{65,1},{2,66},{66,2},{3,67},{67,3},{4,68},{68... | collective-permute-start | bytes 196616 | tf_op jit(solution)/shard_map/ppermute | solution.py:337
  167.4 1.9 %collective-permute-done.3.refs_1_ = bf16[256,128]{1,0:T(8,128)(2,1)S(1)} collective-permute-done((bf16[256,128]{1,0:T(8,128)(2,1)S(1)}, bf16[256,128]{1,0:T(8,128)(2,1)S(1)}, u32[]{:S(2)}, u32[]{:S(2)}) %collective-permute-start.3) | collective-permute-done | bytes 65568 | tf_op jit(solution)/shard_map/ppermute | solution.py:337
  169.2 0.0 all-to-all-done.5.refs_2_
  169.2 0.7 shard_map.103
  (1 shorter events, 0.0 us)
Async XLA Ops:
  0.6 0.8 copy-start
  1.5 57.6 %copy-start.2 = (bf16[32,256]{1,0:T(8,128)(2,1)S(1)}, bf16[32,256]{1,0:T(8,128)(2,1)}, u32[]{:S(2)}) copy-start(bf16[32,256]{1,0:T(8,128)(2,1)} %weight_ref.1) | copy-start | bytes 49156
  2.3 81.3 %copy-start.1 = (bf16[128,256]{1,0:T(8,128)(2,1)S(1)}, bf16[128,256]{1,0:T(8,128)(2,1)}, u32[]{:S(2)}) copy-start(bf16[128,256]{1,0:T(8,128)(2,1)} %grad_ref.1) | copy-start | bytes 196612
  2.3 24.4 %all-to-all-start = ((bf16[8,32,1024]{2,1,0:T(8,128)(2,1)}), bf16[8,32,1024]{2,1,0:T(8,128)(2,1)S(1)}, u32[]{:S(2)}, u32[]{:S(2)}) async-start(bf16[8,32,1024]{2,1,0:T(8,128)(2,1)} %shard_map.94), calls=%async_computation | async-start | bytes 1048576 | tf_op jit(solution)/shard_map/all_to_all | solution.py:272
  10.5 16.1 %collective-permute-start = (bf16[32,1024]{1,0:T(8,128)(2,1)}, bf16[32,1024]{1,0:T(8,128)(2,1)S(1)}, u32[]{:S(2)}, u32[]{:S(2)}) collective-permute-start(bf16[32,1024]{1,0:T(8,128)(2,1)} %bitcast.11), channel_id=1, source_target_pairs={{0,64},{64,0},{1,65},{65,1},{2,66},{66,2},{3,67},{67,3},{4,68},{68... | collective-permute-start | bytes 196616 | tf_op jit(solution)/shard_map/ppermute | solution.py:275
  49.6 9.5 %collective-permute-start.1 = (f32[4,8,32,128]{3,2,1,0:T(8,128)S(1)}, f32[4,8,32,128]{3,2,1,0:T(8,128)S(1)}, u32[]{:S(2)}, u32[]{:S(2)}) collective-permute-start(f32[4,8,32,128]{3,2,1,0:T(8,128)S(1)} %get-tuple-element.21), channel_id=1, source_target_pairs={{0,8},{8,0},{1,9},{9,1},{2,10},{10,2},{3,11},{11,3},{4,12},{12,4},... | collective-permute-start | bytes 1572872 | tf_op jit(solution)/shard_map/ppermute | solution.py:289
  103.5 7.8 %collective-permute-start.2 = (bf16[32,48,128]{2,1,0:T(8,128)(2,1)S(1)}, bf16[32,48,128]{2,1,0:T(8,128)(2,1)S(1)}, u32[]{:S(2)}, u32[]{:S(2)}) collective-permute-start(bf16[32,48,128]{2,1,0:T(8,128)(2,1)S(1)} %all_to_all.32.mine_ref), channel_id=1, source_target_pairs={{0,8},{8,0},{1,9},{9,1},{2,10},{10,2},{3,11},{11,3},{4,12},{12,4},... | collective-permute-start | bytes 1179656 | tf_op jit(solution)/shard_map/ppermute | solution.py:311
  148.7 20.6 %all-to-all-start.5 = ((f32[8,16,128]{2,1,0:T(8,128)}), f32[8,16,128]{2,1,0:T(8,128)S(1)}, u32[]{:S(2)}, u32[]{:S(2)}) async-start(f32[8,16,128]{2,1,0:T(8,128)} %shard_map.102), calls=%async_computation.5 | async-start | bytes 131072 | tf_op jit(solution)/shard_map/all_to_all | solution.py:338
  160.1 9.1 %collective-permute-start.3 = (bf16[256,128]{1,0:T(8,128)(2,1)S(1)}, bf16[256,128]{1,0:T(8,128)(2,1)S(1)}, u32[]{:S(2)}, u32[]{:S(2)}) collective-permute-start(bf16[256,128]{1,0:T(8,128)(2,1)S(1)} %get-tuple-element.27), channel_id=1, source_target_pairs={{0,64},{64,0},{1,65},{65,1},{2,66},{66,2},{3,67},{67,3},{4,68},{68... | collective-permute-start | bytes 196616 | tf_op jit(solution)/shard_map/ppermute | solution.py:337

commit v12 on v10

--- a/solution.py
+++ b/solution.py
@@ -63,20 +63,16 @@
     return lambda s: table[HEAD + s], lambda s: table[HEAD + slots + s]
 
 
-def forward_kernel(table, adj_ref, same_ref, far_ref, keep_ref, send_ref, acc_ref, *tiles):
-    core, side, count = table[0], table[1], table[2]
+def forward_kernel(table, adj_ref, feat_ref, keep_ref, send_ref, acc_ref, *tiles):
+    core, count = table[0], table[2]
     slots, extent, _ = adj_ref.shape
-    blocks = same_ref.shape[2] // extent
+    blocks = feat_ref.shape[2] // extent
     row_of, col_of = slots_of(table, slots)
 
     def source(slot):
         col = col_of(slot)
-        row_device = col // blocks
         nodes = pl.ds(pl.multiple_of((col % blocks) * extent, extent), extent)
-        ring = row_device // SIDES
-        return jnp.where(
-            row_device % SIDES == side, same_ref[ring, :, nodes], far_ref[ring, :, nodes]
-        )
+        return feat_ref[col // blocks, :, nodes]
 
     accumulate_tiles(count, source, adj_ref, *tiles, acc_ref, row_of, NT)
     near, feats = keep_ref.shape[:2]
@@ -243,22 +239,18 @@
     table = jnp.concatenate([jnp.stack([core, side]), tile_count, tile_rows, tile_cols])
     bf16, f32 = jnp.bfloat16, jnp.float32
 
-    def spread(value):
-        copies = call(spread_kernel, (), (value,), pltpu.VMEM((rings, width, nodes), bf16))
-        return lax.all_to_all(copies, "ring", 0, 0, tiled=False)
-
-    own = features.T
-    partner = lax.ppermute(own, "side", swap)
-    same = spread(own)
-    same, partner, table = lax.optimization_barrier((same, partner, table))
-    far = spread(partner)
+    own = call(
+        spread_kernel, (), (features.T,), pltpu.VMEM((rings * SIDES, width, nodes), bf16)
+    )
+    own, table = lax.optimization_barrier((own, table))
+    gathered = lax.all_to_all(own, ("ring", "side"), 0, 0, tiled=False)
 
     half = jax.ShapeDtypeStruct((near, feats, width, extent), f32)
     keep, send = tile_call(
         forward_kernel,
         (table,),
         adjacency,
-        (same, far),
+        (gathered,),
         (half, half),
         [pltpu.VMEM((CORES * owners, width, extent), f32)],
     )
@@ -302,7 +294,7 @@
         (),
         (pieces,),
         (
-            pltpu.VMEM(block_sum, bf16),
+            jax.ShapeDtypeStruct(block_sum, f32),
             jax.ShapeDtypeStruct(block_sum, f32),
             pltpu.VMEM((SIDES * near, PIECE, extent), f32),
         ),

time: 170 us -> 169 us (level)
  blocking collectives: 93.6 us -> 140 us
  starting transfers between devices: 56.8 us -> 12 us
  waiting for transfers between devices: 6.08 us -> 2.84 us
    all_to_all x1 -> x2, blocking collectives: 19.1 us -> 66.3 us  [the longest x1 51.8 us: local(): gathered = lax.all_to_all(own, ('ring', 'side'), 0, 0, tiled=False)]
    all_to_all x2 -> x0, starting transfers between devices: 22.3 us -> none  [the longest x1 14.2 us: local(): lax.all_to_all(weight_piece, ('side', 'near'), 0, 0, tiled=False)]
    ppermute x1 -> x0, starting transfers between devices: 14.3 us -> none  [local(): partner = lax.ppermute(own, 'side', swap)]
    ppermute x1, starting transfers between devices: 7.27 us -> 1.92 us  [local(): swapped = lax.ppermute(other_side, 'side', swap)]
    ppermute x1, starting transfers between devices: 7.97 us -> 5.07 us  [local(): received = lax.ppermute(send, 'core', swap)]
    ppermute x1, waiting for transfers between devices: 2.35 us -> 0.01 us  [local(): swapped = lax.ppermute(other_side, 'side', swap)]
    all_to_all x1, blocking collectives: 25.1 us -> 22.8 us  [local(): terms = lax.all_to_all(terms, ('near', 'feat'), 0, 0, tiled=False)]
    all_to_all x1, blocking collectives: 30.3 us -> 32.1 us  [local(): pieces = lax.all_to_all(pieces, 'ring', 0, 0, tiled=False)]
  transfers between devices with their start and end apart: 6 -> 3, of which waited for: 4 -> 2; matrix products, arithmetic and copies ran while one was open for 0% -> 0% of each run, Pallas kernels for 0% -> 0%
where the time goes in v12:
time: 169 us; the launch traced here: 166 us
  blocking collectives  140 us (83%)
  starting transfers between devices  12 us (7%)
  Pallas kernels  9.02 us (5%)
  waiting for transfers between devices  2.84 us (2%)
    all_to_all x1, blocking collectives, local(): gathered = lax.all_to_all(own, ('ring', 'side'), 0, 0, tiled=False)  51.8 us
    all_to_all x1, blocking collectives, local(): pieces = lax.all_to_all(pieces, 'ring', 0, 0, tiled=False)  32.1 us
    all_to_all x1, blocking collectives, local(): terms = lax.all_to_all(terms, ('near', 'feat'), 0, 0, tiled=False)  22.8 us
    all_to_all x1, blocking collectives, local(): mine = lax.all_to_all(outgoing, ('near', 'feat'), 0, 0, tiled=False)  19 us
    all_to_all x1, blocking collectives, local(): lax.all_to_all(weight_piece, ('side', 'near'), 0, 0, tiled=False)  14.4 us
    pallas_call x2, Pallas kernels, tile_call(): pl.pallas_call(kernel, out_shape=out_shapes, in_specs=[SMEM_SPEC] * len(s...  7.15 us
    ppermute x1, starting transfers between devices, local(): received = lax.ppermute(send, 'core', swap)  5.07 us
    ppermute x1, starting transfers between devices, local(): other = lax.ppermute(mine, 'core', swap)  4.97 us
  transfers between devices with their start and end apart: 3, of which 2 were waited for; matrix products, arithmetic and copies ran while one was open for 0% of the time, Pallas kernels for 0%

profile of v12, /device:TPU:1, one launch (start us, length us, event | category | flops | bytes accessed | tf_op | source)
XLA Modules:
  0.0 166.4 jit_solution(5096434506023685791)
XLA Ops:
  0.6 0.0 copy-start.4
  0.6 0.0 copy-start.3
  1.3 0.0 copy-start
  1.3 0.8 copy-done
  2.2 0.1 shard_map.94
  2.2 0.0 copy-done.4
  2.2 0.0 copy-done.3
  2.2 0.1 concatenate.3.table
  2.3 51.8 %all_to_all.25.feat_ref = bf16[16,32,1024]{2,1,0:T(8,128)(2,1)S(1)} all-to-all(bf16[16,32,1024]{2,1,0:T(8,128)(2,1)S(1)} %shard_map.94), channel_id=1, replica_groups=mesh['ring'=8,'side'=2,'near'=4,'core'=2,'feat'=8] {'ring','side'}, dimensions={0} | all-to-all | bytes 2097152 | tf_op jit(solution)/shard_map/all_to_all | solution.py:246
  54.2 0.0 copy-start.2
  54.2 3.5 %shard_map.95 = (f32[4,8,32,128]{3,2,1,0:T(8,128)S(1)}, f32[4,8,32,128]{3,2,1,0:T(8,128)S(1)}) custom-call(s32[387]{0:T(512)S(1)} %concatenate.3.table, bf16[192,128,128]{2,1,0:T(8,128)(2,1)} %adj_ref.3, bf16[16,32,1024]{2,1,0:T(8,128)(2,1)S(1)} %all_to_all.25.feat_ref), custom_call_target="tpu_custom_call" | custom-call | tf_op jit(solution)/shard_map/pallas_call | solution.py:208
  57.7 5.1 %collective-permute-start = (f32[4,8,32,128]{3,2,1,0:T(8,128)S(1)}, f32[4,8,32,128]{3,2,1,0:T(8,128)S(1)}, u32[]{:S(2)}, u32[]{:S(2)}) collective-permute-start(f32[4,8,32,128]{3,2,1,0:T(8,128)S(1)} %get-tuple-element.17), channel_id=1, source_target_pairs={{0,8},{8,0},{1,9},{9,1},{2,10},{10,2},{3,11},{11,3},{4,12},{12,4},... | collective-permute-start | bytes 1572872 | tf_op jit(solution)/shard_map/ppermute | solution.py:257
  62.7 1.5 collective-permute-done
  64.3 0.0 copy-done.2
  64.3 0.0 copy-start.1
  64.3 0.1 shard_map.96
  64.3 22.8 %all_to_all.26 = bf16[32,48,128]{2,1,0:T(8,128)(2,1)S(1)} all-to-all(bf16[32,48,128]{2,1,0:T(8,128)(2,1)S(1)} %shard_map.96), channel_id=1, replica_groups=mesh['ring'=8,'side'=2,'near'=4,'core'=2,'feat'=8] {'near','feat'}, dimensions={0} | all-to-all | bytes 786432 | tf_op jit(solution)/shard_map/all_to_all | solution.py:265
  87.2 0.0 copy-done.1
  87.2 0.9 shard_map.97
  88.1 19.0 %all_to_all.27.mine_ref = bf16[32,48,128]{2,1,0:T(8,128)(2,1)S(1)} all-to-all(bf16[32,48,128]{2,1,0:T(8,128)(2,1)S(1)} %get-tuple-element.19), channel_id=1, replica_groups=mesh['ring'=8,'side'=2,'near'=4,'core'=2,'feat'=8] {'near','feat'}, dimensions={0} | all-to-all | bytes 786432 | tf_op jit(solution)/shard_map/all_to_all | solution.py:277
  107.1 5.0 %collective-permute-start.1 = (bf16[32,48,128]{2,1,0:T(8,128)(2,1)S(1)}, bf16[32,48,128]{2,1,0:T(8,128)(2,1)S(1)}, u32[]{:S(2)}, u32[]{:S(2)}) collective-permute-start(bf16[32,48,128]{2,1,0:T(8,128)(2,1)S(1)} %all_to_all.27.mine_ref), channel_id=1, source_target_pairs={{0,8},{8,0},{1,9},{9,1},{2,10},{10,2},{3,11},{11,3},{4,12},{12,4},... | collective-permute-start | bytes 1179656 | tf_op jit(solution)/shard_map/ppermute | solution.py:278
  112.1 1.3 collective-permute-done.1.other_ref
  113.4 3.7 %shard_map.98 = bf16[8,528,128]{2,1,0:T(8,128)(2,1)S(1)} custom-call(s32[387]{0:T(512)S(1)} %concatenate.3.table, bf16[192,128,128]{2,1,0:T(8,128)(2,1)} %adj_ref.3, bf16[32,48,128]{2,1,0:T(8,128)(2,1)S(1)} %all_to_all.27.mine_ref, bf16[32,48,128]{2,1,0:T(8,128)(2,1)S(1)} %collective-permute-done.1.other_ref), custom_call_target="tpu_custom_call" | custom-call | tf_op jit(solution)/shard_map/pallas_call | solution.py:208
  117.1 32.1 %all_to_all.28.pieces_ref = bf16[8,528,128]{2,1,0:T(8,128)(2,1)S(1)} all-to-all(bf16[8,528,128]{2,1,0:T(8,128)(2,1)S(1)} %shard_map.98), channel_id=1, replica_groups=mesh['ring'=8,'side'=2,'near'=4,'core'=2,'feat'=8] {'ring'}, dimensions={0} | all-to-all | bytes 2162688 | tf_op jit(solution)/shard_map/all_to_all | solution.py:290
  149.2 0.1 shard_map.99
  149.3 1.9 %collective-permute-start.2 = (f32[256,128]{1,0:T(8,128)S(1)}, f32[256,128]{1,0:T(8,128)S(1)}, u32[]{:S(2)}, u32[]{:S(2)}) collective-permute-start(f32[256,128]{1,0:T(8,128)S(1)} %get-tuple-element.21), channel_id=1, source_target_pairs={{0,64},{64,0},{1,65},{65,1},{2,66},{66,2},{3,67},{67,3},{4,68},{68... | collective-permute-start | bytes 393224 | tf_op jit(solution)/shard_map/ppermute | solution.py:302
  151.2 14.4 %all_to_all.29.refs_2_ = f32[8,16,128]{2,1,0:T(8,128)S(1)} all-to-all(f32[8,16,128]{2,1,0:T(8,128)S(1)} %get-tuple-element.22), channel_id=1, replica_groups=mesh['ring'=8,'side'=2,'near'=4,'core'=2,'feat'=8] {'side','near'}, dimensions={0} | all-to-all | bytes 131072 | tf_op jit(solution)/shard_map/all_to_all | solution.py:303
  165.7 0.0 collective-permute-done.2.refs_1_
  165.7 0.7 shard_map.100
Async XLA Ops:
  0.6 1.6 copy-start.4
  0.6 1.6 copy-start.3
  1.3 0.8 copy-start
  54.2 10.1 %copy-start.2 = (bf16[32,256]{1,0:T(8,128)(2,1)S(1)}, bf16[32,256]{1,0:T(8,128)(2,1)}, u32[]{:S(2)}) copy-start(bf16[32,256]{1,0:T(8,128)(2,1)} %weight_ref.1) | copy-start | bytes 49156
  57.7 6.6 %collective-permute-start = (f32[4,8,32,128]{3,2,1,0:T(8,128)S(1)}, f32[4,8,32,128]{3,2,1,0:T(8,128)S(1)}, u32[]{:S(2)}, u32[]{:S(2)}) collective-permute-start(f32[4,8,32,128]{3,2,1,0:T(8,128)S(1)} %get-tuple-element.17), channel_id=1, source_target_pairs={{0,8},{8,0},{1,9},{9,1},{2,10},{10,2},{3,11},{11,3},{4,12},{12,4},... | collective-permute-start | bytes 1572872 | tf_op jit(solution)/shard_map/ppermute | solution.py:257
  64.3 22.9 %copy-start.1 = (bf16[128,256]{1,0:T(8,128)(2,1)S(1)}, bf16[128,256]{1,0:T(8,128)(2,1)}, u32[]{:S(2)}) copy-start(bf16[128,256]{1,0:T(8,128)(2,1)} %grad_ref.1) | copy-start | bytes 196612
  107.1 6.3 %collective-permute-start.1 = (bf16[32,48,128]{2,1,0:T(8,128)(2,1)S(1)}, bf16[32,48,128]{2,1,0:T(8,128)(2,1)S(1)}, u32[]{:S(2)}, u32[]{:S(2)}) collective-permute-start(bf16[32,48,128]{2,1,0:T(8,128)(2,1)S(1)} %all_to_all.27.mine_ref), channel_id=1, source_target_pairs={{0,8},{8,0},{1,9},{9,1},{2,10},{10,2},{3,11},{11,3},{4,12},{12,4},... | collective-permute-start | bytes 1179656 | tf_op jit(solution)/shard_map/ppermute | solution.py:278
  149.3 16.4 %collective-permute-start.2 = (f32[256,128]{1,0:T(8,128)S(1)}, f32[256,128]{1,0:T(8,128)S(1)}, u32[]{:S(2)}, u32[]{:S(2)}) collective-permute-start(f32[256,128]{1,0:T(8,128)S(1)} %get-tuple-element.21), channel_id=1, source_target_pairs={{0,64},{64,0},{1,65},{65,1},{2,66},{66,2},{3,67},{67,3},{4,68},{68... | collective-permute-start | bytes 393224 | tf_op jit(solution)/shard_map/ppermute | solution.py:302

commit v13 on v10

--- a/solution.py
+++ b/solution.py
@@ -22,7 +22,7 @@
     return lax.dot_general(a, b, dims, preferred_element_type=jnp.float32)
 
 
-def accumulate_tiles(count, source, adj_ref, tiles_ref, done, acc_ref, target_of, dims):
+def accumulate_tiles(count, gather, source, adj_ref, tiles_ref, done, acc_ref, target_of, dims):
     chunks, extent = adj_ref.shape[0] // CHUNK, adj_ref.shape[1]
 
     def load(chunk):
@@ -31,6 +31,7 @@
 
     for chunk in range(chunks):
         load(chunk).start()
+    gather()
     acc_ref[...] = jnp.zeros_like(acc_ref)
 
     def product(slot):
@@ -63,7 +64,9 @@
     return lambda s: table[HEAD + s], lambda s: table[HEAD + slots + s]
 
 
-def forward_kernel(table, adj_ref, same_ref, far_ref, keep_ref, send_ref, acc_ref, *tiles):
+def forward_kernel(
+    table, adj_ref, same_ref, far_ref, keep_ref, send_ref, feat_ref, acc_ref, *tiles
+):
     core, side, count = table[0], table[1], table[2]
     slots, extent, _ = adj_ref.shape
     blocks = same_ref.shape[2] // extent
@@ -71,14 +74,15 @@
 
     def source(slot):
         col = col_of(slot)
-        row_device = col // blocks
         nodes = pl.ds(pl.multiple_of((col % blocks) * extent, extent), extent)
-        ring = row_device // SIDES
-        return jnp.where(
-            row_device % SIDES == side, same_ref[ring, :, nodes], far_ref[ring, :, nodes]
-        )
-
-    accumulate_tiles(count, source, adj_ref, *tiles, acc_ref, row_of, NT)
+        return feat_ref[col // blocks, :, nodes]
+
+    def gather():
+        for ring in range(same_ref.shape[0]):
+            feat_ref[ring * SIDES + side] = same_ref[ring]
+            feat_ref[ring * SIDES + 1 - side] = far_ref[ring]
+
+    accumulate_tiles(count, gather, source, adj_ref, *tiles, acc_ref, row_of, NT)
     near, feats = keep_ref.shape[:2]
     for pair in range(near):
         keep_ref[pair] = acc_ref[pl.ds((pair * CORES + core) * feats, feats)]
@@ -141,16 +145,18 @@
     width = acc_ref.shape[1]
     blocks = acc_ref.shape[0] // (rings * SIDES)
     feats = proj_ref.shape[2]
-    for pair in range(proj_ref.shape[0]):
-        part = slice(pair * feats, (pair + 1) * feats)
-        proj_ref[pair, core] = mine_ref[part, :width]
-        proj_ref[pair, 1 - core] = other_ref[part, :width]
+
+    def gather():
+        for pair in range(proj_ref.shape[0]):
+            part = slice(pair * feats, (pair + 1) * feats)
+            proj_ref[pair, core] = mine_ref[part, :width]
+            proj_ref[pair, 1 - core] = other_ref[part, :width]
 
     def source(slot):
         row = row_of(slot)
         return proj_ref[row // (CORES * feats), (row // feats) % CORES, row % feats]
 
-    accumulate_tiles(count, source, adj_ref, *tiles, acc_ref, col_of, NN)
+    accumulate_tiles(count, gather, source, adj_ref, *tiles, acc_ref, col_of, NN)
     weight_term = jnp.sum(mine_ref[:, width:].astype(jnp.float32), axis=0) + jnp.sum(
         other_ref[:, width:].astype(jnp.float32), axis=0
     )
@@ -165,7 +171,7 @@
 
 def reduce_kernel(pieces_ref, far_ref, same_ref, weight_ref):
     rows = far_ref.shape[0]
-    far_ref[...] = jnp.sum(pieces_ref[:, :rows].astype(jnp.float32), axis=0).astype(far_ref.dtype)
+    far_ref[...] = jnp.sum(pieces_ref[:, :rows].astype(jnp.float32), axis=0)
     same_ref[...] = jnp.sum(pieces_ref[:, rows : 2 * rows].astype(jnp.float32), axis=0)
     weight_term = jnp.sum(pieces_ref[:, 2 * rows :].astype(jnp.float32), axis=0)
     for copy in range(weight_ref.shape[0]):
@@ -177,9 +183,7 @@
     extent = same_ref.shape[1]
     for block in range(nodes // extent):
         part = slice(block * width, (block + 1) * width)
-        grad_ref[:, block * extent : (block + 1) * extent] = same_ref[part] + swapped_ref[
-            part
-        ].astype(jnp.float32)
+        grad_ref[:, block * extent : (block + 1) * extent] = same_ref[part] + swapped_ref[part]
     halves = weight_ref.shape[1] // extent
     near = terms_ref.shape[0] // SIDES
     for pair in range(near):
@@ -260,7 +264,10 @@
         adjacency,
         (same, far),
         (half, half),
-        [pltpu.VMEM((CORES * owners, width, extent), f32)],
+        [
+            pltpu.VMEM((rings * SIDES, width, nodes), bf16),
+            pltpu.VMEM((CORES * owners, width, extent), f32),
+        ],
     )
     received = lax.ppermute(send, "core", swap)
     flat = (owners, width, extent)
@@ -302,7 +309,7 @@
         (),
         (pieces,),
         (
-            pltpu.VMEM(block_sum, bf16),
+            jax.ShapeDtypeStruct(block_sum, f32),
             jax.ShapeDtypeStruct(block_sum, f32),
             pltpu.VMEM((SIDES * near, PIECE, extent), f32),
         ),

time: 170 us -> 169 us (level)
  blocking collectives: 93.6 us -> 103 us
  starting transfers between devices: 56.8 us -> 50.1 us
  waiting for transfers between devices: 6.08 us -> 3.73 us
    all_to_all x1 -> x0, starting transfers between devices: 14.2 us -> none  [local(): lax.all_to_all(weight_piece, ('side', 'near'), 0, 0, tiled=False)]
    all_to_all x0 -> x1, blocking collectives: none -> 9.89 us  [local(): lax.all_to_all(weight_piece, ('side', 'near'), 0, 0, tiled=False)]
    ppermute x1, starting transfers between devices: 7.27 us -> 14.7 us  [local(): swapped = lax.ppermute(other_side, 'side', swap)]
    ppermute x1, waiting for transfers between devices: 2.35 us -> 0.01 us  [local(): swapped = lax.ppermute(other_side, 'side', swap)]
  transfers between devices with their start and end apart: 6 -> 5, of which waited for: 4 -> 3; matrix products, arithmetic and copies ran while one was open for 0% -> 0% of each run, Pallas kernels for 0% -> 0%
where the time goes in v13:
time: 169 us
  blocking collectives  103 us (61%)
  starting transfers between devices  50.1 us (30%)
  Pallas kernels  9.81 us (6%)
  waiting for transfers between devices  3.73 us (2%)
    all_to_all x1, blocking collectives, local(): pieces = lax.all_to_all(pieces, 'ring', 0, 0, tiled=False)  29.8 us
    all_to_all x1, blocking collectives, local(): terms = lax.all_to_all(terms, ('near', 'feat'), 0, 0, tiled=False)  24.9 us
    all_to_all x1, blocking collectives, spread(): return lax.all_to_all(copies, 'ring', 0, 0, tiled=False)  19.1 us
    all_to_all x1, blocking collectives, local(): mine = lax.all_to_all(outgoing, ('near', 'feat'), 0, 0, tiled=False)  19 us
    ppermute x1, starting transfers between devices, local(): swapped = lax.ppermute(other_side, 'side', swap)  14.7 us
    ppermute x1, starting transfers between devices, local(): partner = lax.ppermute(own, 'side', swap)  14.3 us
    all_to_all x1, blocking collectives, local(): lax.all_to_all(weight_piece, ('side', 'near'), 0, 0, tiled=False)  9.89 us
    all_to_all x1, starting transfers between devices, spread(): return lax.all_to_all(copies, 'ring', 0, 0, tiled=False)  8.11 us
  transfers between devices with their start and end apart: 5, of which 3 were waited for; matrix products, arithmetic and copies ran while one was open for 0% of the time, Pallas kernels for 0%

profile of v13, /device:TPU:1, one launch (start us, length us, event | category | flops | bytes accessed | tf_op | source)
XLA Modules:
  0.0 168.7 jit_solution(18315518131288719035)
XLA Ops:
  0.6 0.0 copy-start.4
  0.6 0.0 copy-start
  0.7 0.8 copy-done
  1.5 0.0 copy-start.1
  1.5 0.0 copy-start.5
  1.5 0.8 shard_map.94
  2.3 8.1 %all-to-all-start = ((bf16[8,32,1024]{2,1,0:T(8,128)(2,1)}), bf16[8,32,1024]{2,1,0:T(8,128)(2,1)S(1)}, u32[]{:S(2)}, u32[]{:S(2)}) async-start(bf16[8,32,1024]{2,1,0:T(8,128)(2,1)} %shard_map.94), calls=%async_computation | async-start | bytes 1048576 | tf_op jit(solution)/shard_map/all_to_all | solution.py:252
  10.4 0.0 copy-done.1
  10.4 14.3 %collective-permute-start = (bf16[32,1024]{1,0:T(8,128)(2,1)S(1)}, bf16[32,1024]{1,0:T(8,128)(2,1)S(1)}, u32[]{:S(2)}, u32[]{:S(2)}) collective-permute-start(bf16[32,1024]{1,0:T(8,128)(2,1)S(1)} %bitcast.12), channel_id=1, source_target_pairs={{0,64},{64,0},{1,65},{65,1},{2,66},{66,2},{3,67},{67,3},{4,68},{68... | collective-permute-start | bytes 196616 | tf_op jit(solution)/shard_map/ppermute | solution.py:255
  25.4 0.0 copy-done.4
  25.4 0.0 copy-done.5
  25.4 0.1 concatenate.3.table
  25.5 0.9 collective-permute-done.value_ref
  26.3 0.0 all-to-all-done.same_ref
  26.4 19.1 %all_to_all.30.far_ref = bf16[8,32,1024]{2,1,0:T(8,128)(2,1)S(1)} all-to-all(bf16[8,32,1024]{2,1,0:T(8,128)(2,1)S(1)} %shard_map.95), channel_id=1, replica_groups=mesh['ring'=8,'side'=2,'near'=4,'core'=2,'feat'=8] {'ring'}, dimensions={0} | all-to-all | bytes 1048576 | tf_op jit(solution)/shard_map/all_to_all | solution.py:252
  45.5 0.0 copy-start.3
  45.5 3.5 %shard_map.96 = (f32[4,8,32,128]{3,2,1,0:T(8,128)S(1)}, f32[4,8,32,128]{3,2,1,0:T(8,128)S(1)}) custom-call(s32[387]{0:T(512)S(1)} %concatenate.3.table, bf16[192,128,128]{2,1,0:T(8,128)(2,1)} %adj_ref.3, bf16[8,32,1024]{2,1,0:T(8,128)(2,1)S(1)} %all-to-all-done.same_ref, bf16[8,32,1024]{2,1,0:T(8,128)(2,1)S(1)} %all_to_all.30.far_ref), custom_call_target="tpu_custom_call" | custom-call | tf_op jit(solution)/shard_map/pallas_call | solution.py:216
  49.0 8.0 %collective-permute-start.1 = (f32[4,8,32,128]{3,2,1,0:T(8,128)S(1)}, f32[4,8,32,128]{3,2,1,0:T(8,128)S(1)}, u32[]{:S(2)}, u32[]{:S(2)}) collective-permute-start(f32[4,8,32,128]{3,2,1,0:T(8,128)S(1)} %get-tuple-element.19), channel_id=1, source_target_pairs={{0,8},{8,0},{1,9},{9,1},{2,10},{10,2},{3,11},{11,3},{4,12},{12,4},... | collective-permute-start | bytes 1572872 | tf_op jit(solution)/shard_map/ppermute | solution.py:272
  57.0 1.5 collective-permute-done.1
  58.5 0.0 copy-done.3
  58.5 0.0 copy-start.2
  58.5 0.1 shard_map.97
  58.6 24.9 %all_to_all.31 = bf16[32,48,128]{2,1,0:T(8,128)(2,1)S(1)} all-to-all(bf16[32,48,128]{2,1,0:T(8,128)(2,1)S(1)} %shard_map.97), channel_id=1, replica_groups=mesh['ring'=8,'side'=2,'near'=4,'core'=2,'feat'=8] {'near','feat'}, dimensions={0} | all-to-all | bytes 786432 | tf_op jit(solution)/shard_map/all_to_all | solution.py:280
  83.5 0.0 copy-done.2
  83.5 0.9 shard_map.98
  84.4 19.0 %all_to_all.32.mine_ref = bf16[32,48,128]{2,1,0:T(8,128)(2,1)S(1)} all-to-all(bf16[32,48,128]{2,1,0:T(8,128)(2,1)S(1)} %get-tuple-element.21), channel_id=1, replica_groups=mesh['ring'=8,'side'=2,'near'=4,'core'=2,'feat'=8] {'near','feat'}, dimensions={0} | all-to-all | bytes 786432 | tf_op jit(solution)/shard_map/all_to_all | solution.py:292
  103.4 5.0 %collective-permute-start.2 = (bf16[32,48,128]{2,1,0:T(8,128)(2,1)S(1)}, bf16[32,48,128]{2,1,0:T(8,128)(2,1)S(1)}, u32[]{:S(2)}, u32[]{:S(2)}) collective-permute-start(bf16[32,48,128]{2,1,0:T(8,128)(2,1)S(1)} %all_to_all.32.mine_ref), channel_id=1, source_target_pairs={{0,8},{8,0},{1,9},{9,1},{2,10},{10,2},{3,11},{11,3},{4,12},{12,4},... | collective-permute-start | bytes 1179656 | tf_op jit(solution)/shard_map/ppermute | solution.py:293
  108.4 1.3 collective-permute-done.2.other_ref
  109.7 3.7 %shard_map.99 = bf16[8,528,128]{2,1,0:T(8,128)(2,1)S(1)} custom-call(s32[387]{0:T(512)S(1)} %concatenate.3.table, bf16[192,128,128]{2,1,0:T(8,128)(2,1)} %adj_ref.3, bf16[32,48,128]{2,1,0:T(8,128)(2,1)S(1)} %all_to_all.32.mine_ref, bf16[32,48,128]{2,1,0:T(8,128)(2,1)S(1)} %collective-permute-done.2.other_ref), custom_call_target="tpu_custom_call" | custom-call | tf_op jit(solution)/shard_map/pallas_call | solution.py:216
  113.4 29.8 %all_to_all.33.pieces_ref = bf16[8,528,128]{2,1,0:T(8,128)(2,1)S(1)} all-to-all(bf16[8,528,128]{2,1,0:T(8,128)(2,1)S(1)} %shard_map.99), channel_id=1, replica_groups=mesh['ring'=8,'side'=2,'near'=4,'core'=2,'feat'=8] {'ring'}, dimensions={0} | all-to-all | bytes 2162688 | tf_op jit(solution)/shard_map/all_to_all | solution.py:305
  143.2 0.1 shard_map.100
  143.4 14.7 %collective-permute-start.3 = (f32[256,128]{1,0:T(8,128)S(1)}, f32[256,128]{1,0:T(8,128)S(1)}, u32[]{:S(2)}, u32[]{:S(2)}) collective-permute-start(f32[256,128]{1,0:T(8,128)S(1)} %get-tuple-element.23), channel_id=1, source_target_pairs={{0,64},{64,0},{1,65},{65,1},{2,66},{66,2},{3,67},{67,3},{4,68},{68... | collective-permute-start | bytes 393224 | tf_op jit(solution)/shard_map/ppermute | solution.py:317
  158.1 9.9 %all_to_all.34.refs_2_ = f32[8,16,128]{2,1,0:T(8,128)S(1)} all-to-all(f32[8,16,128]{2,1,0:T(8,128)S(1)} %get-tuple-element.24), channel_id=1, replica_groups=mesh['ring'=8,'side'=2,'near'=4,'core'=2,'feat'=8] {'side','near'}, dimensions={0} | all-to-all | bytes 131072 | tf_op jit(solution)/shard_map/all_to_all | solution.py:318
  168.0 0.0 collective-permute-done.3.refs_1_
  168.0 0.7 shard_map.101
  (1 shorter events, 0.0 us)
Async XLA Ops:
  0.6 24.7 %copy-start.4 = (s32[192]{0:T(256)S(1)}, s32[192]{0:T(256)}, u32[]{:S(2)}) copy-start(s32[192]{0:T(256)} %param.11) | copy-start | bytes 2308
  0.6 0.8 copy-start
  1.5 8.9 %copy-start.1 = (bf16[1024,32]{0,1:T(8,128)(2,1)S(1)}, bf16[1024,32]{0,1:T(8,128)(2,1)}, u32[]{:S(2)}) copy-start(bf16[1024,32]{0,1:T(8,128)(2,1)} %param.7) | copy-start | bytes 196612
  1.5 23.9 %copy-start.5 = (s32[192]{0:T(256)S(1)}, s32[192]{0:T(256)}, u32[]{:S(2)}) copy-start(s32[192]{0:T(256)} %param.12) | copy-start | bytes 2308
  2.3 24.0 %all-to-all-start = ((bf16[8,32,1024]{2,1,0:T(8,128)(2,1)}), bf16[8,32,1024]{2,1,0:T(8,128)(2,1)S(1)}, u32[]{:S(2)}, u32[]{:S(2)}) async-start(bf16[8,32,1024]{2,1,0:T(8,128)(2,1)} %shard_map.94), calls=%async_computation | async-start | bytes 1048576 | tf_op jit(solution)/shard_map/all_to_all | solution.py:252
  10.4 15.9 %collective-permute-start = (bf16[32,1024]{1,0:T(8,128)(2,1)S(1)}, bf16[32,1024]{1,0:T(8,128)(2,1)S(1)}, u32[]{:S(2)}, u32[]{:S(2)}) collective-permute-start(bf16[32,1024]{1,0:T(8,128)(2,1)S(1)} %bitcast.12), channel_id=1, source_target_pairs={{0,64},{64,0},{1,65},{65,1},{2,66},{66,2},{3,67},{67,3},{4,68},{68... | collective-permute-start | bytes 196616 | tf_op jit(solution)/shard_map/ppermute | solution.py:255
  45.5 13.0 %copy-start.3 = (bf16[32,256]{1,0:T(8,128)(2,1)S(1)}, bf16[32,256]{1,0:T(8,128)(2,1)}, u32[]{:S(2)}) copy-start(bf16[32,256]{1,0:T(8,128)(2,1)} %weight_ref.1) | copy-start | bytes 49156
  49.0 9.5 %collective-permute-start.1 = (f32[4,8,32,128]{3,2,1,0:T(8,128)S(1)}, f32[4,8,32,128]{3,2,1,0:T(8,128)S(1)}, u32[]{:S(2)}, u32[]{:S(2)}) collective-permute-start(f32[4,8,32,128]{3,2,1,0:T(8,128)S(1)} %get-tuple-element.19), channel_id=1, source_target_pairs={{0,8},{8,0},{1,9},{9,1},{2,10},{10,2},{3,11},{11,3},{4,12},{12,4},... | collective-permute-start | bytes 1572872 | tf_op jit(solution)/shard_map/ppermute | solution.py:272
  58.5 25.0 %copy-start.2 = (bf16[128,256]{1,0:T(8,128)(2,1)S(1)}, bf16[128,256]{1,0:T(8,128)(2,1)}, u32[]{:S(2)}) copy-start(bf16[128,256]{1,0:T(8,128)(2,1)} %grad_ref.1) | copy-start | bytes 196612
  103.4 6.3 %collective-permute-start.2 = (bf16[32,48,128]{2,1,0:T(8,128)(2,1)S(1)}, bf16[32,48,128]{2,1,0:T(8,128)(2,1)S(1)}, u32[]{:S(2)}, u32[]{:S(2)}) collective-permute-start(bf16[32,48,128]{2,1,0:T(8,128)(2,1)S(1)} %all_to_all.32.mine_ref), channel_id=1, source_target_pairs={{0,8},{8,0},{1,9},{9,1},{2,10},{10,2},{3,11},{11,3},{4,12},{12,4},... | collective-permute-start | bytes 1179656 | tf_op jit(solution)/shard_map/ppermute | solution.py:293
  143.4 24.6 %collective-permute-start.3 = (f32[256,128]{1,0:T(8,128)S(1)}, f32[256,128]{1,0:T(8,128)S(1)}, u32[]{:S(2)}, u32[]{:S(2)}) collective-permute-start(f32[256,128]{1,0:T(8,128)S(1)} %get-tuple-element.23), channel_id=1, source_target_pairs={{0,64},{64,0},{1,65},{65,1},{2,66},{66,2},{3,67},{67,3},{4,68},{68... | collective-permute-start | bytes 393224 | tf_op jit(solution)/shard_map/ppermute | solution.py:317

commit v14 on v13

--- a/solution.py
+++ b/solution.py
@@ -171,7 +171,7 @@
 
 def reduce_kernel(pieces_ref, far_ref, same_ref, weight_ref):
     rows = far_ref.shape[0]
-    far_ref[...] = jnp.sum(pieces_ref[:, :rows].astype(jnp.float32), axis=0)
+    far_ref[...] = jnp.sum(pieces_ref[:, :rows].astype(jnp.float32), axis=0).astype(far_ref.dtype)
     same_ref[...] = jnp.sum(pieces_ref[:, rows : 2 * rows].astype(jnp.float32), axis=0)
     weight_term = jnp.sum(pieces_ref[:, 2 * rows :].astype(jnp.float32), axis=0)
     for copy in range(weight_ref.shape[0]):
@@ -183,7 +183,9 @@
     extent = same_ref.shape[1]
     for block in range(nodes // extent):
         part = slice(block * width, (block + 1) * width)
-        grad_ref[:, block * extent : (block + 1) * extent] = same_ref[part] + swapped_ref[part]
+        grad_ref[:, block * extent : (block + 1) * extent] = same_ref[part] + swapped_ref[
+            part
+        ].astype(jnp.float32)
     halves = weight_ref.shape[1] // extent
     near = terms_ref.shape[0] // SIDES
     for pair in range(near):
@@ -309,7 +311,7 @@
         (),
         (pieces,),
         (
-            jax.ShapeDtypeStruct(block_sum, f32),
+            pltpu.VMEM(block_sum, bf16),
             jax.ShapeDtypeStruct(block_sum, f32),
             pltpu.VMEM((SIDES * near, PIECE, extent), f32),
         ),

time: 169 us -> 170 us (level)
  blocking collectives: 103 us -> 95.4 us
  starting transfers between devices: 50.1 us -> 54.6 us
  waiting for transfers between devices: 3.73 us -> 6.07 us
    all_to_all x0 -> x1, starting transfers between devices: none -> 12 us  [local(): lax.all_to_all(weight_piece, ('side', 'near'), 0, 0, tiled=False)]
    all_to_all x1 -> x0, blocking collectives: 9.89 us -> none  [local(): lax.all_to_all(weight_piece, ('side', 'near'), 0, 0, tiled=False)]
    ppermute x1, starting transfers between devices: 14.7 us -> 7.27 us  [local(): swapped = lax.ppermute(other_side, 'side', swap)]
    all_to_all x1, blocking collectives: 29.8 us -> 32.4 us  [local(): pieces = lax.all_to_all(pieces, 'ring', 0, 0, tiled=False)]
    ppermute x1, waiting for transfers between devices: 0.01 us -> 2.34 us  [local(): swapped = lax.ppermute(other_side, 'side', swap)]
  transfers between devices with their start and end apart: 5 -> 6, of which waited for: 3 -> 4; matrix products, arithmetic and copies ran while one was open for 0% -> 0% of each run, Pallas kernels for 0% -> 0%
where the time goes in v14:
time: 170 us; the launch traced here: 169 us
  blocking collectives  95.4 us (56%)
  starting transfers between devices  54.6 us (32%)
  Pallas kernels  10.3 us (6%)
  waiting for transfers between devices  6.07 us (4%)
    all_to_all x1, blocking collectives, local(): pieces = lax.all_to_all(pieces, 'ring', 0, 0, tiled=False)  32.4 us
    all_to_all x1, blocking collectives, local(): terms = lax.all_to_all(terms, ('near', 'feat'), 0, 0, tiled=False)  24.9 us
    all_to_all x1, blocking collectives, spread(): return lax.all_to_all(copies, 'ring', 0, 0, tiled=False)  19.1 us
    all_to_all x1, blocking collectives, local(): mine = lax.all_to_all(outgoing, ('near', 'feat'), 0, 0, tiled=False)  19 us
    ppermute x1, starting transfers between devices, local(): partner = lax.ppermute(own, 'side', swap)  14.3 us
    all_to_all x1, starting transfers between devices, local(): lax.all_to_all(weight_piece, ('side', 'near'), 0, 0, tiled=False)  12 us
    all_to_all x1, starting transfers between devices, spread(): return lax.all_to_all(copies, 'ring', 0, 0, tiled=False)  8.11 us
    ppermute x1, starting transfers between devices, local(): received = lax.ppermute(send, 'core', swap)  7.97 us
  transfers between devices with their start and end apart: 6, of which 4 were waited for; matrix products, arithmetic and copies ran while one was open for 0% of the time, Pallas kernels for 0%

profile of v14, /device:TPU:1, one launch (start us, length us, event | category | flops | bytes accessed | tf_op | source)
XLA Modules:
  0.0 168.7 jit_solution(16263197748878403495)
XLA Ops:
  0.6 0.0 copy-start.4
  0.6 0.0 copy-start
  0.7 0.8 copy-done
  1.5 0.0 copy-start.1
  1.5 0.0 copy-start.5
  1.5 0.8 shard_map.94
  2.3 8.1 %all-to-all-start = ((bf16[8,32,1024]{2,1,0:T(8,128)(2,1)}), bf16[8,32,1024]{2,1,0:T(8,128)(2,1)S(1)}, u32[]{:S(2)}, u32[]{:S(2)}) async-start(bf16[8,32,1024]{2,1,0:T(8,128)(2,1)} %shard_map.94), calls=%async_computation | async-start | bytes 1048576 | tf_op jit(solution)/shard_map/all_to_all | solution.py:254
  10.4 0.0 copy-done.1
  10.4 14.3 %collective-permute-start = (bf16[32,1024]{1,0:T(8,128)(2,1)S(1)}, bf16[32,1024]{1,0:T(8,128)(2,1)S(1)}, u32[]{:S(2)}, u32[]{:S(2)}) collective-permute-start(bf16[32,1024]{1,0:T(8,128)(2,1)S(1)} %bitcast.12), channel_id=1, source_target_pairs={{0,64},{64,0},{1,65},{65,1},{2,66},{66,2},{3,67},{67,3},{4,68},{68... | collective-permute-start | bytes 196616 | tf_op jit(solution)/shard_map/ppermute | solution.py:257
  25.4 0.0 copy-done.4
  25.4 0.0 copy-done.5
  25.4 0.1 concatenate.3.table
  25.5 0.9 collective-permute-done.value_ref
  26.3 0.0 all-to-all-done.same_ref
  26.4 19.1 %all_to_all.30.far_ref = bf16[8,32,1024]{2,1,0:T(8,128)(2,1)S(1)} all-to-all(bf16[8,32,1024]{2,1,0:T(8,128)(2,1)S(1)} %shard_map.95), channel_id=1, replica_groups=mesh['ring'=8,'side'=2,'near'=4,'core'=2,'feat'=8] {'ring'}, dimensions={0} | all-to-all | bytes 1048576 | tf_op jit(solution)/shard_map/all_to_all | solution.py:254
  45.5 0.0 copy-start.3
  45.5 3.5 %shard_map.96 = (f32[4,8,32,128]{3,2,1,0:T(8,128)S(1)}, f32[4,8,32,128]{3,2,1,0:T(8,128)S(1)}) custom-call(s32[387]{0:T(512)S(1)} %concatenate.3.table, bf16[192,128,128]{2,1,0:T(8,128)(2,1)} %adj_ref.3, bf16[8,32,1024]{2,1,0:T(8,128)(2,1)S(1)} %all-to-all-done.same_ref, bf16[8,32,1024]{2,1,0:T(8,128)(2,1)S(1)} %all_to_all.30.far_ref), custom_call_target="tpu_custom_call" | custom-call | tf_op jit(solution)/shard_map/pallas_call | solution.py:218
  49.0 8.0 %collective-permute-start.1 = (f32[4,8,32,128]{3,2,1,0:T(8,128)S(1)}, f32[4,8,32,128]{3,2,1,0:T(8,128)S(1)}, u32[]{:S(2)}, u32[]{:S(2)}) collective-permute-start(f32[4,8,32,128]{3,2,1,0:T(8,128)S(1)} %get-tuple-element.19), channel_id=1, source_target_pairs={{0,8},{8,0},{1,9},{9,1},{2,10},{10,2},{3,11},{11,3},{4,12},{12,4},... | collective-permute-start | bytes 1572872 | tf_op jit(solution)/shard_map/ppermute | solution.py:274
  57.0 1.5 collective-permute-done.1
  58.5 0.0 copy-done.3
  58.5 0.0 copy-start.2
  58.5 0.1 shard_map.97
  58.6 24.9 %all_to_all.31 = bf16[32,48,128]{2,1,0:T(8,128)(2,1)S(1)} all-to-all(bf16[32,48,128]{2,1,0:T(8,128)(2,1)S(1)} %shard_map.97), channel_id=1, replica_groups=mesh['ring'=8,'side'=2,'near'=4,'core'=2,'feat'=8] {'near','feat'}, dimensions={0} | all-to-all | bytes 786432 | tf_op jit(solution)/shard_map/all_to_all | solution.py:282
  83.5 0.0 copy-done.2
  83.5 0.9 shard_map.98
  84.4 19.0 %all_to_all.32.mine_ref = bf16[32,48,128]{2,1,0:T(8,128)(2,1)S(1)} all-to-all(bf16[32,48,128]{2,1,0:T(8,128)(2,1)S(1)} %get-tuple-element.21), channel_id=1, replica_groups=mesh['ring'=8,'side'=2,'near'=4,'core'=2,'feat'=8] {'near','feat'}, dimensions={0} | all-to-all | bytes 786432 | tf_op jit(solution)/shard_map/all_to_all | solution.py:294
  103.4 5.0 %collective-permute-start.2 = (bf16[32,48,128]{2,1,0:T(8,128)(2,1)S(1)}, bf16[32,48,128]{2,1,0:T(8,128)(2,1)S(1)}, u32[]{:S(2)}, u32[]{:S(2)}) collective-permute-start(bf16[32,48,128]{2,1,0:T(8,128)(2,1)S(1)} %all_to_all.32.mine_ref), channel_id=1, source_target_pairs={{0,8},{8,0},{1,9},{9,1},{2,10},{10,2},{3,11},{11,3},{4,12},{12,4},... | collective-permute-start | bytes 1179656 | tf_op jit(solution)/shard_map/ppermute | solution.py:295
  108.4 1.3 collective-permute-done.2.other_ref
  109.7 3.7 %shard_map.99 = bf16[8,528,128]{2,1,0:T(8,128)(2,1)S(1)} custom-call(s32[387]{0:T(512)S(1)} %concatenate.3.table, bf16[192,128,128]{2,1,0:T(8,128)(2,1)} %adj_ref.3, bf16[32,48,128]{2,1,0:T(8,128)(2,1)S(1)} %all_to_all.32.mine_ref, bf16[32,48,128]{2,1,0:T(8,128)(2,1)S(1)} %collective-permute-done.2.other_ref), custom_call_target="tpu_custom_call" | custom-call | tf_op jit(solution)/shard_map/pallas_call | solution.py:218
  113.4 32.4 %all_to_all.33.pieces_ref = bf16[8,528,128]{2,1,0:T(8,128)(2,1)S(1)} all-to-all(bf16[8,528,128]{2,1,0:T(8,128)(2,1)S(1)} %shard_map.99), channel_id=1, replica_groups=mesh['ring'=8,'side'=2,'near'=4,'core'=2,'feat'=8] {'ring'}, dimensions={0} | all-to-all | bytes 2162688 | tf_op jit(solution)/shard_map/all_to_all | solution.py:307
  145.8 0.7 shard_map.100
  146.4 12.0 %all-to-all-start.5 = ((f32[8,16,128]{2,1,0:T(8,128)}), f32[8,16,128]{2,1,0:T(8,128)S(1)}, u32[]{:S(2)}, u32[]{:S(2)}) async-start(f32[8,16,128]{2,1,0:T(8,128)} %get-tuple-element.24), calls=%async_computation.5 | async-start | bytes 131072 | tf_op jit(solution)/shard_map/all_to_all | solution.py:320
  158.4 7.3 %collective-permute-start.3 = (bf16[256,128]{1,0:T(8,128)(2,1)S(1)}, bf16[256,128]{1,0:T(8,128)(2,1)S(1)}, u32[]{:S(2)}, u32[]{:S(2)}) collective-permute-start(bf16[256,128]{1,0:T(8,128)(2,1)S(1)} %get-tuple-element.23), channel_id=1, source_target_pairs={{0,64},{64,0},{1,65},{65,1},{2,66},{66,2},{3,67},{67,3},{4,68},{68... | collective-permute-start | bytes 196616 | tf_op jit(solution)/shard_map/ppermute | solution.py:319
  165.7 2.3 %collective-permute-done.3.refs_1_ = bf16[256,128]{1,0:T(8,128)(2,1)S(1)} collective-permute-done((bf16[256,128]{1,0:T(8,128)(2,1)S(1)}, bf16[256,128]{1,0:T(8,128)(2,1)S(1)}, u32[]{:S(2)}, u32[]{:S(2)}) %collective-permute-start.3) | collective-permute-done | bytes 65568 | tf_op jit(solution)/shard_map/ppermute | solution.py:319
  168.0 0.0 all-to-all-done.5.refs_2_
  168.0 0.7 shard_map.101
  (1 shorter events, 0.0 us)
Async XLA Ops:
  0.6 24.7 %copy-start.4 = (s32[192]{0:T(256)S(1)}, s32[192]{0:T(256)}, u32[]{:S(2)}) copy-start(s32[192]{0:T(256)} %param.11) | copy-start | bytes 2308
  0.6 0.8 copy-start
  1.5 8.9 %copy-start.1 = (bf16[1024,32]{0,1:T(8,128)(2,1)S(1)}, bf16[1024,32]{0,1:T(8,128)(2,1)}, u32[]{:S(2)}) copy-start(bf16[1024,32]{0,1:T(8,128)(2,1)} %param.7) | copy-start | bytes 196612
  1.5 23.9 %copy-start.5 = (s32[192]{0:T(256)S(1)}, s32[192]{0:T(256)}, u32[]{:S(2)}) copy-start(s32[192]{0:T(256)} %param.12) | copy-start | bytes 2308
  2.3 24.0 %all-to-all-start = ((bf16[8,32,1024]{2,1,0:T(8,128)(2,1)}), bf16[8,32,1024]{2,1,0:T(8,128)(2,1)S(1)}, u32[]{:S(2)}, u32[]{:S(2)}) async-start(bf16[8,32,1024]{2,1,0:T(8,128)(2,1)} %shard_map.94), calls=%async_computation | async-start | bytes 1048576 | tf_op jit(solution)/shard_map/all_to_all | solution.py:254
  10.4 15.9 %collective-permute-start = (bf16[32,1024]{1,0:T(8,128)(2,1)S(1)}, bf16[32,1024]{1,0:T(8,128)(2,1)S(1)}, u32[]{:S(2)}, u32[]{:S(2)}) collective-permute-start(bf16[32,1024]{1,0:T(8,128)(2,1)S(1)} %bitcast.12), channel_id=1, source_target_pairs={{0,64},{64,0},{1,65},{65,1},{2,66},{66,2},{3,67},{67,3},{4,68},{68... | collective-permute-start | bytes 196616 | tf_op jit(solution)/shard_map/ppermute | solution.py:257
  45.5 13.0 %copy-start.3 = (bf16[32,256]{1,0:T(8,128)(2,1)S(1)}, bf16[32,256]{1,0:T(8,128)(2,1)}, u32[]{:S(2)}) copy-start(bf16[32,256]{1,0:T(8,128)(2,1)} %weight_ref.1) | copy-start | bytes 49156
  49.0 9.5 %collective-permute-start.1 = (f32[4,8,32,128]{3,2,1,0:T(8,128)S(1)}, f32[4,8,32,128]{3,2,1,0:T(8,128)S(1)}, u32[]{:S(2)}, u32[]{:S(2)}) collective-permute-start(f32[4,8,32,128]{3,2,1,0:T(8,128)S(1)} %get-tuple-element.19), channel_id=1, source_target_pairs={{0,8},{8,0},{1,9},{9,1},{2,10},{10,2},{3,11},{11,3},{4,12},{12,4},... | collective-permute-start | bytes 1572872 | tf_op jit(solution)/shard_map/ppermute | solution.py:274
  58.5 25.0 %copy-start.2 = (bf16[128,256]{1,0:T(8,128)(2,1)S(1)}, bf16[128,256]{1,0:T(8,128)(2,1)}, u32[]{:S(2)}) copy-start(bf16[128,256]{1,0:T(8,128)(2,1)} %grad_ref.1) | copy-start | bytes 196612
  103.4 6.3 %collective-permute-start.2 = (bf16[32,48,128]{2,1,0:T(8,128)(2,1)S(1)}, bf16[32,48,128]{2,1,0:T(8,128)(2,1)S(1)}, u32[]{:S(2)}, u32[]{:S(2)}) collective-permute-start(bf16[32,48,128]{2,1,0:T(8,128)(2,1)S(1)} %all_to_all.32.mine_ref), channel_id=1, source_target_pairs={{0,8},{8,0},{1,9},{9,1},{2,10},{10,2},{3,11},{11,3},{4,12},{12,4},... | collective-permute-start | bytes 1179656 | tf_op jit(solution)/shard_map/ppermute | solution.py:295
  146.4 21.6 %all-to-all-start.5 = ((f32[8,16,128]{2,1,0:T(8,128)}), f32[8,16,128]{2,1,0:T(8,128)S(1)}, u32[]{:S(2)}, u32[]{:S(2)}) async-start(f32[8,16,128]{2,1,0:T(8,128)} %get-tuple-element.24), calls=%async_computation.5 | async-start | bytes 131072 | tf_op jit(solution)/shard_map/all_to_all | solution.py:320
  158.4 9.6 %collective-permute-start.3 = (bf16[256,128]{1,0:T(8,128)(2,1)S(1)}, bf16[256,128]{1,0:T(8,128)(2,1)S(1)}, u32[]{:S(2)}, u32[]{:S(2)}) collective-permute-start(bf16[256,128]{1,0:T(8,128)(2,1)S(1)} %get-tuple-element.23), channel_id=1, source_target_pairs={{0,64},{64,0},{1,65},{65,1},{2,66},{66,2},{3,67},{67,3},{4,68},{68... | collective-permute-start | bytes 196616 | tf_op jit(solution)/shard_map/ppermute | solution.py:319
